TPU v7x, 32 devices: a whole 2x2x4 slice. The times are simulated.
32 devices in a mesh: tower: 4 (over y, x), intra: 8 (over z, core).
Axes of the slice: x: 2, y: 2, z: 4, core: 2. Of those that a mesh axis runs over, the one named last changes fastest.
Arguments:
- embeddings: bfloat16 [256, 16384], P(None, ('tower', 'intra')), may hold values from -6 to 6
- feature_assign: int32 [4, 32], P('tower'), may hold values from 0 to 31, each once within a row
- sample_owner: int32 [256], replicated, may hold values from 0 to 255, each once
- first_weight: bfloat16 [8, 2048, 1024], P('tower'), may hold values from -0.125 to 0.125
- first_bias: float32 [8, 1024], P('tower'), may hold values from -3 to 3
- tower_weight: bfloat16 [8, 1024, 256], P('tower'), may hold values from -0.1875 to 0.1875
- tower_bias: float32 [8, 256], P('tower'), may hold values from -3 to 3
- proj_weight: bfloat16 [16, 128], replicated, may hold values from -1.5 to 1.5
Outputs:
- interaction: bfloat16 [256, 16, 128], P(('tower', 'intra'))
Inputs may be any that keep to these rules, and one draw needn't show every extreme that they name: `feature_assign`: each row is a permutation of 0 to 31. `sample_owner`: a permutation of 0 to 255.
All inputs are finite; a program needn't handle non-finite values.
Results may differ from a plain program's by a relative error of at most 0.0034.
Values may be sent and summed in bfloat16 or wider, within the bound.
No kernel may reach another device: no remote copies, remote signals or barrier semaphores. Data moves between devices by JAX's collectives and lax.ppermute only.
A program may use at most 64 MiB of HBM per device.

v0:
```python
import functools

import jax
import jax.numpy as jnp
from jax import lax
from jax.experimental import pallas as pl
from jax.experimental.pallas import tpu as pltpu
from jax.sharding import PartitionSpec as P

EDIM = 128
FEW_SAMPLES = 1024


def offsets(size, step=1):
    return range(size - step, -1, -step)


def exchange(blocks, axis, size, step=1):
    return [
        lax.ppermute(block, axis, [(i, i ^ o) for i in range(size)]) if o else block
        for block, o in zip(blocks, offsets(size, step))
    ]


def other_core(intra):
    return 1 if intra > 1 else 0


def exchange_groups(blocks, towers, intra):
    received = []
    for block, o in zip(blocks, offsets(towers)):
        pairs = [
            (t * intra + i, (t ^ o) * intra + (i ^ other_core(intra)))
            for t in range(towers)
            for i in range(intra)
        ]
        received.append(lax.ppermute(block, ("tower", "intra"), pairs) if o else block)
    return received


def load_kernel(count, owner_hbm, emb_hbm, *rest):
    small, (picks_ref, emb_ref), copies = rest[:count], rest[count : count + 2], rest[count + 2 : -2]
    owner_ref, sems = rest[-2:]
    pairs = [(owner_hbm, owner_ref), (emb_hbm, emb_ref), *zip(small, copies)]
    loads = [pltpu.make_async_copy(a, b, sems.at[i]) for i, (a, b) in enumerate(pairs)]
    for load in loads:
        load.start()
    samples = emb_ref.shape[0]
    loads[0].wait()
    owner = jnp.broadcast_to(owner_ref[...].reshape(1, samples), (samples, samples))
    picks = lax.broadcasted_iota(jnp.int32, (samples, samples), 0) == owner
    picks_ref[...] = jnp.where(picks, 1.0, 0.0).astype(jnp.bfloat16)
    for load in loads[1:]:
        load.wait()


def gather_kernel(towers, intra, pair, picks_ref, *rest):
    parts, outs, acc_ref = rest[:pair], rest[pair:-1], rest[-1]
    samples, width = parts[0].shape
    per = samples // (towers * intra)
    held = width // EDIM
    me, place = lax.axis_index("intra"), lax.axis_index("tower")
    for q, part in enumerate(parts):
        acc_ref[:, q * width : (q + 1) * width] = lax.dot_general(
            picks_ref[...], part[...], (((0,), (0,)), ((), ())), preferred_element_type=jnp.float32
        )
    for o, out in zip(offsets(intra, pair), outs):
        block = me ^ o
        owners = [jnp.where(place == t, block, block ^ other_core(intra)) for t in range(towers)]
        starts = [pl.multiple_of((t * intra + owners[t]) * per, per) for t in range(towers)]
        for f in range(pair * held):
            columns = slice(f * EDIM, (f + 1) * EDIM)
            rows = [acc_ref[pl.ds(start, per), columns] for start in starts]
            out[f] = jnp.concatenate(rows, axis=0).astype(out.dtype)


def gather_blocks(owner, embeddings, small, towers, intra, pair, ahead):
    samples, width = embeddings.shape
    rows, held = samples // intra, pair * width // EDIM
    parts = [lax.ppermute(embeddings, "intra", [(i, i ^ q) for i in range(intra)]) for q in range(1, pair)]
    if samples <= FEW_SAMPLES:
        given = [pltpu.with_memory_space_constraint(a, pltpu.HBM) for a in (owner, embeddings, *small)]
        spaces = [pltpu.SMEM if jnp.issubdtype(a.dtype, jnp.integer) else pltpu.VMEM for a in small]
        picks, embeddings, *small = pl.pallas_call(
            functools.partial(load_kernel, len(small)),
            out_shape=[
                pltpu.VMEM((samples, samples), jnp.bfloat16),
                pltpu.VMEM(embeddings.shape, embeddings.dtype),
            ]
            + [space(a.shape, a.dtype) for space, a in zip(spaces, small)],
            in_specs=[pl.BlockSpec(memory_space=pltpu.HBM)] * len(given),
            out_specs=[pl.BlockSpec(memory_space=pltpu.VMEM)] * 2
            + [pl.BlockSpec(memory_space=space) for space in spaces],
            scratch_shapes=[
                pltpu.VMEM(owner.shape, owner.dtype),
                pltpu.SemaphoreType.DMA((len(given),)),
            ],
            compiler_params=pltpu.CompilerParams(vmem_limit_bytes=8 << 20),
            cost_estimate=pl.CostEstimate(flops=ahead, bytes_accessed=0, transcendentals=0),
            name="load",
        )(*given)
        blocks = pl.pallas_call(
            functools.partial(gather_kernel, towers, intra, pair),
            out_shape=[pltpu.VMEM((held, rows, EDIM), embeddings.dtype)] * (intra // pair),
            in_specs=[pl.BlockSpec(memory_space=pltpu.VMEM)] * (1 + pair),
            out_specs=[pl.BlockSpec(memory_space=pltpu.VMEM)] * (intra // pair),
            scratch_shapes=[pltpu.VMEM((samples, pair * width), jnp.float32)],
            compiler_params=pltpu.CompilerParams(vmem_limit_bytes=8 << 20),
            name="gather_rows",
        )(picks, embeddings, *parts)
        return blocks, small
    order = owner.reshape(towers, intra, -1)
    crossed = order[:, jnp.arange(intra) ^ other_core(intra)]
    own = jnp.arange(towers)[:, None, None] == lax.axis_index("tower")
    order = jnp.where(own, order, crossed).transpose(1, 0, 2)
    me = lax.axis_index("intra")
    table = jnp.concatenate([embeddings, *parts], axis=1)
    blocks = []
    for o in offsets(intra, pair):
        mine = lax.dynamic_index_in_dim(order, me ^ o, keepdims=False).reshape(-1)
        blocks.append(jnp.take(table, mine, axis=0).reshape(rows, held, EDIM).transpose(1, 0, 2))
    return blocks, small


def tower_kernel(towers, intra, pair, assign_ref, w1_ref, b1_ref, w2_ref, b2_ref, *rest):
    blocks, outs, (pool_ref, x_ref, y_ref) = rest[: intra // pair], rest[intra // pair : -3], rest[-3:]
    held, rows, _ = blocks[0].shape
    held //= pair
    count, depth, _ = w1_ref.shape
    vectors = w2_ref.shape[2] // EDIM
    per = rows // towers
    slots = depth // EDIM
    me = lax.axis_index("intra")
    for o, block in zip(offsets(intra, pair), blocks):
        for q in range(pair):
            pool_ref[pl.ds((me ^ o ^ q) * held, held)] = block[q * held : (q + 1) * held]
    for k in range(count):
        for j in range(slots):
            x_ref[k, :, j * EDIM : (j + 1) * EDIM] = pool_ref[assign_ref[0, k * slots + j]]
    for k in range(count):
        hidden = jnp.dot(x_ref[k], w1_ref[k], preferred_element_type=jnp.float32)
        hidden = jnp.maximum(hidden + b1_ref[k : k + 1, :], 0.0).astype(jnp.bfloat16)
        result = jnp.dot(hidden, w2_ref[k], preferred_element_type=jnp.float32)
        y_ref[k] = jnp.maximum(result + b2_ref[k : k + 1, :], 0.0)
    place = lax.axis_index("tower")
    for o, out in zip(offsets(towers), outs):
        start = pl.multiple_of((place ^ o) * per, per)
        pieces = [
            y_ref[k, pl.ds(start, per), v * EDIM : (v + 1) * EDIM]
            for k in range(count)
            for v in range(vectors)
        ]
        out[...] = jnp.concatenate(pieces, axis=0).astype(out.dtype)


def run_towers(assign, w1, b1, w2, b2, blocks, towers, intra, pair):
    held, rows, _ = blocks[0].shape
    count, depth, _ = w1.shape
    width = w2.shape[2]
    local = count * (width // EDIM) * (rows // towers)
    w1 = pltpu.with_memory_space_constraint(w1, pltpu.VMEM)
    w2 = pltpu.with_memory_space_constraint(w2, pltpu.VMEM)
    return pl.pallas_call(
        functools.partial(tower_kernel, towers, intra, pair),
        out_shape=[jax.ShapeDtypeStruct((local, EDIM), jnp.bfloat16)] * towers,
        in_specs=[pl.BlockSpec(memory_space=pltpu.SMEM)]
        + [pl.BlockSpec(memory_space=pltpu.VMEM)] * (4 + len(blocks)),
        out_specs=[pl.BlockSpec(memory_space=pltpu.VMEM)] * towers,
        scratch_shapes=[
            pltpu.VMEM((len(blocks) * held, rows, EDIM), jnp.bfloat16),
            pltpu.VMEM((count, rows, depth), jnp.bfloat16),
            pltpu.VMEM((count, rows, width), jnp.float32),
        ],
        compiler_params=pltpu.CompilerParams(vmem_limit_bytes=16 << 20),
        name="towers",
    )(assign, w1, b1, w2, b2, *blocks)


def interact_kernel(towers, proj_ref, *rest):
    blocks, out, all_ref = rest[:towers], rest[towers], rest[towers + 1]
    per, count, _ = out.shape
    local = blocks[0].shape[0]
    place = lax.axis_index("tower")
    for o, block in zip(offsets(towers), blocks):
        start = pl.multiple_of((place ^ o) * local, local)
        all_ref[pl.ds(start, local), :] = block[...].astype(jnp.float32)
    group = max(1, min(per, 128 // count))
    proj = jnp.concatenate([proj_ref[...]] * (2 * group), axis=0)
    for first in range(0, per, group):
        samples = range(first, first + group)
        vectors = [all_ref[pl.ds(d, count, stride=per), :] for d in samples]
        vectors = jnp.concatenate(vectors, axis=0).astype(jnp.bfloat16)
        gram = lax.dot_general(
            vectors, vectors, (((1,), (1,)), ((), ())), preferred_element_type=jnp.float32
        )
        gram = gram * (1.0 / EDIM)
        column = lax.broadcasted_iota(jnp.int32, (count, gram.shape[1]), 1)
        own = [
            jnp.where(
                (column >= g * count) & (column < (g + 1) * count),
                gram[g * count : (g + 1) * count, :],
                0.0,
            )
            for g in range(group)
        ]
        gram = jnp.concatenate(own, axis=0)
        high = gram.astype(jnp.bfloat16)
        low = (gram - high.astype(jnp.float32)).astype(jnp.bfloat16)
        result = jnp.dot(
            jnp.concatenate([high, low], axis=1), proj, preferred_element_type=jnp.float32
        )
        for g, d in enumerate(samples):
            out[d] = result[g * count : (g + 1) * count, :].astype(out.dtype)


def interact(proj, blocks):
    towers = len(blocks)
    local = blocks[0].shape[0]
    count = proj.shape[0]
    per = towers * local // count
    return pl.pallas_call(
        functools.partial(interact_kernel, towers),
        out_shape=jax.ShapeDtypeStruct((per, count, EDIM), jnp.bfloat16),
        in_specs=[pl.BlockSpec(memory_space=pltpu.VMEM)] * (1 + towers),
        out_specs=pl.BlockSpec(memory_space=pltpu.VMEM),
        scratch_shapes=[pltpu.VMEM((towers * local, EDIM), jnp.float32)],
        compiler_params=pltpu.CompilerParams(vmem_limit_bytes=8 << 20),
        name="interact",
    )(proj, *blocks)


def shards(
    embeddings,
    feature_assign,
    sample_owner,
    first_weight,
    first_bias,
    tower_weight,
    tower_bias,
    proj_weight,
):
    towers, intra = lax.axis_size("tower"), lax.axis_size("intra")
    small = (feature_assign, first_bias, tower_bias, proj_weight)
    ahead = 10_000 * (first_weight.size + tower_weight.size)
    pair = 2 if intra % 2 == 0 else 1
    blocks, small = gather_blocks(sample_owner, embeddings, small, towers, intra, pair, ahead)
    feature_assign, first_bias, tower_bias, proj_weight = small
    blocks = exchange(blocks, "intra", intra, pair)
    vectors = run_towers(
        feature_assign, first_weight, first_bias, tower_weight, tower_bias, blocks, towers, intra, pair
    )
    vectors = exchange_groups(vectors, towers, intra)
    return interact(proj_weight, vectors)


def solution(mesh):
    return jax.shard_map(
        shards,
        mesh=mesh,
        in_specs=(
            P(None, ("tower", "intra")),
            P("tower", None),
            P(),
            P("tower", None, None),
            P("tower", None),
            P("tower", None, None),
            P("tower", None),
            P(),
        ),
        out_specs=P(("tower", "intra"), None, None),
        check_vma=False,
    )
```

profile of v0, /device:TPU:0, one launch (start us, length us, event | category | flops | bytes accessed | tf_op | source)
XLA Modules:
  0.0 21.6 jit_solution(5824704398041042685)
XLA Ops:
  0.0 0.0 copy-start.1
  0.0 0.0 copy-start
  0.0 0.5 %collective-permute-start = (bf16[256,512]{1,0:T(8,128)(2,1)}, bf16[256,512]{1,0:T(8,128)(2,1)S(1)}, u32[]{:S(2)}, u32[]{:S(2)}) collective-permute-start(bf16[256,512]{1,0:T(8,128)(2,1)} %emb_hbm.1), channel_id=1, source_target_pairs={{0,1},{1,0},{2,3},{3,2},{4,5},{5,4},{6,7},{7,6},{8,9},{9,8},{10,11... | collective-permute-start | bytes 786440 | tf_op jit(solution)/shard_map/ppermute | solution.py:80
  0.5 1.2 %load.1 = (bf16[256,256]{1,0:T(8,128)(2,1)S(1)}, bf16[256,512]{1,0:T(8,128)(2,1)S(1)}, s32[1,32]{1,0:T(1,128)S(4)}, f32[2,1024]{1,0:T(2,128)S(1)}, f32[2,256]{1,0:T(2,128)S(1)}, /*index=5*/bf16[16,128]{1,0:T(8,128)(2,1)S(1)}) custom-call(s32[256]{0:T(256)} %owner_hbm.1, bf16[256,512]{1,0:T(8,128)(2,1)} %emb_hbm.1, s32[1,32]{1,0:T(1,128)} %rest_0_.1, ...), custom_call_target="tpu_custom_call" | custom-call | flops 47185920000 | tf_op jit(solution)/shard_map/load/pallas_call | solution.py:84
  1.7 0.1 collective-permute-done.rest_1_
  1.8 0.3 %gather_rows.1 = (bf16[8,32,128]{2,1,0:T(8,128)(2,1)S(1)}, bf16[8,32,128]{2,1,0:T(8,128)(2,1)S(1)}, bf16[8,32,128]{2,1,0:T(8,128)(2,1)S(1)}, bf16[8,32,128]{2,1,0:T(8,128)(2,1)S(1)}) custom-call(bf16[256,256]{1,0:T(8,128)(2,1)S(1)} %get-tuple-element.23.picks_ref, bf16[256,512]{1,0:T(8,128)(2,1)S(1)} %get-tuple-element.24.rest_0_, ...), custom_call_target="tpu_custom_call" | custom-call | tf_op jit(solution)/shard_map/gather_rows/pallas_call | solution.py:102
  2.2 5.0 %collective-permute-start.1 = (bf16[8,32,128]{2,1,0:T(8,128)(2,1)S(1)}, bf16[8,32,128]{2,1,0:T(8,128)(2,1)S(1)}, u32[]{:S(2)}, u32[]{:S(2)}) collective-permute-start(bf16[8,32,128]{2,1,0:T(8,128)(2,1)S(1)} %get-tuple-element.25), channel_id=1, source_target_pairs={{0,6},{1,7},{2,4},{3,5},{4,2},{5,3},{6,0},{7,1},{8,14},{9,15},{10,... | collective-permute-start | bytes 196616 | tf_op jit(solution)/shard_map/ppermute | solution.py:20
  7.2 0.0 collective-permute-start.2
  7.2 0.6 %collective-permute-start.3 = (bf16[8,32,128]{2,1,0:T(8,128)(2,1)S(1)}, bf16[8,32,128]{2,1,0:T(8,128)(2,1)S(1)}, u32[]{:S(2)}, u32[]{:S(2)}) collective-permute-start(bf16[8,32,128]{2,1,0:T(8,128)(2,1)S(1)} %get-tuple-element.27), channel_id=1, source_target_pairs={{0,2},{1,3},{2,0},{3,1},{4,6},{5,7},{6,4},{7,5},{8,10},{9,11},{10,... | collective-permute-start | bytes 196616 | tf_op jit(solution)/shard_map/ppermute | solution.py:20
  7.9 2.0 %collective-permute-done.1.rest_0_ = bf16[8,32,128]{2,1,0:T(8,128)(2,1)S(1)} collective-permute-done((bf16[8,32,128]{2,1,0:T(8,128)(2,1)S(1)}, bf16[8,32,128]{2,1,0:T(8,128)(2,1)S(1)}, u32[]{:S(2)}, u32[]{:S(2)}) %collective-permute-start.1) | collective-permute-done | bytes 65568 | tf_op jit(solution)/shard_map/ppermute | solution.py:20
  9.8 3.3 %collective-permute-done.2.rest_1_ = bf16[8,32,128]{2,1,0:T(8,128)(2,1)S(1)} collective-permute-done((bf16[8,32,128]{2,1,0:T(8,128)(2,1)S(1)}, bf16[8,32,128]{2,1,0:T(8,128)(2,1)S(1)}, u32[]{:S(2)}, u32[]{:S(2)}) %collective-permute-start.2) | collective-permute-done | bytes 65568 | tf_op jit(solution)/shard_map/ppermute | solution.py:20
  13.1 0.0 collective-permute-done.3.rest_2_
  13.1 0.0 copy-done.1
  13.1 0.0 copy-done
  13.1 1.7 %towers.1 = (bf16[32,128]{1,0:T(8,128)(2,1)S(1)}, bf16[32,128]{1,0:T(8,128)(2,1)S(1)}, bf16[32,128]{1,0:T(8,128)(2,1)S(1)}, bf16[32,128]{1,0:T(8,128)(2,1)S(1)}) custom-call(s32[1,32]{1,0:T(1,128)S(4)} %get-tuple-element.20.assign_ref, bf16[2,2048,1024]{2,1,0:T(8,128)(2,1)S(1)} %copy-done, f32[2,1024]{1,0:T(2,128)S(1)} %get-tuple-element.21.b1_ref, ...), custom_call_target="tpu_custom_call" | custom-call | tf_op jit(solution)/shard_map/towers/pallas_call | solution.py:163
  14.8 1.8 %collective-permute-start.4 = (bf16[32,128]{1,0:T(8,128)(2,1)S(1)}, bf16[32,128]{1,0:T(8,128)(2,1)S(1)}, u32[]{:S(2)}, u32[]{:S(2)}) collective-permute-start(bf16[32,128]{1,0:T(8,128)(2,1)S(1)} %get-tuple-element.29), channel_id=1, source_target_pairs={{0,25},{1,24},{2,27},{3,26},{4,29},{5,28},{6,31},{7,30},{8,17},{9,... | collective-permute-start | bytes 24584 | tf_op jit(solution)/shard_map/ppermute | solution.py:37
  16.6 0.9 %collective-permute-start.5 = (bf16[32,128]{1,0:T(8,128)(2,1)S(1)}, bf16[32,128]{1,0:T(8,128)(2,1)S(1)}, u32[]{:S(2)}, u32[]{:S(2)}) collective-permute-start(bf16[32,128]{1,0:T(8,128)(2,1)S(1)} %get-tuple-element.30), channel_id=1, source_target_pairs={{0,17},{1,16},{2,19},{3,18},{4,21},{5,20},{6,23},{7,22},{8,25},{9,... | collective-permute-start | bytes 24584 | tf_op jit(solution)/shard_map/ppermute | solution.py:37
  17.6 0.1 collective-permute-start.6
  17.7 1.2 %collective-permute-done.4.rest_0_ = bf16[32,128]{1,0:T(8,128)(2,1)S(1)} collective-permute-done((bf16[32,128]{1,0:T(8,128)(2,1)S(1)}, bf16[32,128]{1,0:T(8,128)(2,1)S(1)}, u32[]{:S(2)}, u32[]{:S(2)}) %collective-permute-start.4) | collective-permute-done | bytes 8224 | tf_op jit(solution)/shard_map/ppermute | solution.py:37
  18.9 0.8 %collective-permute-done.5.rest_1_ = bf16[32,128]{1,0:T(8,128)(2,1)S(1)} collective-permute-done((bf16[32,128]{1,0:T(8,128)(2,1)S(1)}, bf16[32,128]{1,0:T(8,128)(2,1)S(1)}, u32[]{:S(2)}, u32[]{:S(2)}) %collective-permute-start.5) | collective-permute-done | bytes 8224 | tf_op jit(solution)/shard_map/ppermute | solution.py:37
  19.7 1.0 %collective-permute-done.6.rest_2_ = bf16[32,128]{1,0:T(8,128)(2,1)S(1)} collective-permute-done((bf16[32,128]{1,0:T(8,128)(2,1)S(1)}, bf16[32,128]{1,0:T(8,128)(2,1)S(1)}, u32[]{:S(2)}, u32[]{:S(2)}) %collective-permute-start.6) | collective-permute-done | bytes 8224 | tf_op jit(solution)/shard_map/ppermute | solution.py:37
  20.7 0.9 %interact.1 = bf16[8,16,128]{2,1,0:T(8,128)(2,1)} custom-call(bf16[16,128]{1,0:T(8,128)(2,1)S(1)} %get-tuple-element.19.proj_ref, bf16[32,128]{1,0:T(8,128)(2,1)S(1)} %collective-permute-done.4.rest_0_, bf16[32,128]{1,0:T(8,128)(2,1)S(1)} %collective-permute-done.5.rest_1_, bf16[32,128]{1,0:T(8,128)(2,1)S(1)} %collective-permute-done.6.rest_2_, ...), custom_call_target="tpu_custom_call" | custom-call | tf_op jit(solution)/shard_map/interact/pallas_call | solution.py:221
Async XLA Ops:
  0.0 13.1 %copy-start.1 = (bf16[2,1024,256]{2,1,0:T(8,128)(2,1)S(1)}, bf16[2,1024,256]{2,1,0:T(8,128)(2,1)}, u32[]{:S(2)}) copy-start(bf16[2,1024,256]{2,1,0:T(8,128)(2,1)} %w2_ref.1) | copy-start | bytes 3145732
  0.0 13.1 %copy-start = (bf16[2,2048,1024]{2,1,0:T(8,128)(2,1)S(1)}, bf16[2,2048,1024]{2,1,0:T(8,128)(2,1)}, u32[]{:S(2)}) copy-start(bf16[2,2048,1024]{2,1,0:T(8,128)(2,1)} %w1_ref.1) | copy-start | bytes 25165828
  0.0 1.8 %collective-permute-start = (bf16[256,512]{1,0:T(8,128)(2,1)}, bf16[256,512]{1,0:T(8,128)(2,1)S(1)}, u32[]{:S(2)}, u32[]{:S(2)}) collective-permute-start(bf16[256,512]{1,0:T(8,128)(2,1)} %emb_hbm.1), channel_id=1, source_target_pairs={{0,1},{1,0},{2,3},{3,2},{4,5},{5,4},{6,7},{7,6},{8,9},{9,8},{10,11... | collective-permute-start | bytes 786440 | tf_op jit(solution)/shard_map/ppermute | solution.py:80
  2.2 7.7 %collective-permute-start.1 = (bf16[8,32,128]{2,1,0:T(8,128)(2,1)S(1)}, bf16[8,32,128]{2,1,0:T(8,128)(2,1)S(1)}, u32[]{:S(2)}, u32[]{:S(2)}) collective-permute-start(bf16[8,32,128]{2,1,0:T(8,128)(2,1)S(1)} %get-tuple-element.25), channel_id=1, source_target_pairs={{0,6},{1,7},{2,4},{3,5},{4,2},{5,3},{6,0},{7,1},{8,14},{9,15},{10,... | collective-permute-start | bytes 196616 | tf_op jit(solution)/shard_map/ppermute | solution.py:20
  7.2 5.9 %collective-permute-start.2 = (bf16[8,32,128]{2,1,0:T(8,128)(2,1)S(1)}, bf16[8,32,128]{2,1,0:T(8,128)(2,1)S(1)}, u32[]{:S(2)}, u32[]{:S(2)}) collective-permute-start(bf16[8,32,128]{2,1,0:T(8,128)(2,1)S(1)} %get-tuple-element.26), channel_id=1, source_target_pairs={{0,4},{1,5},{2,6},{3,7},{4,0},{5,1},{6,2},{7,3},{8,12},{9,13},{10,... | collective-permute-start | bytes 196616 | tf_op jit(solution)/shard_map/ppermute | solution.py:20
  7.2 5.9 %collective-permute-start.3 = (bf16[8,32,128]{2,1,0:T(8,128)(2,1)S(1)}, bf16[8,32,128]{2,1,0:T(8,128)(2,1)S(1)}, u32[]{:S(2)}, u32[]{:S(2)}) collective-permute-start(bf16[8,32,128]{2,1,0:T(8,128)(2,1)S(1)} %get-tuple-element.27), channel_id=1, source_target_pairs={{0,2},{1,3},{2,0},{3,1},{4,6},{5,7},{6,4},{7,5},{8,10},{9,11},{10,... | collective-permute-start | bytes 196616 | tf_op jit(solution)/shard_map/ppermute | solution.py:20
  14.8 4.0 %collective-permute-start.4 = (bf16[32,128]{1,0:T(8,128)(2,1)S(1)}, bf16[32,128]{1,0:T(8,128)(2,1)S(1)}, u32[]{:S(2)}, u32[]{:S(2)}) collective-permute-start(bf16[32,128]{1,0:T(8,128)(2,1)S(1)} %get-tuple-element.29), channel_id=1, source_target_pairs={{0,25},{1,24},{2,27},{3,26},{4,29},{5,28},{6,31},{7,30},{8,17},{9,... | collective-permute-start | bytes 24584 | tf_op jit(solution)/shard_map/ppermute | solution.py:37
  16.6 3.1 %collective-permute-start.5 = (bf16[32,128]{1,0:T(8,128)(2,1)S(1)}, bf16[32,128]{1,0:T(8,128)(2,1)S(1)}, u32[]{:S(2)}, u32[]{:S(2)}) collective-permute-start(bf16[32,128]{1,0:T(8,128)(2,1)S(1)} %get-tuple-element.30), channel_id=1, source_target_pairs={{0,17},{1,16},{2,19},{3,18},{4,21},{5,20},{6,23},{7,22},{8,25},{9,... | collective-permute-start | bytes 24584 | tf_op jit(solution)/shard_map/ppermute | solution.py:37
  17.6 3.1 %collective-permute-start.6 = (bf16[32,128]{1,0:T(8,128)(2,1)S(1)}, bf16[32,128]{1,0:T(8,128)(2,1)S(1)}, u32[]{:S(2)}, u32[]{:S(2)}) collective-permute-start(bf16[32,128]{1,0:T(8,128)(2,1)S(1)} %get-tuple-element.31), channel_id=1, source_target_pairs={{0,9},{1,8},{2,11},{3,10},{4,13},{5,12},{6,15},{7,14},{8,1},{9,0},... | collective-permute-start | bytes 24584 | tf_op jit(solution)/shard_map/ppermute | solution.py:37
where the time goes:
time: 21.8 us; the launch traced here: 21.6 us
  starting transfers between devices  9.01 us (41%)
  waiting for transfers between devices  8.32 us (38%)
  Pallas kernels  4.24 us (19%)
    ppermute x3, starting transfers between devices, exchange(): lax.ppermute(block, axis, [(i, i ^ o) for i in range(size)])  5.68 us
    ppermute x3, waiting for transfers between devices, exchange(): lax.ppermute(block, axis, [(i, i ^ o) for i in range(size)])  5.25 us
    ppermute x3, waiting for transfers between devices, exchange_groups(): lax.ppermute(block, ('tower', 'intra'), pairs)  2.95 us
    ppermute x3, starting transfers between devices, exchange_groups(): lax.ppermute(block, ('tower', 'intra'), pairs)  2.88 us
    pallas_call x1, Pallas kernels, run_towers(): pl.pallas_call(functools.partial(tower_kernel, towers, intra, pair), out_...  1.72 us
    pallas_call x1, Pallas kernels, gather_blocks(): pl.pallas_call(functools.partial(load_kernel, len(small)), out_shape=[plt...  1.24 us
    pallas_call x1, Pallas kernels, interact(): pl.pallas_call(functools.partial(interact_kernel, towers), out_shape=jax....  0.94 us
    ppermute x1, starting transfers between devices, gather_blocks(): lax.ppermute(embeddings, 'intra', [(i, i ^ q) for i in range(intra)])  0.45 us
  transfers between devices with their start and end apart: 7, of which 6 were waited for; matrix products, arithmetic and copies ran while one was open for 0% of the time, Pallas kernels for 6%

commit v1 on v0

--- a/solution.py
+++ b/solution.py
@@ -12,7 +12,7 @@
 
 
 def offsets(size, step=1):
-    return range(size - step, -1, -step)
+    return [o + step - 1 if o else 0 for o in range(size - step, -1, -step)]
 
 
 def exchange(blocks, axis, size, step=1):
@@ -96,7 +96,6 @@
                 pltpu.SemaphoreType.DMA((len(given),)),
             ],
             compiler_params=pltpu.CompilerParams(vmem_limit_bytes=8 << 20),
-            cost_estimate=pl.CostEstimate(flops=ahead, bytes_accessed=0, transcendentals=0),
             name="load",
         )(*given)
         blocks = pl.pallas_call(
@@ -106,6 +105,7 @@
             out_specs=[pl.BlockSpec(memory_space=pltpu.VMEM)] * (intra // pair),
             scratch_shapes=[pltpu.VMEM((samples, pair * width), jnp.float32)],
             compiler_params=pltpu.CompilerParams(vmem_limit_bytes=8 << 20),
+            cost_estimate=pl.CostEstimate(flops=ahead, bytes_accessed=0, transcendentals=0),
             name="gather_rows",
         )(picks, embeddings, *parts)
         return blocks, small

time: 21.8 us -> 21.6 us (level)
    ppermute x3, starting transfers between devices: 5.68 us -> 5.4 us  [exchange(): lax.ppermute(block, axis, [(i, i ^ o) for i in range(size)])]
  transfers between devices with their start and end apart: 7 -> 7, of which waited for: 6 -> 6; matrix products, arithmetic and copies ran while one was open for 0% -> 0% of each run, Pallas kernels for 6% -> 5%
where the time goes in v1:
time: 21.6 us; the launch traced here: 21.4 us
  starting transfers between devices  8.88 us (41%)
  waiting for transfers between devices  8.46 us (39%)
  Pallas kernels  4.04 us (19%)
    ppermute x3, starting transfers between devices, exchange(): lax.ppermute(block, axis, [(i, i ^ o) for i in range(size)])  5.4 us
    ppermute x3, waiting for transfers between devices, exchange(): lax.ppermute(block, axis, [(i, i ^ o) for i in range(size)])  5.34 us
    ppermute x3, starting transfers between devices, exchange_groups(): lax.ppermute(block, ('tower', 'intra'), pairs)  3.03 us
    ppermute x3, waiting for transfers between devices, exchange_groups(): lax.ppermute(block, ('tower', 'intra'), pairs)  2.79 us
    pallas_call x1, Pallas kernels, run_towers(): pl.pallas_call(functools.partial(tower_kernel, towers, intra, pair), out_...  1.72 us
    pallas_call x1, Pallas kernels, gather_blocks(): pl.pallas_call(functools.partial(load_kernel, len(small)), out_shape=[plt...  1.03 us
    pallas_call x1, Pallas kernels, interact(): pl.pallas_call(functools.partial(interact_kernel, towers), out_shape=jax....  0.94 us
    ppermute x1, starting transfers between devices, gather_blocks(): lax.ppermute(embeddings, 'intra', [(i, i ^ q) for i in range(intra)])  0.45 us
  transfers between devices with their start and end apart: 7, of which 6 were waited for; matrix products, arithmetic and copies ran while one was open for 0% of the time, Pallas kernels for 5%

profile of v1, /device:TPU:0, one launch (start us, length us, event | category | flops | bytes accessed | tf_op | source)
XLA Modules:
  0.0 21.4 jit_solution(1326456999656281285)
XLA Ops:
  0.0 0.5 %collective-permute-start = (bf16[256,512]{1,0:T(8,128)(2,1)}, bf16[256,512]{1,0:T(8,128)(2,1)S(1)}, u32[]{:S(2)}, u32[]{:S(2)}) collective-permute-start(bf16[256,512]{1,0:T(8,128)(2,1)} %emb_hbm.1), channel_id=1, source_target_pairs={{0,1},{1,0},{2,3},{3,2},{4,5},{5,4},{6,7},{7,6},{8,9},{9,8},{10,11... | collective-permute-start | bytes 786440 | tf_op jit(solution)/shard_map/ppermute | solution.py:80
  0.5 1.0 %load.1 = (bf16[256,256]{1,0:T(8,128)(2,1)S(1)}, bf16[256,512]{1,0:T(8,128)(2,1)S(1)}, s32[1,32]{1,0:T(1,128)S(4)}, f32[2,1024]{1,0:T(2,128)S(1)}, f32[2,256]{1,0:T(2,128)S(1)}, /*index=5*/bf16[16,128]{1,0:T(8,128)(2,1)S(1)}) custom-call(s32[256]{0:T(256)} %owner_hbm.1, bf16[256,512]{1,0:T(8,128)(2,1)} %emb_hbm.1, s32[1,32]{1,0:T(1,128)} %rest_0_.1, ...), custom_call_target="tpu_custom_call" | custom-call | tf_op jit(solution)/shard_map/load/pallas_call | solution.py:84
  1.5 0.3 %collective-permute-done.rest_1_ = bf16[256,512]{1,0:T(8,128)(2,1)S(1)} collective-permute-done((bf16[256,512]{1,0:T(8,128)(2,1)}, bf16[256,512]{1,0:T(8,128)(2,1)S(1)}, u32[]{:S(2)}, u32[]{:S(2)}) %collective-permute-start) | collective-permute-done | bytes 262176 | tf_op jit(solution)/shard_map/ppermute | solution.py:80
  1.8 0.0 copy-start
  1.8 0.0 copy-start.1
  1.8 0.3 %gather_rows.1 = (bf16[8,32,128]{2,1,0:T(8,128)(2,1)S(1)}, bf16[8,32,128]{2,1,0:T(8,128)(2,1)S(1)}, bf16[8,32,128]{2,1,0:T(8,128)(2,1)S(1)}, bf16[8,32,128]{2,1,0:T(8,128)(2,1)S(1)}) custom-call(bf16[256,256]{1,0:T(8,128)(2,1)S(1)} %get-tuple-element.23.picks_ref, bf16[256,512]{1,0:T(8,128)(2,1)S(1)} %get-tuple-element.24.rest_0_, ...), custom_call_target="tpu_custom_call" | custom-call | flops 47185920000 | tf_op jit(solution)/shard_map/gather_rows/pallas_call | solution.py:101
  2.2 4.8 %collective-permute-start.1 = (bf16[8,32,128]{2,1,0:T(8,128)(2,1)S(1)}, bf16[8,32,128]{2,1,0:T(8,128)(2,1)S(1)}, u32[]{:S(2)}, u32[]{:S(2)}) collective-permute-start(bf16[8,32,128]{2,1,0:T(8,128)(2,1)S(1)} %get-tuple-element.25), channel_id=1, source_target_pairs={{0,7},{1,6},{2,5},{3,4},{4,3},{5,2},{6,1},{7,0},{8,15},{9,14},{10,... | collective-permute-start | bytes 196616 | tf_op jit(solution)/shard_map/ppermute | solution.py:20
  7.0 0.0 collective-permute-start.2
  7.0 0.6 %collective-permute-start.3 = (bf16[8,32,128]{2,1,0:T(8,128)(2,1)S(1)}, bf16[8,32,128]{2,1,0:T(8,128)(2,1)S(1)}, u32[]{:S(2)}, u32[]{:S(2)}) collective-permute-start(bf16[8,32,128]{2,1,0:T(8,128)(2,1)S(1)} %get-tuple-element.27), channel_id=1, source_target_pairs={{0,3},{1,2},{2,1},{3,0},{4,7},{5,6},{6,5},{7,4},{8,11},{9,10},{10,... | collective-permute-start | bytes 196616 | tf_op jit(solution)/shard_map/ppermute | solution.py:20
  7.6 1.9 %collective-permute-done.1.rest_0_ = bf16[8,32,128]{2,1,0:T(8,128)(2,1)S(1)} collective-permute-done((bf16[8,32,128]{2,1,0:T(8,128)(2,1)S(1)}, bf16[8,32,128]{2,1,0:T(8,128)(2,1)S(1)}, u32[]{:S(2)}, u32[]{:S(2)}) %collective-permute-start.1) | collective-permute-done | bytes 65568 | tf_op jit(solution)/shard_map/ppermute | solution.py:20
  9.5 3.4 %collective-permute-done.2.rest_1_ = bf16[8,32,128]{2,1,0:T(8,128)(2,1)S(1)} collective-permute-done((bf16[8,32,128]{2,1,0:T(8,128)(2,1)S(1)}, bf16[8,32,128]{2,1,0:T(8,128)(2,1)S(1)}, u32[]{:S(2)}, u32[]{:S(2)}) %collective-permute-start.2) | collective-permute-done | bytes 65568 | tf_op jit(solution)/shard_map/ppermute | solution.py:20
  12.9 0.0 collective-permute-done.3.rest_2_
  12.9 0.0 copy-done
  12.9 0.0 copy-done.1
  12.9 1.7 %towers.1 = (bf16[32,128]{1,0:T(8,128)(2,1)S(1)}, bf16[32,128]{1,0:T(8,128)(2,1)S(1)}, bf16[32,128]{1,0:T(8,128)(2,1)S(1)}, bf16[32,128]{1,0:T(8,128)(2,1)S(1)}) custom-call(s32[1,32]{1,0:T(1,128)S(4)} %get-tuple-element.20.assign_ref, bf16[2,2048,1024]{2,1,0:T(8,128)(2,1)S(1)} %copy-done, f32[2,1024]{1,0:T(2,128)S(1)} %get-tuple-element.21.b1_ref, ...), custom_call_target="tpu_custom_call" | custom-call | tf_op jit(solution)/shard_map/towers/pallas_call | solution.py:163
  14.7 2.3 %collective-permute-start.4 = (bf16[32,128]{1,0:T(8,128)(2,1)S(1)}, bf16[32,128]{1,0:T(8,128)(2,1)S(1)}, u32[]{:S(2)}, u32[]{:S(2)}) collective-permute-start(bf16[32,128]{1,0:T(8,128)(2,1)S(1)} %get-tuple-element.29), channel_id=1, source_target_pairs={{0,25},{1,24},{2,27},{3,26},{4,29},{5,28},{6,31},{7,30},{8,17},{9,... | collective-permute-start | bytes 24584 | tf_op jit(solution)/shard_map/ppermute | solution.py:37
  16.9 0.5 %collective-permute-start.5 = (bf16[32,128]{1,0:T(8,128)(2,1)S(1)}, bf16[32,128]{1,0:T(8,128)(2,1)S(1)}, u32[]{:S(2)}, u32[]{:S(2)}) collective-permute-start(bf16[32,128]{1,0:T(8,128)(2,1)S(1)} %get-tuple-element.30), channel_id=1, source_target_pairs={{0,17},{1,16},{2,19},{3,18},{4,21},{5,20},{6,23},{7,22},{8,25},{9,... | collective-permute-start | bytes 24584 | tf_op jit(solution)/shard_map/ppermute | solution.py:37
  17.4 0.3 %collective-permute-start.6 = (bf16[32,128]{1,0:T(8,128)(2,1)S(1)}, bf16[32,128]{1,0:T(8,128)(2,1)S(1)}, u32[]{:S(2)}, u32[]{:S(2)}) collective-permute-start(bf16[32,128]{1,0:T(8,128)(2,1)S(1)} %get-tuple-element.31), channel_id=1, source_target_pairs={{0,9},{1,8},{2,11},{3,10},{4,13},{5,12},{6,15},{7,14},{8,1},{9,0},... | collective-permute-start | bytes 24584 | tf_op jit(solution)/shard_map/ppermute | solution.py:37
  17.7 1.0 %collective-permute-done.4.rest_0_ = bf16[32,128]{1,0:T(8,128)(2,1)S(1)} collective-permute-done((bf16[32,128]{1,0:T(8,128)(2,1)S(1)}, bf16[32,128]{1,0:T(8,128)(2,1)S(1)}, u32[]{:S(2)}, u32[]{:S(2)}) %collective-permute-start.4) | collective-permute-done | bytes 8224 | tf_op jit(solution)/shard_map/ppermute | solution.py:37
  18.7 1.3 %collective-permute-done.5.rest_1_ = bf16[32,128]{1,0:T(8,128)(2,1)S(1)} collective-permute-done((bf16[32,128]{1,0:T(8,128)(2,1)S(1)}, bf16[32,128]{1,0:T(8,128)(2,1)S(1)}, u32[]{:S(2)}, u32[]{:S(2)}) %collective-permute-start.5) | collective-permute-done | bytes 8224 | tf_op jit(solution)/shard_map/ppermute | solution.py:37
  20.0 0.5 %collective-permute-done.6.rest_2_ = bf16[32,128]{1,0:T(8,128)(2,1)S(1)} collective-permute-done((bf16[32,128]{1,0:T(8,128)(2,1)S(1)}, bf16[32,128]{1,0:T(8,128)(2,1)S(1)}, u32[]{:S(2)}, u32[]{:S(2)}) %collective-permute-start.6) | collective-permute-done | bytes 8224 | tf_op jit(solution)/shard_map/ppermute | solution.py:37
  20.5 0.9 %interact.1 = bf16[8,16,128]{2,1,0:T(8,128)(2,1)} custom-call(bf16[16,128]{1,0:T(8,128)(2,1)S(1)} %get-tuple-element.19.proj_ref, bf16[32,128]{1,0:T(8,128)(2,1)S(1)} %collective-permute-done.4.rest_0_, bf16[32,128]{1,0:T(8,128)(2,1)S(1)} %collective-permute-done.5.rest_1_, bf16[32,128]{1,0:T(8,128)(2,1)S(1)} %collective-permute-done.6.rest_2_, ...), custom_call_target="tpu_custom_call" | custom-call | tf_op jit(solution)/shard_map/interact/pallas_call | solution.py:221
Async XLA Ops:
  0.0 1.8 %collective-permute-start = (bf16[256,512]{1,0:T(8,128)(2,1)}, bf16[256,512]{1,0:T(8,128)(2,1)S(1)}, u32[]{:S(2)}, u32[]{:S(2)}) collective-permute-start(bf16[256,512]{1,0:T(8,128)(2,1)} %emb_hbm.1), channel_id=1, source_target_pairs={{0,1},{1,0},{2,3},{3,2},{4,5},{5,4},{6,7},{7,6},{8,9},{9,8},{10,11... | collective-permute-start | bytes 786440 | tf_op jit(solution)/shard_map/ppermute | solution.py:80
  1.8 11.1 %copy-start = (bf16[2,2048,1024]{2,1,0:T(8,128)(2,1)S(1)}, bf16[2,2048,1024]{2,1,0:T(8,128)(2,1)}, u32[]{:S(2)}) copy-start(bf16[2,2048,1024]{2,1,0:T(8,128)(2,1)} %w1_ref.1) | copy-start | bytes 25165828
  1.8 11.1 %copy-start.1 = (bf16[2,1024,256]{2,1,0:T(8,128)(2,1)S(1)}, bf16[2,1024,256]{2,1,0:T(8,128)(2,1)}, u32[]{:S(2)}) copy-start(bf16[2,1024,256]{2,1,0:T(8,128)(2,1)} %w2_ref.1) | copy-start | bytes 3145732
  2.2 7.3 %collective-permute-start.1 = (bf16[8,32,128]{2,1,0:T(8,128)(2,1)S(1)}, bf16[8,32,128]{2,1,0:T(8,128)(2,1)S(1)}, u32[]{:S(2)}, u32[]{:S(2)}) collective-permute-start(bf16[8,32,128]{2,1,0:T(8,128)(2,1)S(1)} %get-tuple-element.25), channel_id=1, source_target_pairs={{0,7},{1,6},{2,5},{3,4},{4,3},{5,2},{6,1},{7,0},{8,15},{9,14},{10,... | collective-permute-start | bytes 196616 | tf_op jit(solution)/shard_map/ppermute | solution.py:20
  7.0 6.0 %collective-permute-start.2 = (bf16[8,32,128]{2,1,0:T(8,128)(2,1)S(1)}, bf16[8,32,128]{2,1,0:T(8,128)(2,1)S(1)}, u32[]{:S(2)}, u32[]{:S(2)}) collective-permute-start(bf16[8,32,128]{2,1,0:T(8,128)(2,1)S(1)} %get-tuple-element.26), channel_id=1, source_target_pairs={{0,5},{1,4},{2,7},{3,6},{4,1},{5,0},{6,3},{7,2},{8,13},{9,12},{10,... | collective-permute-start | bytes 196616 | tf_op jit(solution)/shard_map/ppermute | solution.py:20
  7.0 6.0 %collective-permute-start.3 = (bf16[8,32,128]{2,1,0:T(8,128)(2,1)S(1)}, bf16[8,32,128]{2,1,0:T(8,128)(2,1)S(1)}, u32[]{:S(2)}, u32[]{:S(2)}) collective-permute-start(bf16[8,32,128]{2,1,0:T(8,128)(2,1)S(1)} %get-tuple-element.27), channel_id=1, source_target_pairs={{0,3},{1,2},{2,1},{3,0},{4,7},{5,6},{6,5},{7,4},{8,11},{9,10},{10,... | collective-permute-start | bytes 196616 | tf_op jit(solution)/shard_map/ppermute | solution.py:20
  14.7 4.0 %collective-permute-start.4 = (bf16[32,128]{1,0:T(8,128)(2,1)S(1)}, bf16[32,128]{1,0:T(8,128)(2,1)S(1)}, u32[]{:S(2)}, u32[]{:S(2)}) collective-permute-start(bf16[32,128]{1,0:T(8,128)(2,1)S(1)} %get-tuple-element.29), channel_id=1, source_target_pairs={{0,25},{1,24},{2,27},{3,26},{4,29},{5,28},{6,31},{7,30},{8,17},{9,... | collective-permute-start | bytes 24584 | tf_op jit(solution)/shard_map/ppermute | solution.py:37
  16.9 3.1 %collective-permute-start.5 = (bf16[32,128]{1,0:T(8,128)(2,1)S(1)}, bf16[32,128]{1,0:T(8,128)(2,1)S(1)}, u32[]{:S(2)}, u32[]{:S(2)}) collective-permute-start(bf16[32,128]{1,0:T(8,128)(2,1)S(1)} %get-tuple-element.30), channel_id=1, source_target_pairs={{0,17},{1,16},{2,19},{3,18},{4,21},{5,20},{6,23},{7,22},{8,25},{9,... | collective-permute-start | bytes 24584 | tf_op jit(solution)/shard_map/ppermute | solution.py:37
  17.4 3.1 %collective-permute-start.6 = (bf16[32,128]{1,0:T(8,128)(2,1)S(1)}, bf16[32,128]{1,0:T(8,128)(2,1)S(1)}, u32[]{:S(2)}, u32[]{:S(2)}) collective-permute-start(bf16[32,128]{1,0:T(8,128)(2,1)S(1)} %get-tuple-element.31), channel_id=1, source_target_pairs={{0,9},{1,8},{2,11},{3,10},{4,13},{5,12},{6,15},{7,14},{8,1},{9,0},... | collective-permute-start | bytes 24584 | tf_op jit(solution)/shard_map/ppermute | solution.py:37

commit v2 on v1

--- a/solution.py
+++ b/solution.py
@@ -39,9 +39,10 @@
 
 
 def load_kernel(count, owner_hbm, emb_hbm, *rest):
-    small, (picks_ref, emb_ref), copies = rest[:count], rest[count : count + 2], rest[count + 2 : -2]
-    owner_ref, sems = rest[-2:]
-    pairs = [(owner_hbm, owner_ref), (emb_hbm, emb_ref), *zip(small, copies)]
+    small, (picks_ref, emb_ref, slots_ref), copies = rest[:count], rest[count : count + 3], rest[count + 3 : -3]
+    owner_ref, assign_ref, sems = rest[-3:]
+    targets = (assign_ref, *copies)
+    pairs = [(owner_hbm, owner_ref), (emb_hbm, emb_ref), *zip(small, targets)]
     loads = [pltpu.make_async_copy(a, b, sems.at[i]) for i, (a, b) in enumerate(pairs)]
     for load in loads:
         load.start()
@@ -50,7 +51,10 @@
     owner = jnp.broadcast_to(owner_ref[...].reshape(1, samples), (samples, samples))
     picks = lax.broadcasted_iota(jnp.int32, (samples, samples), 0) == owner
     picks_ref[...] = jnp.where(picks, 1.0, 0.0).astype(jnp.bfloat16)
-    for load in loads[1:]:
+    loads[2].wait()
+    for slot in range(assign_ref.shape[1]):
+        slots_ref[0, assign_ref[0, slot]] = slot
+    for load in (loads[1], *loads[3:]):
         load.wait()
 
 
@@ -80,19 +84,21 @@
     parts = [lax.ppermute(embeddings, "intra", [(i, i ^ q) for i in range(intra)]) for q in range(1, pair)]
     if samples <= FEW_SAMPLES:
         given = [pltpu.with_memory_space_constraint(a, pltpu.HBM) for a in (owner, embeddings, *small)]
-        spaces = [pltpu.SMEM if jnp.issubdtype(a.dtype, jnp.integer) else pltpu.VMEM for a in small]
         picks, embeddings, *small = pl.pallas_call(
             functools.partial(load_kernel, len(small)),
             out_shape=[
                 pltpu.VMEM((samples, samples), jnp.bfloat16),
                 pltpu.VMEM(embeddings.shape, embeddings.dtype),
+                pltpu.SMEM(small[0].shape, small[0].dtype),
             ]
-            + [space(a.shape, a.dtype) for space, a in zip(spaces, small)],
+            + [pltpu.VMEM(a.shape, a.dtype) for a in small[1:]],
             in_specs=[pl.BlockSpec(memory_space=pltpu.HBM)] * len(given),
             out_specs=[pl.BlockSpec(memory_space=pltpu.VMEM)] * 2
-            + [pl.BlockSpec(memory_space=space) for space in spaces],
+            + [pl.BlockSpec(memory_space=pltpu.SMEM)]
+            + [pl.BlockSpec(memory_space=pltpu.VMEM)] * (len(small) - 1),
             scratch_shapes=[
                 pltpu.VMEM(owner.shape, owner.dtype),
+                pltpu.SMEM(small[0].shape, small[0].dtype),
                 pltpu.SemaphoreType.DMA((len(given),)),
             ],
             compiler_params=pltpu.CompilerParams(vmem_limit_bytes=8 << 20),
@@ -119,28 +125,61 @@
     for o in offsets(intra, pair):
         mine = lax.dynamic_index_in_dim(order, me ^ o, keepdims=False).reshape(-1)
         blocks.append(jnp.take(table, mine, axis=0).reshape(rows, held, EDIM).transpose(1, 0, 2))
-    return blocks, small
-
-
-def tower_kernel(towers, intra, pair, assign_ref, w1_ref, b1_ref, w2_ref, b2_ref, *rest):
-    blocks, outs, (pool_ref, x_ref, y_ref) = rest[: intra // pair], rest[intra // pair : -3], rest[-3:]
+    assign = small[0][0]
+    same = assign[None, :] == jnp.arange(assign.size)[:, None]
+    slots = jnp.sum(jnp.where(same, jnp.arange(assign.size)[None, :], 0), axis=1)
+    return blocks, (slots.astype(assign.dtype)[None, :], *small[1:])
+
+
+def first_layer(intra, pair, order, slots_ref, w1_ref, x_ref, blocks, before_ref=None):
     held, rows, _ = blocks[0].shape
     held //= pair
-    count, depth, _ = w1_ref.shape
+    count, depth, hid = w1_ref.shape
+    per_tower = depth // EDIM
+    me = lax.axis_index("intra")
+    slots = []
+    for o, block in zip(order, blocks):
+        for q in range(pair):
+            for f in range(held):
+                slot = slots_ref[0, (me ^ o ^ q) * held + f]
+                n = len(slots)
+                slots.append((slot // per_tower, pl.multiple_of((slot % per_tower) * EDIM, EDIM)))
+                for k in range(count):
+                    own = jnp.where(slots[n][0] == k, 1.0, 0.0).astype(jnp.bfloat16)
+                    x_ref[k * rows : (k + 1) * rows, n * EDIM : (n + 1) * EDIM] = block[q * held + f] * own
+    wide = 2 * EDIM
+    for h in range(0, hid, wide):
+        columns = slice(h, min(h + wide, hid))
+        total = None if before_ref is None else before_ref[:, columns]
+        for n in range(0, len(slots), 2):
+            some = slots[n : n + 2]
+            weight = [w1_ref[k, pl.ds(start, EDIM), columns] for k, start in some]
+            term = jnp.dot(
+                x_ref[:, n * EDIM : (n + len(some)) * EDIM],
+                jnp.concatenate(weight, axis=0),
+                preferred_element_type=jnp.float32,
+            )
+            total = term if total is None else total + term
+        yield columns, total
+
+
+def early_kernel(intra, pair, order, slots_ref, w1_ref, *rest):
+    blocks, out_ref, x_ref = rest[:-2], rest[-2], rest[-1]
+    for columns, total in first_layer(intra, pair, order, slots_ref, w1_ref, x_ref, blocks):
+        out_ref[:, columns] = total
+
+
+def tower_kernel(towers, intra, pair, order, slots_ref, w1_ref, b1_ref, w2_ref, b2_ref, sums_ref, *rest):
+    blocks, outs, (x_ref, hidden_ref, y_ref) = rest[: len(order)], rest[len(order) : -3], rest[-3:]
+    count, rows, _ = y_ref.shape
     vectors = w2_ref.shape[2] // EDIM
     per = rows // towers
-    slots = depth // EDIM
-    me = lax.axis_index("intra")
-    for o, block in zip(offsets(intra, pair), blocks):
-        for q in range(pair):
-            pool_ref[pl.ds((me ^ o ^ q) * held, held)] = block[q * held : (q + 1) * held]
+    for columns, total in first_layer(intra, pair, order, slots_ref, w1_ref, x_ref, blocks, sums_ref):
+        for k in range(count):
+            hidden = total[k * rows : (k + 1) * rows] + b1_ref[k : k + 1, columns]
+            hidden_ref[k, :, columns] = jnp.maximum(hidden, 0.0).astype(jnp.bfloat16)
     for k in range(count):
-        for j in range(slots):
-            x_ref[k, :, j * EDIM : (j + 1) * EDIM] = pool_ref[assign_ref[0, k * slots + j]]
-    for k in range(count):
-        hidden = jnp.dot(x_ref[k], w1_ref[k], preferred_element_type=jnp.float32)
-        hidden = jnp.maximum(hidden + b1_ref[k : k + 1, :], 0.0).astype(jnp.bfloat16)
-        result = jnp.dot(hidden, w2_ref[k], preferred_element_type=jnp.float32)
+        result = jnp.dot(hidden_ref[k], w2_ref[k], preferred_element_type=jnp.float32)
         y_ref[k] = jnp.maximum(result + b2_ref[k : k + 1, :], 0.0)
     place = lax.axis_index("tower")
     for o, out in zip(offsets(towers), outs):
@@ -153,27 +192,44 @@
         out[...] = jnp.concatenate(pieces, axis=0).astype(out.dtype)
 
 
-def run_towers(assign, w1, b1, w2, b2, blocks, towers, intra, pair):
+def run_towers(slots, w1, b1, w2, b2, blocks, towers, intra, pair):
+    order = offsets(intra, pair)
+    first = max(len(blocks) // 2 - 1, 0)
+    early, late = (*blocks[:first], blocks[-1]), tuple(blocks[first:-1])
     held, rows, _ = blocks[0].shape
-    count, depth, _ = w1.shape
+    count, depth, hid = w1.shape
     width = w2.shape[2]
     local = count * (width // EDIM) * (rows // towers)
     w1 = pltpu.with_memory_space_constraint(w1, pltpu.VMEM)
     w2 = pltpu.with_memory_space_constraint(w2, pltpu.VMEM)
+    params = pltpu.CompilerParams(vmem_limit_bytes=16 << 20)
+    sums = pl.pallas_call(
+        functools.partial(early_kernel, intra, pair, (*order[:first], order[-1])),
+        out_shape=pltpu.VMEM((count * rows, hid), jnp.float32),
+        in_specs=[pl.BlockSpec(memory_space=pltpu.SMEM)]
+        + [pl.BlockSpec(memory_space=pltpu.VMEM)] * (1 + len(early)),
+        out_specs=pl.BlockSpec(memory_space=pltpu.VMEM),
+        scratch_shapes=[pltpu.VMEM((count * rows, len(early) * held * EDIM), jnp.bfloat16)],
+        compiler_params=params,
+        cost_estimate=pl.CostEstimate(
+            flops=2 * count * rows * depth * hid, bytes_accessed=0, transcendentals=0
+        ),
+        name="towers_early",
+    )(slots, w1, *early)
     return pl.pallas_call(
-        functools.partial(tower_kernel, towers, intra, pair),
-        out_shape=[jax.ShapeDtypeStruct((local, EDIM), jnp.bfloat16)] * towers,
+        functools.partial(tower_kernel, towers, intra, pair, order[first:-1]),
+        out_shape=[pltpu.VMEM((local, EDIM), jnp.bfloat16)] * towers,
         in_specs=[pl.BlockSpec(memory_space=pltpu.SMEM)]
-        + [pl.BlockSpec(memory_space=pltpu.VMEM)] * (4 + len(blocks)),
+        + [pl.BlockSpec(memory_space=pltpu.VMEM)] * (5 + len(late)),
         out_specs=[pl.BlockSpec(memory_space=pltpu.VMEM)] * towers,
         scratch_shapes=[
-            pltpu.VMEM((len(blocks) * held, rows, EDIM), jnp.bfloat16),
-            pltpu.VMEM((count, rows, depth), jnp.bfloat16),
+            pltpu.VMEM((count * rows, max(len(late), 1) * held * EDIM), jnp.bfloat16),
+            pltpu.VMEM((count, rows, hid), jnp.bfloat16),
             pltpu.VMEM((count, rows, width), jnp.float32),
         ],
-        compiler_params=pltpu.CompilerParams(vmem_limit_bytes=16 << 20),
+        compiler_params=params,
         name="towers",
-    )(assign, w1, b1, w2, b2, *blocks)
+    )(slots, w1, b1, w2, b2, sums, *late)
 
 
 def interact_kernel(towers, proj_ref, *rest):
@@ -244,10 +300,10 @@
     ahead = 10_000 * (first_weight.size + tower_weight.size)
     pair = 2 if intra % 2 == 0 else 1
     blocks, small = gather_blocks(sample_owner, embeddings, small, towers, intra, pair, ahead)
-    feature_assign, first_bias, tower_bias, proj_weight = small
+    slots, first_bias, tower_bias, proj_weight = small
     blocks = exchange(blocks, "intra", intra, pair)
     vectors = run_towers(
-        feature_assign, first_weight, first_bias, tower_weight, tower_bias, blocks, towers, intra, pair
+        slots, first_weight, first_bias, tower_weight, tower_bias, blocks, towers, intra, pair
     )
     vectors = exchange_groups(vectors, towers, intra)
     return interact(proj_weight, vectors)

time: 21.6 us -> 20.9 us (0.968)
  waiting for transfers between devices: 8.46 us -> 7.59 us
    ppermute x3, waiting for transfers between devices: 5.34 us -> 4.46 us  [exchange(): lax.ppermute(block, axis, [(i, i ^ o) for i in range(size)])]
    pallas_call x1 -> x2, Pallas kernels: 1.72 us -> 1.93 us  [the longest x1 1.06 us: run_towers(): pl.pallas_call(functools.partial(tower_kernel, towers, intra, pair, order...]
  transfers between devices with their start and end apart: 7 -> 7, of which waited for: 6 -> 6; matrix products, arithmetic and copies ran while one was open for 0% -> 0% of each run, Pallas kernels for 5% -> 9%
where the time goes in v2:
time: 20.9 us; the launch traced here: 20.8 us
  starting transfers between devices  8.88 us (42%)
  waiting for transfers between devices  7.59 us (36%)
  Pallas kernels  4.24 us (20%)
    ppermute x3, starting transfers between devices, exchange(): lax.ppermute(block, axis, [(i, i ^ o) for i in range(size)])  5.4 us
    ppermute x3, waiting for transfers between devices, exchange(): lax.ppermute(block, axis, [(i, i ^ o) for i in range(size)])  4.46 us
    ppermute x3, starting transfers between devices, exchange_groups(): lax.ppermute(block, ('tower', 'intra'), pairs)  3.03 us
    ppermute x3, waiting for transfers between devices, exchange_groups(): lax.ppermute(block, ('tower', 'intra'), pairs)  2.79 us
    pallas_call x1, Pallas kernels, run_towers(): pl.pallas_call(functools.partial(tower_kernel, towers, intra, pair, order...  1.06 us
    pallas_call x1, Pallas kernels, gather_blocks(): pl.pallas_call(functools.partial(load_kernel, len(small)), out_shape=[plt...  1.02 us
    pallas_call x1, Pallas kernels, interact(): pl.pallas_call(functools.partial(interact_kernel, towers), out_shape=jax....  0.94 us
    pallas_call x1, Pallas kernels, run_towers(): pl.pallas_call(functools.partial(early_kernel, intra, pair, (*order[:firs...  0.87 us
  transfers between devices with their start and end apart: 7, of which 6 were waited for; matrix products, arithmetic and copies ran while one was open for 0% of the time, Pallas kernels for 9%

profile of v2, /device:TPU:0, one launch (start us, length us, event | category | flops | bytes accessed | tf_op | source)
XLA Modules:
  0.0 20.8 jit_solution(12454105846679742781)
XLA Ops:
  0.0 0.5 %collective-permute-start = (bf16[256,512]{1,0:T(8,128)(2,1)}, bf16[256,512]{1,0:T(8,128)(2,1)S(1)}, u32[]{:S(2)}, u32[]{:S(2)}) collective-permute-start(bf16[256,512]{1,0:T(8,128)(2,1)} %emb_hbm.1), channel_id=1, source_target_pairs={{0,1},{1,0},{2,3},{3,2},{4,5},{5,4},{6,7},{7,6},{8,9},{9,8},{10,11... | collective-permute-start | bytes 786440 | tf_op jit(solution)/shard_map/ppermute | solution.py:84
  0.5 1.0 %load.1 = (bf16[256,256]{1,0:T(8,128)(2,1)S(1)}, bf16[256,512]{1,0:T(8,128)(2,1)S(1)}, s32[1,32]{1,0:T(1,128)S(4)}, f32[2,1024]{1,0:T(2,128)S(1)}, f32[2,256]{1,0:T(2,128)S(1)}, /*index=5*/bf16[16,128]{1,0:T(8,128)(2,1)S(1)}) custom-call(s32[256]{0:T(256)} %owner_hbm.1, bf16[256,512]{1,0:T(8,128)(2,1)} %emb_hbm.1, s32[1,32]{1,0:T(1,128)} %rest_0_.1, ...), custom_call_target="tpu_custom_call" | custom-call | tf_op jit(solution)/shard_map/load/pallas_call | solution.py:87
  1.5 0.3 %collective-permute-done.rest_1_ = bf16[256,512]{1,0:T(8,128)(2,1)S(1)} collective-permute-done((bf16[256,512]{1,0:T(8,128)(2,1)}, bf16[256,512]{1,0:T(8,128)(2,1)S(1)}, u32[]{:S(2)}, u32[]{:S(2)}) %collective-permute-start) | collective-permute-done | bytes 262176 | tf_op jit(solution)/shard_map/ppermute | solution.py:84
  1.8 0.0 copy-start
  1.8 0.3 %gather_rows.1 = (bf16[8,32,128]{2,1,0:T(8,128)(2,1)S(1)}, bf16[8,32,128]{2,1,0:T(8,128)(2,1)S(1)}, bf16[8,32,128]{2,1,0:T(8,128)(2,1)S(1)}, bf16[8,32,128]{2,1,0:T(8,128)(2,1)S(1)}) custom-call(bf16[256,256]{1,0:T(8,128)(2,1)S(1)} %get-tuple-element.23.picks_ref, bf16[256,512]{1,0:T(8,128)(2,1)S(1)} %get-tuple-element.24.rest_0_, ...), custom_call_target="tpu_custom_call" | custom-call | flops 47185920000 | tf_op jit(solution)/shard_map/gather_rows/pallas_call | solution.py:107
  2.2 0.0 copy-start.1
  2.2 4.8 %collective-permute-start.1 = (bf16[8,32,128]{2,1,0:T(8,128)(2,1)S(1)}, bf16[8,32,128]{2,1,0:T(8,128)(2,1)S(1)}, u32[]{:S(2)}, u32[]{:S(2)}) collective-permute-start(bf16[8,32,128]{2,1,0:T(8,128)(2,1)S(1)} %get-tuple-element.25), channel_id=1, source_target_pairs={{0,7},{1,6},{2,5},{3,4},{4,3},{5,2},{6,1},{7,0},{8,15},{9,14},{10,... | collective-permute-start | bytes 196616 | tf_op jit(solution)/shard_map/ppermute | solution.py:20
  7.0 0.0 collective-permute-start.2
  7.0 0.6 %collective-permute-start.3 = (bf16[8,32,128]{2,1,0:T(8,128)(2,1)S(1)}, bf16[8,32,128]{2,1,0:T(8,128)(2,1)S(1)}, u32[]{:S(2)}, u32[]{:S(2)}) collective-permute-start(bf16[8,32,128]{2,1,0:T(8,128)(2,1)S(1)} %get-tuple-element.28), channel_id=1, source_target_pairs={{0,3},{1,2},{2,1},{3,0},{4,7},{5,6},{6,5},{7,4},{8,11},{9,10},{10,... | collective-permute-start | bytes 196616 | tf_op jit(solution)/shard_map/ppermute | solution.py:20
  7.6 1.9 %collective-permute-done.1.rest_0_ = bf16[8,32,128]{2,1,0:T(8,128)(2,1)S(1)} collective-permute-done((bf16[8,32,128]{2,1,0:T(8,128)(2,1)S(1)}, bf16[8,32,128]{2,1,0:T(8,128)(2,1)S(1)}, u32[]{:S(2)}, u32[]{:S(2)}) %collective-permute-start.1) | collective-permute-done | bytes 65568 | tf_op jit(solution)/shard_map/ppermute | solution.py:20
  9.5 0.0 copy-done
  9.5 0.9 %towers_early.1.sums_ref = f32[64,1024]{1,0:T(8,128)S(1)} custom-call(s32[1,32]{1,0:T(1,128)S(4)} %get-tuple-element.20.slots_ref, bf16[2,2048,1024]{2,1,0:T(8,128)(2,1)S(1)} %copy-done, bf16[8,32,128]{2,1,0:T(8,128)(2,1)S(1)} %collective-permute-done.1.rest_0_, bf16[8,32,128]{2,1,0:T(8,128)(2,1)S(1)} %get-tuple-element.26.rest_1_), custom_call_target="tpu_custom_call" | custom-call | flops 268435456 | tf_op jit(solution)/shard_map/towers_early/pallas_call | solution.py:206
  10.4 2.5 %collective-permute-done.2.rest_0_ = bf16[8,32,128]{2,1,0:T(8,128)(2,1)S(1)} collective-permute-done((bf16[8,32,128]{2,1,0:T(8,128)(2,1)S(1)}, bf16[8,32,128]{2,1,0:T(8,128)(2,1)S(1)}, u32[]{:S(2)}, u32[]{:S(2)}) %collective-permute-start.2) | collective-permute-done | bytes 65568 | tf_op jit(solution)/shard_map/ppermute | solution.py:20
  12.9 0.0 collective-permute-done.3.rest_1_
  12.9 0.0 copy-done.1
  12.9 1.1 %towers.1 = (bf16[32,128]{1,0:T(8,128)(2,1)S(1)}, bf16[32,128]{1,0:T(8,128)(2,1)S(1)}, bf16[32,128]{1,0:T(8,128)(2,1)S(1)}, bf16[32,128]{1,0:T(8,128)(2,1)S(1)}) custom-call(s32[1,32]{1,0:T(1,128)S(4)} %get-tuple-element.20.slots_ref, bf16[2,2048,1024]{2,1,0:T(8,128)(2,1)S(1)} %copy-done, f32[2,1024]{1,0:T(2,128)S(1)} %get-tuple-element.21.b1_ref, ...), custom_call_target="tpu_custom_call" | custom-call | tf_op jit(solution)/shard_map/towers/pallas_call | solution.py:219
  14.0 2.3 %collective-permute-start.4 = (bf16[32,128]{1,0:T(8,128)(2,1)S(1)}, bf16[32,128]{1,0:T(8,128)(2,1)S(1)}, u32[]{:S(2)}, u32[]{:S(2)}) collective-permute-start(bf16[32,128]{1,0:T(8,128)(2,1)S(1)} %get-tuple-element.29), channel_id=1, source_target_pairs={{0,25},{1,24},{2,27},{3,26},{4,29},{5,28},{6,31},{7,30},{8,17},{9,... | collective-permute-start | bytes 24584 | tf_op jit(solution)/shard_map/ppermute | solution.py:37
  16.3 0.5 %collective-permute-start.5 = (bf16[32,128]{1,0:T(8,128)(2,1)S(1)}, bf16[32,128]{1,0:T(8,128)(2,1)S(1)}, u32[]{:S(2)}, u32[]{:S(2)}) collective-permute-start(bf16[32,128]{1,0:T(8,128)(2,1)S(1)} %get-tuple-element.30), channel_id=1, source_target_pairs={{0,17},{1,16},{2,19},{3,18},{4,21},{5,20},{6,23},{7,22},{8,25},{9,... | collective-permute-start | bytes 24584 | tf_op jit(solution)/shard_map/ppermute | solution.py:37
  16.7 0.3 %collective-permute-start.6 = (bf16[32,128]{1,0:T(8,128)(2,1)S(1)}, bf16[32,128]{1,0:T(8,128)(2,1)S(1)}, u32[]{:S(2)}, u32[]{:S(2)}) collective-permute-start(bf16[32,128]{1,0:T(8,128)(2,1)S(1)} %get-tuple-element.31), channel_id=1, source_target_pairs={{0,9},{1,8},{2,11},{3,10},{4,13},{5,12},{6,15},{7,14},{8,1},{9,0},... | collective-permute-start | bytes 24584 | tf_op jit(solution)/shard_map/ppermute | solution.py:37
  17.0 1.0 %collective-permute-done.4.rest_0_ = bf16[32,128]{1,0:T(8,128)(2,1)S(1)} collective-permute-done((bf16[32,128]{1,0:T(8,128)(2,1)S(1)}, bf16[32,128]{1,0:T(8,128)(2,1)S(1)}, u32[]{:S(2)}, u32[]{:S(2)}) %collective-permute-start.4) | collective-permute-done | bytes 8224 | tf_op jit(solution)/shard_map/ppermute | solution.py:37
  18.0 1.3 %collective-permute-done.5.rest_1_ = bf16[32,128]{1,0:T(8,128)(2,1)S(1)} collective-permute-done((bf16[32,128]{1,0:T(8,128)(2,1)S(1)}, bf16[32,128]{1,0:T(8,128)(2,1)S(1)}, u32[]{:S(2)}, u32[]{:S(2)}) %collective-permute-start.5) | collective-permute-done | bytes 8224 | tf_op jit(solution)/shard_map/ppermute | solution.py:37
  19.4 0.5 %collective-permute-done.6.rest_2_ = bf16[32,128]{1,0:T(8,128)(2,1)S(1)} collective-permute-done((bf16[32,128]{1,0:T(8,128)(2,1)S(1)}, bf16[32,128]{1,0:T(8,128)(2,1)S(1)}, u32[]{:S(2)}, u32[]{:S(2)}) %collective-permute-start.6) | collective-permute-done | bytes 8224 | tf_op jit(solution)/shard_map/ppermute | solution.py:37
  19.8 0.9 %interact.1 = bf16[8,16,128]{2,1,0:T(8,128)(2,1)} custom-call(bf16[16,128]{1,0:T(8,128)(2,1)S(1)} %get-tuple-element.19.proj_ref, bf16[32,128]{1,0:T(8,128)(2,1)S(1)} %collective-permute-done.4.rest_0_, bf16[32,128]{1,0:T(8,128)(2,1)S(1)} %collective-permute-done.5.rest_1_, bf16[32,128]{1,0:T(8,128)(2,1)S(1)} %collective-permute-done.6.rest_2_, ...), custom_call_target="tpu_custom_call" | custom-call | tf_op jit(solution)/shard_map/interact/pallas_call | solution.py:277
Async XLA Ops:
  0.0 1.8 %collective-permute-start = (bf16[256,512]{1,0:T(8,128)(2,1)}, bf16[256,512]{1,0:T(8,128)(2,1)S(1)}, u32[]{:S(2)}, u32[]{:S(2)}) collective-permute-start(bf16[256,512]{1,0:T(8,128)(2,1)} %emb_hbm.1), channel_id=1, source_target_pairs={{0,1},{1,0},{2,3},{3,2},{4,5},{5,4},{6,7},{7,6},{8,9},{9,8},{10,11... | collective-permute-start | bytes 786440 | tf_op jit(solution)/shard_map/ppermute | solution.py:84
  1.8 7.7 %copy-start = (bf16[2,2048,1024]{2,1,0:T(8,128)(2,1)S(1)}, bf16[2,2048,1024]{2,1,0:T(8,128)(2,1)}, u32[]{:S(2)}) copy-start(bf16[2,2048,1024]{2,1,0:T(8,128)(2,1)} %w1_ref.3) | copy-start | bytes 25165828
  2.2 10.8 %copy-start.1 = (bf16[2,1024,256]{2,1,0:T(8,128)(2,1)S(1)}, bf16[2,1024,256]{2,1,0:T(8,128)(2,1)}, u32[]{:S(2)}) copy-start(bf16[2,1024,256]{2,1,0:T(8,128)(2,1)} %w2_ref.1) | copy-start | bytes 3145732
  2.2 7.3 %collective-permute-start.1 = (bf16[8,32,128]{2,1,0:T(8,128)(2,1)S(1)}, bf16[8,32,128]{2,1,0:T(8,128)(2,1)S(1)}, u32[]{:S(2)}, u32[]{:S(2)}) collective-permute-start(bf16[8,32,128]{2,1,0:T(8,128)(2,1)S(1)} %get-tuple-element.25), channel_id=1, source_target_pairs={{0,7},{1,6},{2,5},{3,4},{4,3},{5,2},{6,1},{7,0},{8,15},{9,14},{10,... | collective-permute-start | bytes 196616 | tf_op jit(solution)/shard_map/ppermute | solution.py:20
  7.0 6.0 %collective-permute-start.2 = (bf16[8,32,128]{2,1,0:T(8,128)(2,1)S(1)}, bf16[8,32,128]{2,1,0:T(8,128)(2,1)S(1)}, u32[]{:S(2)}, u32[]{:S(2)}) collective-permute-start(bf16[8,32,128]{2,1,0:T(8,128)(2,1)S(1)} %get-tuple-element.27), channel_id=1, source_target_pairs={{0,5},{1,4},{2,7},{3,6},{4,1},{5,0},{6,3},{7,2},{8,13},{9,12},{10,... | collective-permute-start | bytes 196616 | tf_op jit(solution)/shard_map/ppermute | solution.py:20
  7.0 6.0 %collective-permute-start.3 = (bf16[8,32,128]{2,1,0:T(8,128)(2,1)S(1)}, bf16[8,32,128]{2,1,0:T(8,128)(2,1)S(1)}, u32[]{:S(2)}, u32[]{:S(2)}) collective-permute-start(bf16[8,32,128]{2,1,0:T(8,128)(2,1)S(1)} %get-tuple-element.28), channel_id=1, source_target_pairs={{0,3},{1,2},{2,1},{3,0},{4,7},{5,6},{6,5},{7,4},{8,11},{9,10},{10,... | collective-permute-start | bytes 196616 | tf_op jit(solution)/shard_map/ppermute | solution.py:20
  14.0 4.0 %collective-permute-start.4 = (bf16[32,128]{1,0:T(8,128)(2,1)S(1)}, bf16[32,128]{1,0:T(8,128)(2,1)S(1)}, u32[]{:S(2)}, u32[]{:S(2)}) collective-permute-start(bf16[32,128]{1,0:T(8,128)(2,1)S(1)} %get-tuple-element.29), channel_id=1, source_target_pairs={{0,25},{1,24},{2,27},{3,26},{4,29},{5,28},{6,31},{7,30},{8,17},{9,... | collective-permute-start | bytes 24584 | tf_op jit(solution)/shard_map/ppermute | solution.py:37
  16.3 3.1 %collective-permute-start.5 = (bf16[32,128]{1,0:T(8,128)(2,1)S(1)}, bf16[32,128]{1,0:T(8,128)(2,1)S(1)}, u32[]{:S(2)}, u32[]{:S(2)}) collective-permute-start(bf16[32,128]{1,0:T(8,128)(2,1)S(1)} %get-tuple-element.30), channel_id=1, source_target_pairs={{0,17},{1,16},{2,19},{3,18},{4,21},{5,20},{6,23},{7,22},{8,25},{9,... | collective-permute-start | bytes 24584 | tf_op jit(solution)/shard_map/ppermute | solution.py:37
  16.7 3.1 %collective-permute-start.6 = (bf16[32,128]{1,0:T(8,128)(2,1)S(1)}, bf16[32,128]{1,0:T(8,128)(2,1)S(1)}, u32[]{:S(2)}, u32[]{:S(2)}) collective-permute-start(bf16[32,128]{1,0:T(8,128)(2,1)S(1)} %get-tuple-element.31), channel_id=1, source_target_pairs={{0,9},{1,8},{2,11},{3,10},{4,13},{5,12},{6,15},{7,14},{8,1},{9,0},... | collective-permute-start | bytes 24584 | tf_op jit(solution)/shard_map/ppermute | solution.py:37

commit v3 on v2

--- a/solution.py
+++ b/solution.py
@@ -11,14 +11,23 @@
 FEW_SAMPLES = 1024
 
 
-def offsets(size, step=1):
-    return [o + step - 1 if o else 0 for o in range(size - step, -1, -step)]
-
-
-def exchange(blocks, axis, size, step=1):
+def offsets(size):
+    return range(size - 1, -1, -1)
+
+
+def steps(intra, pair):
+    return (*range(1, intra // pair), 0)
+
+
+def partner(me, step, intra, pair):
+    chips = intra // pair
+    return (me // pair + step + chips) % chips * pair + (me % pair + (pair - 1 if step else 0)) % pair
+
+
+def exchange_chips(blocks, intra, pair):
     return [
-        lax.ppermute(block, axis, [(i, i ^ o) for i in range(size)]) if o else block
-        for block, o in zip(blocks, offsets(size, step))
+        lax.ppermute(block, "intra", [(i, partner(i, s, intra, pair)) for i in range(intra)]) if s else block
+        for block, s in zip(blocks, steps(intra, pair))
     ]
 
 
@@ -68,8 +77,8 @@
         acc_ref[:, q * width : (q + 1) * width] = lax.dot_general(
             picks_ref[...], part[...], (((0,), (0,)), ((), ())), preferred_element_type=jnp.float32
         )
-    for o, out in zip(offsets(intra, pair), outs):
-        block = me ^ o
+    for s, out in zip(steps(intra, pair), outs):
+        block = partner(me, s, intra, pair)
         owners = [jnp.where(place == t, block, block ^ other_core(intra)) for t in range(towers)]
         starts = [pl.multiple_of((t * intra + owners[t]) * per, per) for t in range(towers)]
         for f in range(pair * held):
@@ -122,8 +131,8 @@
     me = lax.axis_index("intra")
     table = jnp.concatenate([embeddings, *parts], axis=1)
     blocks = []
-    for o in offsets(intra, pair):
-        mine = lax.dynamic_index_in_dim(order, me ^ o, keepdims=False).reshape(-1)
+    for s in steps(intra, pair):
+        mine = lax.dynamic_index_in_dim(order, partner(me, s, intra, pair), keepdims=False).reshape(-1)
         blocks.append(jnp.take(table, mine, axis=0).reshape(rows, held, EDIM).transpose(1, 0, 2))
     assign = small[0][0]
     same = assign[None, :] == jnp.arange(assign.size)[:, None]
@@ -138,10 +147,11 @@
     per_tower = depth // EDIM
     me = lax.axis_index("intra")
     slots = []
-    for o, block in zip(order, blocks):
+    for s, block in zip(order, blocks):
+        source = partner(me, -s, intra, pair)
         for q in range(pair):
             for f in range(held):
-                slot = slots_ref[0, (me ^ o ^ q) * held + f]
+                slot = slots_ref[0, (source ^ q) * held + f]
                 n = len(slots)
                 slots.append((slot // per_tower, pl.multiple_of((slot % per_tower) * EDIM, EDIM)))
                 for k in range(count):
@@ -193,7 +203,7 @@
 
 
 def run_towers(slots, w1, b1, w2, b2, blocks, towers, intra, pair):
-    order = offsets(intra, pair)
+    order = steps(intra, pair)
     first = max(len(blocks) // 2 - 1, 0)
     early, late = (*blocks[:first], blocks[-1]), tuple(blocks[first:-1])
     held, rows, _ = blocks[0].shape
@@ -301,7 +311,7 @@
     pair = 2 if intra % 2 == 0 else 1
     blocks, small = gather_blocks(sample_owner, embeddings, small, towers, intra, pair, ahead)
     slots, first_bias, tower_bias, proj_weight = small
-    blocks = exchange(blocks, "intra", intra, pair)
+    blocks = exchange_chips(blocks, intra, pair)
     vectors = run_towers(
         slots, first_weight, first_bias, tower_weight, tower_bias, blocks, towers, intra, pair
     )

time: 20.9 us -> 20.9 us (level)
  waiting for transfers between devices: 7.59 us -> 6.51 us
  starting transfers between devices: 8.88 us -> 9.89 us
    ppermute x3, waiting for transfers between devices: 4.46 us -> 3.26 us  [exchange_chips(): lax.ppermute(block, 'intra', [(i, partner(i, s, intra, pair)) for i in ra...]
    ppermute x3, starting transfers between devices: 5.4 us -> 6.41 us  [exchange_chips(): lax.ppermute(block, 'intra', [(i, partner(i, s, intra, pair)) for i in ra...]
  transfers between devices with their start and end apart: 7 -> 7, of which waited for: 6 -> 7; matrix products, arithmetic and copies ran while one was open for 0% -> 0% of each run, Pallas kernels for 9% -> 9%
where the time goes in v3:
time: 20.9 us; the launch traced here: 20.7 us
  starting transfers between devices  9.89 us (47%)
  waiting for transfers between devices  6.51 us (31%)
  Pallas kernels  4.24 us (20%)
    ppermute x3, starting transfers between devices, exchange_chips(): lax.ppermute(block, 'intra', [(i, partner(i, s, intra, pair)) for i in ra...  6.41 us
    ppermute x3, waiting for transfers between devices, exchange_chips(): lax.ppermute(block, 'intra', [(i, partner(i, s, intra, pair)) for i in ra...  3.26 us
    ppermute x3, starting transfers between devices, exchange_groups(): lax.ppermute(block, ('tower', 'intra'), pairs)  3.03 us
    ppermute x3, waiting for transfers between devices, exchange_groups(): lax.ppermute(block, ('tower', 'intra'), pairs)  2.91 us
    pallas_call x1, Pallas kernels, run_towers(): pl.pallas_call(functools.partial(tower_kernel, towers, intra, pair, order...  1.06 us
    pallas_call x1, Pallas kernels, gather_blocks(): pl.pallas_call(functools.partial(load_kernel, len(small)), out_shape=[plt...  1.02 us
    pallas_call x1, Pallas kernels, interact(): pl.pallas_call(functools.partial(interact_kernel, towers), out_shape=jax....  0.94 us
    pallas_call x1, Pallas kernels, run_towers(): pl.pallas_call(functools.partial(early_kernel, intra, pair, (*order[:firs...  0.87 us
  transfers between devices with their start and end apart: 7, of which 7 were waited for; matrix products, arithmetic and copies ran while one was open for 0% of the time, Pallas kernels for 9%

profile of v3, /device:TPU:0, one launch (start us, length us, event | category | flops | bytes accessed | tf_op | source)
XLA Modules:
  0.0 20.7 jit_solution(3668750937568118735)
XLA Ops:
  0.0 0.5 %collective-permute-start = (bf16[256,512]{1,0:T(8,128)(2,1)}, bf16[256,512]{1,0:T(8,128)(2,1)S(1)}, u32[]{:S(2)}, u32[]{:S(2)}) collective-permute-start(bf16[256,512]{1,0:T(8,128)(2,1)} %emb_hbm.1), channel_id=1, source_target_pairs={{0,1},{1,0},{2,3},{3,2},{4,5},{5,4},{6,7},{7,6},{8,9},{9,8},{10,11... | collective-permute-start | bytes 786440 | tf_op jit(solution)/shard_map/ppermute | solution.py:93
  0.5 1.0 %load.1 = (bf16[256,256]{1,0:T(8,128)(2,1)S(1)}, bf16[256,512]{1,0:T(8,128)(2,1)S(1)}, s32[1,32]{1,0:T(1,128)S(4)}, f32[2,1024]{1,0:T(2,128)S(1)}, f32[2,256]{1,0:T(2,128)S(1)}, /*index=5*/bf16[16,128]{1,0:T(8,128)(2,1)S(1)}) custom-call(s32[256]{0:T(256)} %owner_hbm.1, bf16[256,512]{1,0:T(8,128)(2,1)} %emb_hbm.1, s32[1,32]{1,0:T(1,128)} %rest_0_.1, ...), custom_call_target="tpu_custom_call" | custom-call | tf_op jit(solution)/shard_map/load/pallas_call | solution.py:96
  1.5 0.3 %collective-permute-done.rest_1_ = bf16[256,512]{1,0:T(8,128)(2,1)S(1)} collective-permute-done((bf16[256,512]{1,0:T(8,128)(2,1)}, bf16[256,512]{1,0:T(8,128)(2,1)S(1)}, u32[]{:S(2)}, u32[]{:S(2)}) %collective-permute-start) | collective-permute-done | bytes 262176 | tf_op jit(solution)/shard_map/ppermute | solution.py:93
  1.8 0.0 copy-start
  1.8 0.3 %gather_rows.1 = (bf16[8,32,128]{2,1,0:T(8,128)(2,1)S(1)}, bf16[8,32,128]{2,1,0:T(8,128)(2,1)S(1)}, bf16[8,32,128]{2,1,0:T(8,128)(2,1)S(1)}, bf16[8,32,128]{2,1,0:T(8,128)(2,1)S(1)}) custom-call(bf16[256,256]{1,0:T(8,128)(2,1)S(1)} %get-tuple-element.23.picks_ref, bf16[256,512]{1,0:T(8,128)(2,1)S(1)} %get-tuple-element.24.rest_0_, ...), custom_call_target="tpu_custom_call" | custom-call | flops 47185920000 | tf_op jit(solution)/shard_map/gather_rows/pallas_call | solution.py:116
  2.2 0.0 copy-start.1
  2.2 2.7 %collective-permute-start.1 = (bf16[8,32,128]{2,1,0:T(8,128)(2,1)S(1)}, bf16[8,32,128]{2,1,0:T(8,128)(2,1)S(1)}, u32[]{:S(2)}, u32[]{:S(2)}) collective-permute-start(bf16[8,32,128]{2,1,0:T(8,128)(2,1)S(1)} %get-tuple-element.25), channel_id=1, source_target_pairs={{0,3},{1,2},{2,5},{3,4},{4,7},{5,6},{6,1},{7,0},{8,11},{9,10},{10,... | collective-permute-start | bytes 196616 | tf_op jit(solution)/shard_map/ppermute | solution.py:29
  4.9 2.6 %collective-permute-start.2 = (bf16[8,32,128]{2,1,0:T(8,128)(2,1)S(1)}, bf16[8,32,128]{2,1,0:T(8,128)(2,1)S(1)}, u32[]{:S(2)}, u32[]{:S(2)}) collective-permute-start(bf16[8,32,128]{2,1,0:T(8,128)(2,1)S(1)} %get-tuple-element.27), channel_id=1, source_target_pairs={{0,5},{1,4},{2,7},{3,6},{4,1},{5,0},{6,3},{7,2},{8,13},{9,12},{10,... | collective-permute-start | bytes 196616 | tf_op jit(solution)/shard_map/ppermute | solution.py:29
  7.5 1.1 %collective-permute-start.3 = (bf16[8,32,128]{2,1,0:T(8,128)(2,1)S(1)}, bf16[8,32,128]{2,1,0:T(8,128)(2,1)S(1)}, u32[]{:S(2)}, u32[]{:S(2)}) collective-permute-start(bf16[8,32,128]{2,1,0:T(8,128)(2,1)S(1)} %get-tuple-element.28), channel_id=1, source_target_pairs={{0,7},{1,6},{2,1},{3,0},{4,3},{5,2},{6,5},{7,4},{8,15},{9,14},{10,... | collective-permute-start | bytes 196616 | tf_op jit(solution)/shard_map/ppermute | solution.py:29
  8.6 0.5 %collective-permute-done.1.rest_0_ = bf16[8,32,128]{2,1,0:T(8,128)(2,1)S(1)} collective-permute-done((bf16[8,32,128]{2,1,0:T(8,128)(2,1)S(1)}, bf16[8,32,128]{2,1,0:T(8,128)(2,1)S(1)}, u32[]{:S(2)}, u32[]{:S(2)}) %collective-permute-start.1) | collective-permute-done | bytes 65568 | tf_op jit(solution)/shard_map/ppermute | solution.py:29
  9.2 0.0 copy-done
  9.2 0.9 %towers_early.1.sums_ref = f32[64,1024]{1,0:T(8,128)S(1)} custom-call(s32[1,32]{1,0:T(1,128)S(4)} %get-tuple-element.20.slots_ref, bf16[2,2048,1024]{2,1,0:T(8,128)(2,1)S(1)} %copy-done, bf16[8,32,128]{2,1,0:T(8,128)(2,1)S(1)} %collective-permute-done.1.rest_0_, bf16[8,32,128]{2,1,0:T(8,128)(2,1)S(1)} %get-tuple-element.26.rest_1_), custom_call_target="tpu_custom_call" | custom-call | flops 268435456 | tf_op jit(solution)/shard_map/towers_early/pallas_call | solution.py:216
  10.0 2.4 %collective-permute-done.2.rest_0_ = bf16[8,32,128]{2,1,0:T(8,128)(2,1)S(1)} collective-permute-done((bf16[8,32,128]{2,1,0:T(8,128)(2,1)S(1)}, bf16[8,32,128]{2,1,0:T(8,128)(2,1)S(1)}, u32[]{:S(2)}, u32[]{:S(2)}) %collective-permute-start.2) | collective-permute-done | bytes 65568 | tf_op jit(solution)/shard_map/ppermute | solution.py:29
  12.5 0.3 %collective-permute-done.3.rest_1_ = bf16[8,32,128]{2,1,0:T(8,128)(2,1)S(1)} collective-permute-done((bf16[8,32,128]{2,1,0:T(8,128)(2,1)S(1)}, bf16[8,32,128]{2,1,0:T(8,128)(2,1)S(1)}, u32[]{:S(2)}, u32[]{:S(2)}) %collective-permute-start.3) | collective-permute-done | bytes 65568 | tf_op jit(solution)/shard_map/ppermute | solution.py:29
  12.7 0.0 copy-done.1
  12.7 1.1 %towers.1 = (bf16[32,128]{1,0:T(8,128)(2,1)S(1)}, bf16[32,128]{1,0:T(8,128)(2,1)S(1)}, bf16[32,128]{1,0:T(8,128)(2,1)S(1)}, bf16[32,128]{1,0:T(8,128)(2,1)S(1)}) custom-call(s32[1,32]{1,0:T(1,128)S(4)} %get-tuple-element.20.slots_ref, bf16[2,2048,1024]{2,1,0:T(8,128)(2,1)S(1)} %copy-done, f32[2,1024]{1,0:T(2,128)S(1)} %get-tuple-element.21.b1_ref, ...), custom_call_target="tpu_custom_call" | custom-call | tf_op jit(solution)/shard_map/towers/pallas_call | solution.py:229
  13.8 2.4 %collective-permute-start.4 = (bf16[32,128]{1,0:T(8,128)(2,1)S(1)}, bf16[32,128]{1,0:T(8,128)(2,1)S(1)}, u32[]{:S(2)}, u32[]{:S(2)}) collective-permute-start(bf16[32,128]{1,0:T(8,128)(2,1)S(1)} %get-tuple-element.29), channel_id=1, source_target_pairs={{0,25},{1,24},{2,27},{3,26},{4,29},{5,28},{6,31},{7,30},{8,17},{9,... | collective-permute-start | bytes 24584 | tf_op jit(solution)/shard_map/ppermute | solution.py:46
  16.2 0.5 %collective-permute-start.5 = (bf16[32,128]{1,0:T(8,128)(2,1)S(1)}, bf16[32,128]{1,0:T(8,128)(2,1)S(1)}, u32[]{:S(2)}, u32[]{:S(2)}) collective-permute-start(bf16[32,128]{1,0:T(8,128)(2,1)S(1)} %get-tuple-element.30), channel_id=1, source_target_pairs={{0,17},{1,16},{2,19},{3,18},{4,21},{5,20},{6,23},{7,22},{8,25},{9,... | collective-permute-start | bytes 24584 | tf_op jit(solution)/shard_map/ppermute | solution.py:46
  16.7 0.2 collective-permute-start.6
  16.8 1.0 %collective-permute-done.4.rest_0_ = bf16[32,128]{1,0:T(8,128)(2,1)S(1)} collective-permute-done((bf16[32,128]{1,0:T(8,128)(2,1)S(1)}, bf16[32,128]{1,0:T(8,128)(2,1)S(1)}, u32[]{:S(2)}, u32[]{:S(2)}) %collective-permute-start.4) | collective-permute-done | bytes 8224 | tf_op jit(solution)/shard_map/ppermute | solution.py:46
  17.9 1.4 %collective-permute-done.5.rest_1_ = bf16[32,128]{1,0:T(8,128)(2,1)S(1)} collective-permute-done((bf16[32,128]{1,0:T(8,128)(2,1)S(1)}, bf16[32,128]{1,0:T(8,128)(2,1)S(1)}, u32[]{:S(2)}, u32[]{:S(2)}) %collective-permute-start.5) | collective-permute-done | bytes 8224 | tf_op jit(solution)/shard_map/ppermute | solution.py:46
  19.3 0.5 %collective-permute-done.6.rest_2_ = bf16[32,128]{1,0:T(8,128)(2,1)S(1)} collective-permute-done((bf16[32,128]{1,0:T(8,128)(2,1)S(1)}, bf16[32,128]{1,0:T(8,128)(2,1)S(1)}, u32[]{:S(2)}, u32[]{:S(2)}) %collective-permute-start.6) | collective-permute-done | bytes 8224 | tf_op jit(solution)/shard_map/ppermute | solution.py:46
  19.8 0.9 %interact.1 = bf16[8,16,128]{2,1,0:T(8,128)(2,1)} custom-call(bf16[16,128]{1,0:T(8,128)(2,1)S(1)} %get-tuple-element.19.proj_ref, bf16[32,128]{1,0:T(8,128)(2,1)S(1)} %collective-permute-done.4.rest_0_, bf16[32,128]{1,0:T(8,128)(2,1)S(1)} %collective-permute-done.5.rest_1_, bf16[32,128]{1,0:T(8,128)(2,1)S(1)} %collective-permute-done.6.rest_2_, ...), custom_call_target="tpu_custom_call" | custom-call | tf_op jit(solution)/shard_map/interact/pallas_call | solution.py:287
Async XLA Ops:
  0.0 1.8 %collective-permute-start = (bf16[256,512]{1,0:T(8,128)(2,1)}, bf16[256,512]{1,0:T(8,128)(2,1)S(1)}, u32[]{:S(2)}, u32[]{:S(2)}) collective-permute-start(bf16[256,512]{1,0:T(8,128)(2,1)} %emb_hbm.1), channel_id=1, source_target_pairs={{0,1},{1,0},{2,3},{3,2},{4,5},{5,4},{6,7},{7,6},{8,9},{9,8},{10,11... | collective-permute-start | bytes 786440 | tf_op jit(solution)/shard_map/ppermute | solution.py:93
  1.8 7.3 %copy-start = (bf16[2,2048,1024]{2,1,0:T(8,128)(2,1)S(1)}, bf16[2,2048,1024]{2,1,0:T(8,128)(2,1)}, u32[]{:S(2)}) copy-start(bf16[2,2048,1024]{2,1,0:T(8,128)(2,1)} %w1_ref.3) | copy-start | bytes 25165828
  2.2 10.6 %copy-start.1 = (bf16[2,1024,256]{2,1,0:T(8,128)(2,1)S(1)}, bf16[2,1024,256]{2,1,0:T(8,128)(2,1)}, u32[]{:S(2)}) copy-start(bf16[2,1024,256]{2,1,0:T(8,128)(2,1)} %w2_ref.1) | copy-start | bytes 3145732
  2.2 7.0 %collective-permute-start.1 = (bf16[8,32,128]{2,1,0:T(8,128)(2,1)S(1)}, bf16[8,32,128]{2,1,0:T(8,128)(2,1)S(1)}, u32[]{:S(2)}, u32[]{:S(2)}) collective-permute-start(bf16[8,32,128]{2,1,0:T(8,128)(2,1)S(1)} %get-tuple-element.25), channel_id=1, source_target_pairs={{0,3},{1,2},{2,5},{3,4},{4,7},{5,6},{6,1},{7,0},{8,11},{9,10},{10,... | collective-permute-start | bytes 196616 | tf_op jit(solution)/shard_map/ppermute | solution.py:29
  4.9 7.5 %collective-permute-start.2 = (bf16[8,32,128]{2,1,0:T(8,128)(2,1)S(1)}, bf16[8,32,128]{2,1,0:T(8,128)(2,1)S(1)}, u32[]{:S(2)}, u32[]{:S(2)}) collective-permute-start(bf16[8,32,128]{2,1,0:T(8,128)(2,1)S(1)} %get-tuple-element.27), channel_id=1, source_target_pairs={{0,5},{1,4},{2,7},{3,6},{4,1},{5,0},{6,3},{7,2},{8,13},{9,12},{10,... | collective-permute-start | bytes 196616 | tf_op jit(solution)/shard_map/ppermute | solution.py:29
  7.5 5.2 %collective-permute-start.3 = (bf16[8,32,128]{2,1,0:T(8,128)(2,1)S(1)}, bf16[8,32,128]{2,1,0:T(8,128)(2,1)S(1)}, u32[]{:S(2)}, u32[]{:S(2)}) collective-permute-start(bf16[8,32,128]{2,1,0:T(8,128)(2,1)S(1)} %get-tuple-element.28), channel_id=1, source_target_pairs={{0,7},{1,6},{2,1},{3,0},{4,3},{5,2},{6,5},{7,4},{8,15},{9,14},{10,... | collective-permute-start | bytes 196616 | tf_op jit(solution)/shard_map/ppermute | solution.py:29
  13.8 4.0 %collective-permute-start.4 = (bf16[32,128]{1,0:T(8,128)(2,1)S(1)}, bf16[32,128]{1,0:T(8,128)(2,1)S(1)}, u32[]{:S(2)}, u32[]{:S(2)}) collective-permute-start(bf16[32,128]{1,0:T(8,128)(2,1)S(1)} %get-tuple-element.29), channel_id=1, source_target_pairs={{0,25},{1,24},{2,27},{3,26},{4,29},{5,28},{6,31},{7,30},{8,17},{9,... | collective-permute-start | bytes 24584 | tf_op jit(solution)/shard_map/ppermute | solution.py:46
  16.2 3.1 %collective-permute-start.5 = (bf16[32,128]{1,0:T(8,128)(2,1)S(1)}, bf16[32,128]{1,0:T(8,128)(2,1)S(1)}, u32[]{:S(2)}, u32[]{:S(2)}) collective-permute-start(bf16[32,128]{1,0:T(8,128)(2,1)S(1)} %get-tuple-element.30), channel_id=1, source_target_pairs={{0,17},{1,16},{2,19},{3,18},{4,21},{5,20},{6,23},{7,22},{8,25},{9,... | collective-permute-start | bytes 24584 | tf_op jit(solution)/shard_map/ppermute | solution.py:46
  16.7 3.1 %collective-permute-start.6 = (bf16[32,128]{1,0:T(8,128)(2,1)S(1)}, bf16[32,128]{1,0:T(8,128)(2,1)S(1)}, u32[]{:S(2)}, u32[]{:S(2)}) collective-permute-start(bf16[32,128]{1,0:T(8,128)(2,1)S(1)} %get-tuple-element.31), channel_id=1, source_target_pairs={{0,9},{1,8},{2,11},{3,10},{4,13},{5,12},{6,15},{7,14},{8,1},{9,0},... | collective-permute-start | bytes 24584 | tf_op jit(solution)/shard_map/ppermute | solution.py:46

commit v4 on v3

--- a/solution.py
+++ b/solution.py
@@ -19,9 +19,22 @@
     return (*range(1, intra // pair), 0)
 
 
+def ring_place(chip, chips):
+    place = chip
+    bits = (chips - 1).bit_length() if chips & (chips - 1) == 0 else 0
+    for n in range(1, bits):
+        place = place ^ (chip >> n)
+    return place
+
+
+def ring_chip(place, chips):
+    return place ^ (place >> 1) if chips & (chips - 1) == 0 else place
+
+
 def partner(me, step, intra, pair):
     chips = intra // pair
-    return (me // pair + step + chips) % chips * pair + (me % pair + (pair - 1 if step else 0)) % pair
+    place = (ring_place(me // pair, chips) + step + chips) % chips
+    return ring_chip(place, chips) * pair + (me % pair + (pair - 1 if step else 0)) % pair
 
 
 def exchange_chips(blocks, intra, pair):

time: 20.9 us -> 20.7 us (level)
  waiting for transfers between devices: 6.51 us -> 6.23 us
    ppermute x3, waiting for transfers between devices: 3.26 us -> 3.04 us  [exchange_chips(): lax.ppermute(block, 'intra', [(i, partner(i, s, intra, pair)) for i in ra...]
  transfers between devices with their start and end apart: 7 -> 7, of which waited for: 7 -> 6; matrix products, arithmetic and copies ran while one was open for 0% -> 0% of each run, Pallas kernels for 9% -> 9%
where the time goes in v4:
time: 20.7 us; the launch traced here: 20.5 us
  starting transfers between devices  9.97 us (48%)
  waiting for transfers between devices  6.23 us (30%)
  Pallas kernels  4.26 us (21%)
    ppermute x3, starting transfers between devices, exchange_chips(): lax.ppermute(block, 'intra', [(i, partner(i, s, intra, pair)) for i in ra...  6.52 us
    ppermute x3, waiting for transfers between devices, exchange_chips(): lax.ppermute(block, 'intra', [(i, partner(i, s, intra, pair)) for i in ra...  3.04 us
    ppermute x3, starting transfers between devices, exchange_groups(): lax.ppermute(block, ('tower', 'intra'), pairs)  2.99 us
    ppermute x3, waiting for transfers between devices, exchange_groups(): lax.ppermute(block, ('tower', 'intra'), pairs)  2.85 us
    pallas_call x1, Pallas kernels, run_towers(): pl.pallas_call(functools.partial(tower_kernel, towers, intra, pair, order...  1.07 us
    pallas_call x1, Pallas kernels, gather_blocks(): pl.pallas_call(functools.partial(load_kernel, len(small)), out_shape=[plt...  1.02 us
    pallas_call x1, Pallas kernels, interact(): pl.pallas_call(functools.partial(interact_kernel, towers), out_shape=jax....  0.94 us
    pallas_call x1, Pallas kernels, run_towers(): pl.pallas_call(functools.partial(early_kernel, intra, pair, (*order[:firs...  0.88 us
  transfers between devices with their start and end apart: 7, of which 6 were waited for; matrix products, arithmetic and copies ran while one was open for 0% of the time, Pallas kernels for 9%

profile of v4, /device:TPU:0, one launch (start us, length us, event | category | flops | bytes accessed | tf_op | source)
XLA Modules:
  0.0 20.5 jit_solution(16229621185328127626)
XLA Ops:
  0.0 0.5 %collective-permute-start = (bf16[256,512]{1,0:T(8,128)(2,1)}, bf16[256,512]{1,0:T(8,128)(2,1)S(1)}, u32[]{:S(2)}, u32[]{:S(2)}) collective-permute-start(bf16[256,512]{1,0:T(8,128)(2,1)} %emb_hbm.1), channel_id=1, source_target_pairs={{0,1},{1,0},{2,3},{3,2},{4,5},{5,4},{6,7},{7,6},{8,9},{9,8},{10,11... | collective-permute-start | bytes 786440 | tf_op jit(solution)/shard_map/ppermute | solution.py:106
  0.5 1.0 %load.1 = (bf16[256,256]{1,0:T(8,128)(2,1)S(1)}, bf16[256,512]{1,0:T(8,128)(2,1)S(1)}, s32[1,32]{1,0:T(1,128)S(4)}, f32[2,1024]{1,0:T(2,128)S(1)}, f32[2,256]{1,0:T(2,128)S(1)}, /*index=5*/bf16[16,128]{1,0:T(8,128)(2,1)S(1)}) custom-call(s32[256]{0:T(256)} %owner_hbm.1, bf16[256,512]{1,0:T(8,128)(2,1)} %emb_hbm.1, s32[1,32]{1,0:T(1,128)} %rest_0_.1, ...), custom_call_target="tpu_custom_call" | custom-call | tf_op jit(solution)/shard_map/load/pallas_call | solution.py:109
  1.5 0.3 %collective-permute-done.rest_1_ = bf16[256,512]{1,0:T(8,128)(2,1)S(1)} collective-permute-done((bf16[256,512]{1,0:T(8,128)(2,1)}, bf16[256,512]{1,0:T(8,128)(2,1)S(1)}, u32[]{:S(2)}, u32[]{:S(2)}) %collective-permute-start) | collective-permute-done | bytes 262176 | tf_op jit(solution)/shard_map/ppermute | solution.py:106
  1.8 0.0 copy-start
  1.8 0.3 %gather_rows.1 = (bf16[8,32,128]{2,1,0:T(8,128)(2,1)S(1)}, bf16[8,32,128]{2,1,0:T(8,128)(2,1)S(1)}, bf16[8,32,128]{2,1,0:T(8,128)(2,1)S(1)}, bf16[8,32,128]{2,1,0:T(8,128)(2,1)S(1)}) custom-call(bf16[256,256]{1,0:T(8,128)(2,1)S(1)} %get-tuple-element.23.picks_ref, bf16[256,512]{1,0:T(8,128)(2,1)S(1)} %get-tuple-element.24.rest_0_, ...), custom_call_target="tpu_custom_call" | custom-call | flops 47185920000 | tf_op jit(solution)/shard_map/gather_rows/pallas_call | solution.py:129
  2.2 0.0 copy-start.1
  2.2 2.7 %collective-permute-start.1 = (bf16[8,32,128]{2,1,0:T(8,128)(2,1)S(1)}, bf16[8,32,128]{2,1,0:T(8,128)(2,1)S(1)}, u32[]{:S(2)}, u32[]{:S(2)}) collective-permute-start(bf16[8,32,128]{2,1,0:T(8,128)(2,1)S(1)} %get-tuple-element.25), channel_id=1, source_target_pairs={{0,3},{1,2},{2,7},{3,6},{4,1},{5,0},{6,5},{7,4},{8,11},{9,10},{10,... | collective-permute-start | bytes 196616 | tf_op jit(solution)/shard_map/ppermute | solution.py:42
  4.9 2.5 %collective-permute-start.2 = (bf16[8,32,128]{2,1,0:T(8,128)(2,1)S(1)}, bf16[8,32,128]{2,1,0:T(8,128)(2,1)S(1)}, u32[]{:S(2)}, u32[]{:S(2)}) collective-permute-start(bf16[8,32,128]{2,1,0:T(8,128)(2,1)S(1)} %get-tuple-element.27), channel_id=1, source_target_pairs={{0,7},{1,6},{2,5},{3,4},{4,3},{5,2},{6,1},{7,0},{8,15},{9,14},{10,... | collective-permute-start | bytes 196616 | tf_op jit(solution)/shard_map/ppermute | solution.py:42
  7.4 1.3 %collective-permute-start.3 = (bf16[8,32,128]{2,1,0:T(8,128)(2,1)S(1)}, bf16[8,32,128]{2,1,0:T(8,128)(2,1)S(1)}, u32[]{:S(2)}, u32[]{:S(2)}) collective-permute-start(bf16[8,32,128]{2,1,0:T(8,128)(2,1)S(1)} %get-tuple-element.28), channel_id=1, source_target_pairs={{0,5},{1,4},{2,1},{3,0},{4,7},{5,6},{6,3},{7,2},{8,13},{9,12},{10,... | collective-permute-start | bytes 196616 | tf_op jit(solution)/shard_map/ppermute | solution.py:42
  8.7 0.0 collective-permute-done.1.rest_0_
  8.7 0.0 copy-done
  8.7 0.9 %towers_early.1.sums_ref = f32[64,1024]{1,0:T(8,128)S(1)} custom-call(s32[1,32]{1,0:T(1,128)S(4)} %get-tuple-element.20.slots_ref, bf16[2,2048,1024]{2,1,0:T(8,128)(2,1)S(1)} %copy-done, bf16[8,32,128]{2,1,0:T(8,128)(2,1)S(1)} %collective-permute-done.1.rest_0_, bf16[8,32,128]{2,1,0:T(8,128)(2,1)S(1)} %get-tuple-element.26.rest_1_), custom_call_target="tpu_custom_call" | custom-call | flops 268435456 | tf_op jit(solution)/shard_map/towers_early/pallas_call | solution.py:229
  9.6 1.7 %collective-permute-done.2.rest_0_ = bf16[8,32,128]{2,1,0:T(8,128)(2,1)S(1)} collective-permute-done((bf16[8,32,128]{2,1,0:T(8,128)(2,1)S(1)}, bf16[8,32,128]{2,1,0:T(8,128)(2,1)S(1)}, u32[]{:S(2)}, u32[]{:S(2)}) %collective-permute-start.2) | collective-permute-done | bytes 65568 | tf_op jit(solution)/shard_map/ppermute | solution.py:42
  11.3 1.3 %collective-permute-done.3.rest_1_ = bf16[8,32,128]{2,1,0:T(8,128)(2,1)S(1)} collective-permute-done((bf16[8,32,128]{2,1,0:T(8,128)(2,1)S(1)}, bf16[8,32,128]{2,1,0:T(8,128)(2,1)S(1)}, u32[]{:S(2)}, u32[]{:S(2)}) %collective-permute-start.3) | collective-permute-done | bytes 65568 | tf_op jit(solution)/shard_map/ppermute | solution.py:42
  12.6 0.0 copy-done.1
  12.7 1.1 %towers.1 = (bf16[32,128]{1,0:T(8,128)(2,1)S(1)}, bf16[32,128]{1,0:T(8,128)(2,1)S(1)}, bf16[32,128]{1,0:T(8,128)(2,1)S(1)}, bf16[32,128]{1,0:T(8,128)(2,1)S(1)}) custom-call(s32[1,32]{1,0:T(1,128)S(4)} %get-tuple-element.20.slots_ref, bf16[2,2048,1024]{2,1,0:T(8,128)(2,1)S(1)} %copy-done, f32[2,1024]{1,0:T(2,128)S(1)} %get-tuple-element.21.b1_ref, ...), custom_call_target="tpu_custom_call" | custom-call | tf_op jit(solution)/shard_map/towers/pallas_call | solution.py:242
  13.7 2.2 %collective-permute-start.4 = (bf16[32,128]{1,0:T(8,128)(2,1)S(1)}, bf16[32,128]{1,0:T(8,128)(2,1)S(1)}, u32[]{:S(2)}, u32[]{:S(2)}) collective-permute-start(bf16[32,128]{1,0:T(8,128)(2,1)S(1)} %get-tuple-element.29), channel_id=1, source_target_pairs={{0,25},{1,24},{2,27},{3,26},{4,29},{5,28},{6,31},{7,30},{8,17},{9,... | collective-permute-start | bytes 24584 | tf_op jit(solution)/shard_map/ppermute | solution.py:59
  16.0 0.5 %collective-permute-start.5 = (bf16[32,128]{1,0:T(8,128)(2,1)S(1)}, bf16[32,128]{1,0:T(8,128)(2,1)S(1)}, u32[]{:S(2)}, u32[]{:S(2)}) collective-permute-start(bf16[32,128]{1,0:T(8,128)(2,1)S(1)} %get-tuple-element.30), channel_id=1, source_target_pairs={{0,17},{1,16},{2,19},{3,18},{4,21},{5,20},{6,23},{7,22},{8,25},{9,... | collective-permute-start | bytes 24584 | tf_op jit(solution)/shard_map/ppermute | solution.py:59
  16.5 0.2 %collective-permute-start.6 = (bf16[32,128]{1,0:T(8,128)(2,1)S(1)}, bf16[32,128]{1,0:T(8,128)(2,1)S(1)}, u32[]{:S(2)}, u32[]{:S(2)}) collective-permute-start(bf16[32,128]{1,0:T(8,128)(2,1)S(1)} %get-tuple-element.31), channel_id=1, source_target_pairs={{0,9},{1,8},{2,11},{3,10},{4,13},{5,12},{6,15},{7,14},{8,1},{9,0},... | collective-permute-start | bytes 24584 | tf_op jit(solution)/shard_map/ppermute | solution.py:59
  16.7 1.0 %collective-permute-done.4.rest_0_ = bf16[32,128]{1,0:T(8,128)(2,1)S(1)} collective-permute-done((bf16[32,128]{1,0:T(8,128)(2,1)S(1)}, bf16[32,128]{1,0:T(8,128)(2,1)S(1)}, u32[]{:S(2)}, u32[]{:S(2)}) %collective-permute-start.4) | collective-permute-done | bytes 8224 | tf_op jit(solution)/shard_map/ppermute | solution.py:59
  17.8 1.3 %collective-permute-done.5.rest_1_ = bf16[32,128]{1,0:T(8,128)(2,1)S(1)} collective-permute-done((bf16[32,128]{1,0:T(8,128)(2,1)S(1)}, bf16[32,128]{1,0:T(8,128)(2,1)S(1)}, u32[]{:S(2)}, u32[]{:S(2)}) %collective-permute-start.5) | collective-permute-done | bytes 8224 | tf_op jit(solution)/shard_map/ppermute | solution.py:59
  19.0 0.5 %collective-permute-done.6.rest_2_ = bf16[32,128]{1,0:T(8,128)(2,1)S(1)} collective-permute-done((bf16[32,128]{1,0:T(8,128)(2,1)S(1)}, bf16[32,128]{1,0:T(8,128)(2,1)S(1)}, u32[]{:S(2)}, u32[]{:S(2)}) %collective-permute-start.6) | collective-permute-done | bytes 8224 | tf_op jit(solution)/shard_map/ppermute | solution.py:59
  19.6 0.9 %interact.1 = bf16[8,16,128]{2,1,0:T(8,128)(2,1)} custom-call(bf16[16,128]{1,0:T(8,128)(2,1)S(1)} %get-tuple-element.19.proj_ref, bf16[32,128]{1,0:T(8,128)(2,1)S(1)} %collective-permute-done.4.rest_0_, bf16[32,128]{1,0:T(8,128)(2,1)S(1)} %collective-permute-done.5.rest_1_, bf16[32,128]{1,0:T(8,128)(2,1)S(1)} %collective-permute-done.6.rest_2_, ...), custom_call_target="tpu_custom_call" | custom-call | tf_op jit(solution)/shard_map/interact/pallas_call | solution.py:300
Async XLA Ops:
  0.0 1.8 %collective-permute-start = (bf16[256,512]{1,0:T(8,128)(2,1)}, bf16[256,512]{1,0:T(8,128)(2,1)S(1)}, u32[]{:S(2)}, u32[]{:S(2)}) collective-permute-start(bf16[256,512]{1,0:T(8,128)(2,1)} %emb_hbm.1), channel_id=1, source_target_pairs={{0,1},{1,0},{2,3},{3,2},{4,5},{5,4},{6,7},{7,6},{8,9},{9,8},{10,11... | collective-permute-start | bytes 786440 | tf_op jit(solution)/shard_map/ppermute | solution.py:106
  1.8 6.9 %copy-start = (bf16[2,2048,1024]{2,1,0:T(8,128)(2,1)S(1)}, bf16[2,2048,1024]{2,1,0:T(8,128)(2,1)}, u32[]{:S(2)}) copy-start(bf16[2,2048,1024]{2,1,0:T(8,128)(2,1)} %w1_ref.3) | copy-start | bytes 25165828
  2.2 10.5 %copy-start.1 = (bf16[2,1024,256]{2,1,0:T(8,128)(2,1)S(1)}, bf16[2,1024,256]{2,1,0:T(8,128)(2,1)}, u32[]{:S(2)}) copy-start(bf16[2,1024,256]{2,1,0:T(8,128)(2,1)} %w2_ref.1) | copy-start | bytes 3145732
  2.2 6.5 %collective-permute-start.1 = (bf16[8,32,128]{2,1,0:T(8,128)(2,1)S(1)}, bf16[8,32,128]{2,1,0:T(8,128)(2,1)S(1)}, u32[]{:S(2)}, u32[]{:S(2)}) collective-permute-start(bf16[8,32,128]{2,1,0:T(8,128)(2,1)S(1)} %get-tuple-element.25), channel_id=1, source_target_pairs={{0,3},{1,2},{2,7},{3,6},{4,1},{5,0},{6,5},{7,4},{8,11},{9,10},{10,... | collective-permute-start | bytes 196616 | tf_op jit(solution)/shard_map/ppermute | solution.py:42
  4.9 6.4 %collective-permute-start.2 = (bf16[8,32,128]{2,1,0:T(8,128)(2,1)S(1)}, bf16[8,32,128]{2,1,0:T(8,128)(2,1)S(1)}, u32[]{:S(2)}, u32[]{:S(2)}) collective-permute-start(bf16[8,32,128]{2,1,0:T(8,128)(2,1)S(1)} %get-tuple-element.27), channel_id=1, source_target_pairs={{0,7},{1,6},{2,5},{3,4},{4,3},{5,2},{6,1},{7,0},{8,15},{9,14},{10,... | collective-permute-start | bytes 196616 | tf_op jit(solution)/shard_map/ppermute | solution.py:42
  7.4 5.3 %collective-permute-start.3 = (bf16[8,32,128]{2,1,0:T(8,128)(2,1)S(1)}, bf16[8,32,128]{2,1,0:T(8,128)(2,1)S(1)}, u32[]{:S(2)}, u32[]{:S(2)}) collective-permute-start(bf16[8,32,128]{2,1,0:T(8,128)(2,1)S(1)} %get-tuple-element.28), channel_id=1, source_target_pairs={{0,5},{1,4},{2,1},{3,0},{4,7},{5,6},{6,3},{7,2},{8,13},{9,12},{10,... | collective-permute-start | bytes 196616 | tf_op jit(solution)/shard_map/ppermute | solution.py:42
  13.7 4.0 %collective-permute-start.4 = (bf16[32,128]{1,0:T(8,128)(2,1)S(1)}, bf16[32,128]{1,0:T(8,128)(2,1)S(1)}, u32[]{:S(2)}, u32[]{:S(2)}) collective-permute-start(bf16[32,128]{1,0:T(8,128)(2,1)S(1)} %get-tuple-element.29), channel_id=1, source_target_pairs={{0,25},{1,24},{2,27},{3,26},{4,29},{5,28},{6,31},{7,30},{8,17},{9,... | collective-permute-start | bytes 24584 | tf_op jit(solution)/shard_map/ppermute | solution.py:59
  16.0 3.1 %collective-permute-start.5 = (bf16[32,128]{1,0:T(8,128)(2,1)S(1)}, bf16[32,128]{1,0:T(8,128)(2,1)S(1)}, u32[]{:S(2)}, u32[]{:S(2)}) collective-permute-start(bf16[32,128]{1,0:T(8,128)(2,1)S(1)} %get-tuple-element.30), channel_id=1, source_target_pairs={{0,17},{1,16},{2,19},{3,18},{4,21},{5,20},{6,23},{7,22},{8,25},{9,... | collective-permute-start | bytes 24584 | tf_op jit(solution)/shard_map/ppermute | solution.py:59
  16.5 3.1 %collective-permute-start.6 = (bf16[32,128]{1,0:T(8,128)(2,1)S(1)}, bf16[32,128]{1,0:T(8,128)(2,1)S(1)}, u32[]{:S(2)}, u32[]{:S(2)}) collective-permute-start(bf16[32,128]{1,0:T(8,128)(2,1)S(1)} %get-tuple-element.31), channel_id=1, source_target_pairs={{0,9},{1,8},{2,11},{3,10},{4,13},{5,12},{6,15},{7,14},{8,1},{9,0},... | collective-permute-start | bytes 24584 | tf_op jit(solution)/shard_map/ppermute | solution.py:59

commit v5 on v4

--- a/solution.py
+++ b/solution.py
@@ -187,8 +187,8 @@
 
 
 def early_kernel(intra, pair, order, slots_ref, w1_ref, *rest):
-    blocks, out_ref, x_ref = rest[:-2], rest[-2], rest[-1]
-    for columns, total in first_layer(intra, pair, order, slots_ref, w1_ref, x_ref, blocks):
+    blocks, before, (out_ref, x_ref) = rest[: len(order)], rest[len(order) : -2], rest[-2:]
+    for columns, total in first_layer(intra, pair, order, slots_ref, w1_ref, x_ref, blocks, *before):
         out_ref[:, columns] = total
 
 
@@ -217,8 +217,10 @@
 
 def run_towers(slots, w1, b1, w2, b2, blocks, towers, intra, pair):
     order = steps(intra, pair)
-    first = max(len(blocks) // 2 - 1, 0)
-    early, late = (*blocks[:first], blocks[-1]), tuple(blocks[first:-1])
+    remote = len(blocks) - 1
+    cuts = (0, max(remote // 2, min(remote - 1, 1)), remote - 1)
+    stages = [[-1, *range(*cuts[:2])], [*range(*cuts[1:])]]
+    late = [remote - 1] if remote else []
     held, rows, _ = blocks[0].shape
     count, depth, hid = w1.shape
     width = w2.shape[2]
@@ -226,21 +228,25 @@
     w1 = pltpu.with_memory_space_constraint(w1, pltpu.VMEM)
     w2 = pltpu.with_memory_space_constraint(w2, pltpu.VMEM)
     params = pltpu.CompilerParams(vmem_limit_bytes=16 << 20)
-    sums = pl.pallas_call(
-        functools.partial(early_kernel, intra, pair, (*order[:first], order[-1])),
-        out_shape=pltpu.VMEM((count * rows, hid), jnp.float32),
-        in_specs=[pl.BlockSpec(memory_space=pltpu.SMEM)]
-        + [pl.BlockSpec(memory_space=pltpu.VMEM)] * (1 + len(early)),
-        out_specs=pl.BlockSpec(memory_space=pltpu.VMEM),
-        scratch_shapes=[pltpu.VMEM((count * rows, len(early) * held * EDIM), jnp.bfloat16)],
-        compiler_params=params,
-        cost_estimate=pl.CostEstimate(
-            flops=2 * count * rows * depth * hid, bytes_accessed=0, transcendentals=0
-        ),
-        name="towers_early",
-    )(slots, w1, *early)
+    sums = ()
+    for stage in stages:
+        if not stage:
+            continue
+        sums = pl.pallas_call(
+            functools.partial(early_kernel, intra, pair, [order[n] for n in stage]),
+            out_shape=[pltpu.VMEM((count * rows, hid), jnp.float32)],
+            in_specs=[pl.BlockSpec(memory_space=pltpu.SMEM)]
+            + [pl.BlockSpec(memory_space=pltpu.VMEM)] * (1 + len(stage) + len(sums)),
+            out_specs=[pl.BlockSpec(memory_space=pltpu.VMEM)],
+            scratch_shapes=[pltpu.VMEM((count * rows, len(stage) * held * EDIM), jnp.bfloat16)],
+            compiler_params=params,
+            cost_estimate=pl.CostEstimate(
+                flops=2 * count * rows * depth * hid, bytes_accessed=0, transcendentals=0
+            ),
+            name="towers_early",
+        )(slots, w1, *(blocks[n] for n in stage), *sums)
     return pl.pallas_call(
-        functools.partial(tower_kernel, towers, intra, pair, order[first:-1]),
+        functools.partial(tower_kernel, towers, intra, pair, [order[n] for n in late]),
         out_shape=[pltpu.VMEM((local, EDIM), jnp.bfloat16)] * towers,
         in_specs=[pl.BlockSpec(memory_space=pltpu.SMEM)]
         + [pl.BlockSpec(memory_space=pltpu.VMEM)] * (5 + len(late)),
@@ -252,7 +258,7 @@
         ],
         compiler_params=params,
         name="towers",
-    )(slots, w1, b1, w2, b2, sums, *late)
+    )(slots, w1, b1, w2, b2, *sums, *(blocks[n] for n in late))
 
 
 def interact_kernel(towers, proj_ref, *rest):

time: 20.7 us -> 20.2 us (0.976)
  waiting for transfers between devices: 6.23 us -> 5.67 us
    ppermute x3, waiting for transfers between devices: 3.04 us -> 2.5 us  [exchange_chips(): lax.ppermute(block, 'intra', [(i, partner(i, s, intra, pair)) for i in ra...]
    pallas_call x2 -> x3, Pallas kernels: 1.95 us -> 2.09 us  [the longest x2 1.4 us: run_towers(): pl.pallas_call(functools.partial(early_kernel, intra, pair, [order[n] for...]
  transfers between devices with their start and end apart: 7 -> 7, of which waited for: 6 -> 6; matrix products, arithmetic and copies ran while one was open for 0% -> 0% of each run, Pallas kernels for 9% -> 12%
where the time goes in v5:
time: 20.2 us; the launch traced here: 20.1 us
  starting transfers between devices  9.97 us (49%)
  waiting for transfers between devices  5.67 us (28%)
  Pallas kernels  4.4 us (22%)
    ppermute x3, starting transfers between devices, exchange_chips(): lax.ppermute(block, 'intra', [(i, partner(i, s, intra, pair)) for i in ra...  6.52 us
    ppermute x3, starting transfers between devices, exchange_groups(): lax.ppermute(block, ('tower', 'intra'), pairs)  2.99 us
    ppermute x3, waiting for transfers between devices, exchange_groups(): lax.ppermute(block, ('tower', 'intra'), pairs)  2.82 us
    ppermute x3, waiting for transfers between devices, exchange_chips(): lax.ppermute(block, 'intra', [(i, partner(i, s, intra, pair)) for i in ra...  2.5 us
    pallas_call x2, Pallas kernels, run_towers(): pl.pallas_call(functools.partial(early_kernel, intra, pair, [order[n] for...  1.4 us
    pallas_call x1, Pallas kernels, gather_blocks(): pl.pallas_call(functools.partial(load_kernel, len(small)), out_shape=[plt...  1.02 us
    pallas_call x1, Pallas kernels, interact(): pl.pallas_call(functools.partial(interact_kernel, towers), out_shape=jax....  0.94 us
    pallas_call x1, Pallas kernels, run_towers(): pl.pallas_call(functools.partial(tower_kernel, towers, intra, pair, [orde...  0.69 us
  transfers between devices with their start and end apart: 7, of which 6 were waited for; matrix products, arithmetic and copies ran while one was open for 0% of the time, Pallas kernels for 12%

profile of v5, /device:TPU:0, one launch (start us, length us, event | category | flops | bytes accessed | tf_op | source)
XLA Modules:
  0.0 20.1 jit_solution(158116536945150034)
XLA Ops:
  0.0 0.5 %collective-permute-start = (bf16[256,512]{1,0:T(8,128)(2,1)}, bf16[256,512]{1,0:T(8,128)(2,1)S(1)}, u32[]{:S(2)}, u32[]{:S(2)}) collective-permute-start(bf16[256,512]{1,0:T(8,128)(2,1)} %emb_hbm.1), channel_id=1, source_target_pairs={{0,1},{1,0},{2,3},{3,2},{4,5},{5,4},{6,7},{7,6},{8,9},{9,8},{10,11... | collective-permute-start | bytes 786440 | tf_op jit(solution)/shard_map/ppermute | solution.py:106
  0.5 1.0 %load.1 = (bf16[256,256]{1,0:T(8,128)(2,1)S(1)}, bf16[256,512]{1,0:T(8,128)(2,1)S(1)}, s32[1,32]{1,0:T(1,128)S(4)}, f32[2,1024]{1,0:T(2,128)S(1)}, f32[2,256]{1,0:T(2,128)S(1)}, /*index=5*/bf16[16,128]{1,0:T(8,128)(2,1)S(1)}) custom-call(s32[256]{0:T(256)} %owner_hbm.1, bf16[256,512]{1,0:T(8,128)(2,1)} %emb_hbm.1, s32[1,32]{1,0:T(1,128)} %rest_0_.1, ...), custom_call_target="tpu_custom_call" | custom-call | tf_op jit(solution)/shard_map/load/pallas_call | solution.py:109
  1.5 0.3 %collective-permute-done.rest_1_ = bf16[256,512]{1,0:T(8,128)(2,1)S(1)} collective-permute-done((bf16[256,512]{1,0:T(8,128)(2,1)}, bf16[256,512]{1,0:T(8,128)(2,1)S(1)}, u32[]{:S(2)}, u32[]{:S(2)}) %collective-permute-start) | collective-permute-done | bytes 262176 | tf_op jit(solution)/shard_map/ppermute | solution.py:106
  1.8 0.0 copy-start
  1.8 0.3 %gather_rows.1 = (bf16[8,32,128]{2,1,0:T(8,128)(2,1)S(1)}, bf16[8,32,128]{2,1,0:T(8,128)(2,1)S(1)}, bf16[8,32,128]{2,1,0:T(8,128)(2,1)S(1)}, bf16[8,32,128]{2,1,0:T(8,128)(2,1)S(1)}) custom-call(bf16[256,256]{1,0:T(8,128)(2,1)S(1)} %get-tuple-element.23.picks_ref, bf16[256,512]{1,0:T(8,128)(2,1)S(1)} %get-tuple-element.24.rest_0_, ...), custom_call_target="tpu_custom_call" | custom-call | flops 47185920000 | tf_op jit(solution)/shard_map/gather_rows/pallas_call | solution.py:129
  2.2 2.7 %collective-permute-start.2 = (bf16[8,32,128]{2,1,0:T(8,128)(2,1)S(1)}, bf16[8,32,128]{2,1,0:T(8,128)(2,1)S(1)}, u32[]{:S(2)}, u32[]{:S(2)}) collective-permute-start(bf16[8,32,128]{2,1,0:T(8,128)(2,1)S(1)} %get-tuple-element.27), channel_id=1, source_target_pairs={{0,3},{1,2},{2,7},{3,6},{4,1},{5,0},{6,5},{7,4},{8,11},{9,10},{10,... | collective-permute-start | bytes 196616 | tf_op jit(solution)/shard_map/ppermute | solution.py:42
  4.9 2.5 %collective-permute-start.1 = (bf16[8,32,128]{2,1,0:T(8,128)(2,1)S(1)}, bf16[8,32,128]{2,1,0:T(8,128)(2,1)S(1)}, u32[]{:S(2)}, u32[]{:S(2)}) collective-permute-start(bf16[8,32,128]{2,1,0:T(8,128)(2,1)S(1)} %get-tuple-element.25), channel_id=1, source_target_pairs={{0,7},{1,6},{2,5},{3,4},{4,3},{5,2},{6,1},{7,0},{8,15},{9,14},{10,... | collective-permute-start | bytes 196616 | tf_op jit(solution)/shard_map/ppermute | solution.py:42
  7.4 1.3 %collective-permute-start.3 = (bf16[8,32,128]{2,1,0:T(8,128)(2,1)S(1)}, bf16[8,32,128]{2,1,0:T(8,128)(2,1)S(1)}, u32[]{:S(2)}, u32[]{:S(2)}) collective-permute-start(bf16[8,32,128]{2,1,0:T(8,128)(2,1)S(1)} %get-tuple-element.28), channel_id=1, source_target_pairs={{0,5},{1,4},{2,1},{3,0},{4,7},{5,6},{6,3},{7,2},{8,13},{9,12},{10,... | collective-permute-start | bytes 196616 | tf_op jit(solution)/shard_map/ppermute | solution.py:42
  8.7 0.0 collective-permute-done.2.rest_1_
  8.7 0.0 copy-done
  8.7 0.0 copy-start.1
  8.7 0.9 %towers_early.2.rest_1_ = f32[64,1024]{1,0:T(8,128)S(1)} custom-call(s32[1,32]{1,0:T(1,128)S(4)} %get-tuple-element.20.slots_ref, bf16[2,2048,1024]{2,1,0:T(8,128)(2,1)S(1)} %copy-done, bf16[8,32,128]{2,1,0:T(8,128)(2,1)S(1)} %get-tuple-element.26.rest_0_, bf16[8,32,128]{2,1,0:T(8,128)(2,1)S(1)} %collective-permute-done.2.rest_1_), custom_call_target="tpu_custom_call" | custom-call | flops 268435456 | tf_op jit(solution)/shard_map/towers_early/pallas_call | solution.py:235
  9.6 1.7 %collective-permute-done.1.rest_0_ = bf16[8,32,128]{2,1,0:T(8,128)(2,1)S(1)} collective-permute-done((bf16[8,32,128]{2,1,0:T(8,128)(2,1)S(1)}, bf16[8,32,128]{2,1,0:T(8,128)(2,1)S(1)}, u32[]{:S(2)}, u32[]{:S(2)}) %collective-permute-start.1) | collective-permute-done | bytes 65568 | tf_op jit(solution)/shard_map/ppermute | solution.py:42
  11.3 0.5 %towers_early.3.sums_ref = f32[64,1024]{1,0:T(8,128)S(1)} custom-call(s32[1,32]{1,0:T(1,128)S(4)} %get-tuple-element.20.slots_ref, bf16[2,2048,1024]{2,1,0:T(8,128)(2,1)S(1)} %copy-done, bf16[8,32,128]{2,1,0:T(8,128)(2,1)S(1)} %collective-permute-done.1.rest_0_, f32[64,1024]{1,0:T(8,128)S(1)} %towers_early.2.rest_1_), custom_call_target="tpu_custom_call" | custom-call | flops 268435456 | tf_op jit(solution)/shard_map/towers_early/pallas_call | solution.py:235
  11.8 0.8 %collective-permute-done.3.rest_0_ = bf16[8,32,128]{2,1,0:T(8,128)(2,1)S(1)} collective-permute-done((bf16[8,32,128]{2,1,0:T(8,128)(2,1)S(1)}, bf16[8,32,128]{2,1,0:T(8,128)(2,1)S(1)}, u32[]{:S(2)}, u32[]{:S(2)}) %collective-permute-start.3) | collective-permute-done | bytes 65568 | tf_op jit(solution)/shard_map/ppermute | solution.py:42
  12.6 0.0 copy-done.1
  12.6 0.7 %towers.1 = (bf16[32,128]{1,0:T(8,128)(2,1)S(1)}, bf16[32,128]{1,0:T(8,128)(2,1)S(1)}, bf16[32,128]{1,0:T(8,128)(2,1)S(1)}, bf16[32,128]{1,0:T(8,128)(2,1)S(1)}) custom-call(s32[1,32]{1,0:T(1,128)S(4)} %get-tuple-element.20.slots_ref, bf16[2,2048,1024]{2,1,0:T(8,128)(2,1)S(1)} %copy-done, f32[2,1024]{1,0:T(2,128)S(1)} %get-tuple-element.21.b1_ref, ...), custom_call_target="tpu_custom_call" | custom-call | tf_op jit(solution)/shard_map/towers/pallas_call | solution.py:248
  13.3 2.2 %collective-permute-start.4 = (bf16[32,128]{1,0:T(8,128)(2,1)S(1)}, bf16[32,128]{1,0:T(8,128)(2,1)S(1)}, u32[]{:S(2)}, u32[]{:S(2)}) collective-permute-start(bf16[32,128]{1,0:T(8,128)(2,1)S(1)} %get-tuple-element.29), channel_id=1, source_target_pairs={{0,25},{1,24},{2,27},{3,26},{4,29},{5,28},{6,31},{7,30},{8,17},{9,... | collective-permute-start | bytes 24584 | tf_op jit(solution)/shard_map/ppermute | solution.py:59
  15.6 0.5 %collective-permute-start.5 = (bf16[32,128]{1,0:T(8,128)(2,1)S(1)}, bf16[32,128]{1,0:T(8,128)(2,1)S(1)}, u32[]{:S(2)}, u32[]{:S(2)}) collective-permute-start(bf16[32,128]{1,0:T(8,128)(2,1)S(1)} %get-tuple-element.30), channel_id=1, source_target_pairs={{0,17},{1,16},{2,19},{3,18},{4,21},{5,20},{6,23},{7,22},{8,25},{9,... | collective-permute-start | bytes 24584 | tf_op jit(solution)/shard_map/ppermute | solution.py:59
  16.1 0.3 %collective-permute-start.6 = (bf16[32,128]{1,0:T(8,128)(2,1)S(1)}, bf16[32,128]{1,0:T(8,128)(2,1)S(1)}, u32[]{:S(2)}, u32[]{:S(2)}) collective-permute-start(bf16[32,128]{1,0:T(8,128)(2,1)S(1)} %get-tuple-element.31), channel_id=1, source_target_pairs={{0,9},{1,8},{2,11},{3,10},{4,13},{5,12},{6,15},{7,14},{8,1},{9,0},... | collective-permute-start | bytes 24584 | tf_op jit(solution)/shard_map/ppermute | solution.py:59
  16.3 1.0 %collective-permute-done.4.rest_0_ = bf16[32,128]{1,0:T(8,128)(2,1)S(1)} collective-permute-done((bf16[32,128]{1,0:T(8,128)(2,1)S(1)}, bf16[32,128]{1,0:T(8,128)(2,1)S(1)}, u32[]{:S(2)}, u32[]{:S(2)}) %collective-permute-start.4) | collective-permute-done | bytes 8224 | tf_op jit(solution)/shard_map/ppermute | solution.py:59
  17.4 1.3 %collective-permute-done.5.rest_1_ = bf16[32,128]{1,0:T(8,128)(2,1)S(1)} collective-permute-done((bf16[32,128]{1,0:T(8,128)(2,1)S(1)}, bf16[32,128]{1,0:T(8,128)(2,1)S(1)}, u32[]{:S(2)}, u32[]{:S(2)}) %collective-permute-start.5) | collective-permute-done | bytes 8224 | tf_op jit(solution)/shard_map/ppermute | solution.py:59
  18.6 0.5 %collective-permute-done.6.rest_2_ = bf16[32,128]{1,0:T(8,128)(2,1)S(1)} collective-permute-done((bf16[32,128]{1,0:T(8,128)(2,1)S(1)}, bf16[32,128]{1,0:T(8,128)(2,1)S(1)}, u32[]{:S(2)}, u32[]{:S(2)}) %collective-permute-start.6) | collective-permute-done | bytes 8224 | tf_op jit(solution)/shard_map/ppermute | solution.py:59
  19.1 0.9 %interact.1 = bf16[8,16,128]{2,1,0:T(8,128)(2,1)} custom-call(bf16[16,128]{1,0:T(8,128)(2,1)S(1)} %get-tuple-element.19.proj_ref, bf16[32,128]{1,0:T(8,128)(2,1)S(1)} %collective-permute-done.4.rest_0_, bf16[32,128]{1,0:T(8,128)(2,1)S(1)} %collective-permute-done.5.rest_1_, bf16[32,128]{1,0:T(8,128)(2,1)S(1)} %collective-permute-done.6.rest_2_, ...), custom_call_target="tpu_custom_call" | custom-call | tf_op jit(solution)/shard_map/interact/pallas_call | solution.py:306
Async XLA Ops:
  0.0 1.8 %collective-permute-start = (bf16[256,512]{1,0:T(8,128)(2,1)}, bf16[256,512]{1,0:T(8,128)(2,1)S(1)}, u32[]{:S(2)}, u32[]{:S(2)}) collective-permute-start(bf16[256,512]{1,0:T(8,128)(2,1)} %emb_hbm.1), channel_id=1, source_target_pairs={{0,1},{1,0},{2,3},{3,2},{4,5},{5,4},{6,7},{7,6},{8,9},{9,8},{10,11... | collective-permute-start | bytes 786440 | tf_op jit(solution)/shard_map/ppermute | solution.py:106
  1.8 6.9 %copy-start = (bf16[2,2048,1024]{2,1,0:T(8,128)(2,1)S(1)}, bf16[2,2048,1024]{2,1,0:T(8,128)(2,1)}, u32[]{:S(2)}) copy-start(bf16[2,2048,1024]{2,1,0:T(8,128)(2,1)} %w1_ref.5) | copy-start | bytes 25165828
  2.2 6.5 %collective-permute-start.2 = (bf16[8,32,128]{2,1,0:T(8,128)(2,1)S(1)}, bf16[8,32,128]{2,1,0:T(8,128)(2,1)S(1)}, u32[]{:S(2)}, u32[]{:S(2)}) collective-permute-start(bf16[8,32,128]{2,1,0:T(8,128)(2,1)S(1)} %get-tuple-element.27), channel_id=1, source_target_pairs={{0,3},{1,2},{2,7},{3,6},{4,1},{5,0},{6,5},{7,4},{8,11},{9,10},{10,... | collective-permute-start | bytes 196616 | tf_op jit(solution)/shard_map/ppermute | solution.py:42
  4.9 6.4 %collective-permute-start.1 = (bf16[8,32,128]{2,1,0:T(8,128)(2,1)S(1)}, bf16[8,32,128]{2,1,0:T(8,128)(2,1)S(1)}, u32[]{:S(2)}, u32[]{:S(2)}) collective-permute-start(bf16[8,32,128]{2,1,0:T(8,128)(2,1)S(1)} %get-tuple-element.25), channel_id=1, source_target_pairs={{0,7},{1,6},{2,5},{3,4},{4,3},{5,2},{6,1},{7,0},{8,15},{9,14},{10,... | collective-permute-start | bytes 196616 | tf_op jit(solution)/shard_map/ppermute | solution.py:42
  7.4 5.3 %collective-permute-start.3 = (bf16[8,32,128]{2,1,0:T(8,128)(2,1)S(1)}, bf16[8,32,128]{2,1,0:T(8,128)(2,1)S(1)}, u32[]{:S(2)}, u32[]{:S(2)}) collective-permute-start(bf16[8,32,128]{2,1,0:T(8,128)(2,1)S(1)} %get-tuple-element.28), channel_id=1, source_target_pairs={{0,5},{1,4},{2,1},{3,0},{4,7},{5,6},{6,3},{7,2},{8,13},{9,12},{10,... | collective-permute-start | bytes 196616 | tf_op jit(solution)/shard_map/ppermute | solution.py:42
  8.7 3.9 %copy-start.1 = (bf16[2,1024,256]{2,1,0:T(8,128)(2,1)S(1)}, bf16[2,1024,256]{2,1,0:T(8,128)(2,1)}, u32[]{:S(2)}) copy-start(bf16[2,1024,256]{2,1,0:T(8,128)(2,1)} %w2_ref.1) | copy-start | bytes 3145732
  13.3 4.0 %collective-permute-start.4 = (bf16[32,128]{1,0:T(8,128)(2,1)S(1)}, bf16[32,128]{1,0:T(8,128)(2,1)S(1)}, u32[]{:S(2)}, u32[]{:S(2)}) collective-permute-start(bf16[32,128]{1,0:T(8,128)(2,1)S(1)} %get-tuple-element.29), channel_id=1, source_target_pairs={{0,25},{1,24},{2,27},{3,26},{4,29},{5,28},{6,31},{7,30},{8,17},{9,... | collective-permute-start | bytes 24584 | tf_op jit(solution)/shard_map/ppermute | solution.py:59
  15.6 3.1 %collective-permute-start.5 = (bf16[32,128]{1,0:T(8,128)(2,1)S(1)}, bf16[32,128]{1,0:T(8,128)(2,1)S(1)}, u32[]{:S(2)}, u32[]{:S(2)}) collective-permute-start(bf16[32,128]{1,0:T(8,128)(2,1)S(1)} %get-tuple-element.30), channel_id=1, source_target_pairs={{0,17},{1,16},{2,19},{3,18},{4,21},{5,20},{6,23},{7,22},{8,25},{9,... | collective-permute-start | bytes 24584 | tf_op jit(solution)/shard_map/ppermute | solution.py:59
  16.1 3.1 %collective-permute-start.6 = (bf16[32,128]{1,0:T(8,128)(2,1)S(1)}, bf16[32,128]{1,0:T(8,128)(2,1)S(1)}, u32[]{:S(2)}, u32[]{:S(2)}) collective-permute-start(bf16[32,128]{1,0:T(8,128)(2,1)S(1)} %get-tuple-element.31), channel_id=1, source_target_pairs={{0,9},{1,8},{2,11},{3,10},{4,13},{5,12},{6,15},{7,14},{8,1},{9,0},... | collective-permute-start | bytes 24584 | tf_op jit(solution)/shard_map/ppermute | solution.py:59

commit v6 on v5

--- a/solution.py
+++ b/solution.py
@@ -11,8 +11,8 @@
 FEW_SAMPLES = 1024
 
 
-def offsets(size):
-    return range(size - 1, -1, -1)
+def rounds(towers, pair):
+    return range(towers // pair - 1, -1, -1)
 
 
 def steps(intra, pair):
@@ -44,20 +44,18 @@
     ]
 
 
-def other_core(intra):
-    return 1 if intra > 1 else 0
-
-
-def exchange_groups(blocks, towers, intra):
+def exchange_groups(blocks, towers, intra, pair):
+    half = towers // pair
     received = []
-    for block, o in zip(blocks, offsets(towers)):
+    for block, j in zip(blocks, rounds(towers, pair)):
         pairs = [
-            (t * intra + i, (t ^ o) * intra + (i ^ other_core(intra)))
+            (t * intra + i, (t ^ (j + i % pair * half)) * intra + i)
             for t in range(towers)
             for i in range(intra)
         ]
-        received.append(lax.ppermute(block, ("tower", "intra"), pairs) if o else block)
-    return received
+        received.append(lax.ppermute(block, ("tower", "intra"), pairs))
+    swaps = [(i, i ^ q) for q in range(1, pair) for i in range(intra)]
+    return [*received, *(lax.ppermute(block, "intra", swaps) for block in received if swaps)]
 
 
 def load_kernel(count, owner_hbm, emb_hbm, *rest):
@@ -84,7 +82,7 @@
     parts, outs, acc_ref = rest[:pair], rest[pair:-1], rest[-1]
     samples, width = parts[0].shape
     per = samples // (towers * intra)
-    held = width // EDIM
+    held, half = width // EDIM, towers // pair
     me, place = lax.axis_index("intra"), lax.axis_index("tower")
     for q, part in enumerate(parts):
         acc_ref[:, q * width : (q + 1) * width] = lax.dot_general(
@@ -92,8 +90,13 @@
         )
     for s, out in zip(steps(intra, pair), outs):
         block = partner(me, s, intra, pair)
-        owners = [jnp.where(place == t, block, block ^ other_core(intra)) for t in range(towers)]
-        starts = [pl.multiple_of((t * intra + owners[t]) * per, per) for t in range(towers)]
+        starts = [
+            pl.multiple_of(
+                ((place ^ (j + block % pair * half)) * intra + block // pair * pair + e) * per, per
+            )
+            for j in range(half)
+            for e in range(pair)
+        ]
         for f in range(pair * held):
             columns = slice(f * EDIM, (f + 1) * EDIM)
             rows = [acc_ref[pl.ds(start, per), columns] for start in starts]
@@ -138,14 +141,14 @@
         )(picks, embeddings, *parts)
         return blocks, small
     order = owner.reshape(towers, intra, -1)
-    crossed = order[:, jnp.arange(intra) ^ other_core(intra)]
-    own = jnp.arange(towers)[:, None, None] == lax.axis_index("tower")
-    order = jnp.where(own, order, crossed).transpose(1, 0, 2)
+    place, half = lax.axis_index("tower"), towers // pair
     me = lax.axis_index("intra")
     table = jnp.concatenate([embeddings, *parts], axis=1)
     blocks = []
     for s in steps(intra, pair):
-        mine = lax.dynamic_index_in_dim(order, partner(me, s, intra, pair), keepdims=False).reshape(-1)
+        block = partner(me, s, intra, pair)
+        groups = place ^ (jnp.arange(half) + block % pair * half)
+        mine = order[groups[:, None], block // pair * pair + jnp.arange(pair)[None, :]].reshape(-1)
         blocks.append(jnp.take(table, mine, axis=0).reshape(rows, held, EDIM).transpose(1, 0, 2))
     assign = small[0][0]
     same = assign[None, :] == jnp.arange(assign.size)[:, None]
@@ -204,11 +207,10 @@
     for k in range(count):
         result = jnp.dot(hidden_ref[k], w2_ref[k], preferred_element_type=jnp.float32)
         y_ref[k] = jnp.maximum(result + b2_ref[k : k + 1, :], 0.0)
-    place = lax.axis_index("tower")
-    for o, out in zip(offsets(towers), outs):
-        start = pl.multiple_of((place ^ o) * per, per)
+    for j, out in zip(rounds(towers, pair), outs):
         pieces = [
-            y_ref[k, pl.ds(start, per), v * EDIM : (v + 1) * EDIM]
+            y_ref[k, n * per : (n + 1) * per, v * EDIM : (v + 1) * EDIM]
+            for n in range(j * pair, (j + 1) * pair)
             for k in range(count)
             for v in range(vectors)
         ]
@@ -224,7 +226,7 @@
     held, rows, _ = blocks[0].shape
     count, depth, hid = w1.shape
     width = w2.shape[2]
-    local = count * (width // EDIM) * (rows // towers)
+    local = pair * count * (width // EDIM) * (rows // towers)
     w1 = pltpu.with_memory_space_constraint(w1, pltpu.VMEM)
     w2 = pltpu.with_memory_space_constraint(w2, pltpu.VMEM)
     params = pltpu.CompilerParams(vmem_limit_bytes=16 << 20)
@@ -247,10 +249,10 @@
         )(slots, w1, *(blocks[n] for n in stage), *sums)
     return pl.pallas_call(
         functools.partial(tower_kernel, towers, intra, pair, [order[n] for n in late]),
-        out_shape=[pltpu.VMEM((local, EDIM), jnp.bfloat16)] * towers,
+        out_shape=[pltpu.VMEM((local, EDIM), jnp.bfloat16)] * (towers // pair),
         in_specs=[pl.BlockSpec(memory_space=pltpu.SMEM)]
         + [pl.BlockSpec(memory_space=pltpu.VMEM)] * (5 + len(late)),
-        out_specs=[pl.BlockSpec(memory_space=pltpu.VMEM)] * towers,
+        out_specs=[pl.BlockSpec(memory_space=pltpu.VMEM)] * (towers // pair),
         scratch_shapes=[
             pltpu.VMEM((count * rows, max(len(late), 1) * held * EDIM), jnp.bfloat16),
             pltpu.VMEM((count, rows, hid), jnp.bfloat16),
@@ -261,14 +263,16 @@
     )(slots, w1, b1, w2, b2, *sums, *(blocks[n] for n in late))
 
 
-def interact_kernel(towers, proj_ref, *rest):
+def interact_kernel(towers, pair, proj_ref, *rest):
     blocks, out, all_ref = rest[:towers], rest[towers], rest[towers + 1]
     per, count, _ = out.shape
-    local = blocks[0].shape[0]
-    place = lax.axis_index("tower")
-    for o, block in zip(offsets(towers), blocks):
-        start = pl.multiple_of((place ^ o) * local, local)
-        all_ref[pl.ds(start, local), :] = block[...].astype(jnp.float32)
+    local, half = blocks[0].shape[0] // pair, towers // pair
+    place, core = lax.axis_index("tower"), lax.axis_index("intra") % pair
+    own = pl.multiple_of(core * local, local)
+    for n, block in enumerate(blocks):
+        offset = rounds(towers, pair)[n % half] + (core ^ (n // half)) * half
+        start = pl.multiple_of((place ^ offset) * local, local)
+        all_ref[pl.ds(start, local), :] = block[pl.ds(own, local), :].astype(jnp.float32)
     group = max(1, min(per, 128 // count))
     proj = jnp.concatenate([proj_ref[...]] * (2 * group), axis=0)
     for first in range(0, per, group):
@@ -298,13 +302,13 @@
             out[d] = result[g * count : (g + 1) * count, :].astype(out.dtype)
 
 
-def interact(proj, blocks):
+def interact(proj, blocks, pair):
     towers = len(blocks)
-    local = blocks[0].shape[0]
+    local = blocks[0].shape[0] // pair
     count = proj.shape[0]
     per = towers * local // count
     return pl.pallas_call(
-        functools.partial(interact_kernel, towers),
+        functools.partial(interact_kernel, towers, pair),
         out_shape=jax.ShapeDtypeStruct((per, count, EDIM), jnp.bfloat16),
         in_specs=[pl.BlockSpec(memory_space=pltpu.VMEM)] * (1 + towers),
         out_specs=pl.BlockSpec(memory_space=pltpu.VMEM),
@@ -327,15 +331,15 @@
     towers, intra = lax.axis_size("tower"), lax.axis_size("intra")
     small = (feature_assign, first_bias, tower_bias, proj_weight)
     ahead = 10_000 * (first_weight.size + tower_weight.size)
-    pair = 2 if intra % 2 == 0 else 1
+    pair = 2 if intra % 2 == 0 and towers % 2 == 0 else 1
     blocks, small = gather_blocks(sample_owner, embeddings, small, towers, intra, pair, ahead)
     slots, first_bias, tower_bias, proj_weight = small
     blocks = exchange_chips(blocks, intra, pair)
     vectors = run_towers(
         slots, first_weight, first_bias, tower_weight, tower_bias, blocks, towers, intra, pair
     )
-    vectors = exchange_groups(vectors, towers, intra)
-    return interact(proj_weight, vectors)
+    vectors = exchange_groups(vectors, towers, intra, pair)
+    return interact(proj_weight, vectors, pair)
 
 
 def solution(mesh):

time: 20.2 us -> 22.1 us (1.094)
  starting transfers between devices: 9.97 us -> 12.1 us
  waiting for transfers between devices: 5.67 us -> 5.35 us
    ppermute x3 -> x4, starting transfers between devices: 2.99 us -> 5.14 us  [the longest x2 2.94 us: exchange_groups(): lax.ppermute(block, 'intra', swaps)]
    ppermute x3 -> x4, waiting for transfers between devices: 2.82 us -> 2.5 us  [the longest x2 1.67 us: exchange_groups(): received.append(lax.ppermute(block, ('tower', 'intra'), pairs))]
  transfers between devices with their start and end apart: 7 -> 8, of which waited for: 6 -> 5; matrix products, arithmetic and copies ran while one was open for 0% -> 0% of each run, Pallas kernels for 12% -> 11%
where the time goes in v6:
time: 22.1 us; the launch traced here: 21.9 us
  starting transfers between devices  12.1 us (55%)
  waiting for transfers between devices  5.35 us (24%)
  Pallas kernels  4.4 us (20%)
    ppermute x3, starting transfers between devices, exchange_chips(): lax.ppermute(block, 'intra', [(i, partner(i, s, intra, pair)) for i in ra...  6.52 us
    ppermute x2, starting transfers between devices, exchange_groups(): lax.ppermute(block, 'intra', swaps)  2.94 us
    ppermute x3, waiting for transfers between devices, exchange_chips(): lax.ppermute(block, 'intra', [(i, partner(i, s, intra, pair)) for i in ra...  2.5 us
    ppermute x2, starting transfers between devices, exchange_groups(): received.append(lax.ppermute(block, ('tower', 'intra'), pairs))  2.2 us
    ppermute x2, waiting for transfers between devices, exchange_groups(): received.append(lax.ppermute(block, ('tower', 'intra'), pairs))  1.67 us
    pallas_call x2, Pallas kernels, run_towers(): pl.pallas_call(functools.partial(early_kernel, intra, pair, [order[n] for...  1.4 us
    pallas_call x1, Pallas kernels, gather_blocks(): pl.pallas_call(functools.partial(load_kernel, len(small)), out_shape=[plt...  1.02 us
    pallas_call x1, Pallas kernels, interact(): pl.pallas_call(functools.partial(interact_kernel, towers, pair), out_shap...  0.94 us
  transfers between devices with their start and end apart: 8, of which 5 were waited for; matrix products, arithmetic and copies ran while one was open for 0% of the time, Pallas kernels for 11%

profile of v6, /device:TPU:0, one launch (start us, length us, event | category | flops | bytes accessed | tf_op | source)
XLA Modules:
  0.0 21.9 jit_solution(15267378248053456566)
XLA Ops:
  0.0 0.5 %collective-permute-start = (bf16[256,512]{1,0:T(8,128)(2,1)}, bf16[256,512]{1,0:T(8,128)(2,1)S(1)}, u32[]{:S(2)}, u32[]{:S(2)}) collective-permute-start(bf16[256,512]{1,0:T(8,128)(2,1)} %emb_hbm.1), channel_id=1, source_target_pairs={{0,1},{1,0},{2,3},{3,2},{4,5},{5,4},{6,7},{7,6},{8,9},{9,8},{10,11... | collective-permute-start | bytes 786440 | tf_op jit(solution)/shard_map/ppermute | solution.py:109
  0.5 1.0 %load.1 = (bf16[256,256]{1,0:T(8,128)(2,1)S(1)}, bf16[256,512]{1,0:T(8,128)(2,1)S(1)}, s32[1,32]{1,0:T(1,128)S(4)}, f32[2,1024]{1,0:T(2,128)S(1)}, f32[2,256]{1,0:T(2,128)S(1)}, /*index=5*/bf16[16,128]{1,0:T(8,128)(2,1)S(1)}) custom-call(s32[256]{0:T(256)} %owner_hbm.1, bf16[256,512]{1,0:T(8,128)(2,1)} %emb_hbm.1, s32[1,32]{1,0:T(1,128)} %rest_0_.1, ...), custom_call_target="tpu_custom_call" | custom-call | tf_op jit(solution)/shard_map/load/pallas_call | solution.py:112
  1.5 0.3 %collective-permute-done.rest_1_ = bf16[256,512]{1,0:T(8,128)(2,1)S(1)} collective-permute-done((bf16[256,512]{1,0:T(8,128)(2,1)}, bf16[256,512]{1,0:T(8,128)(2,1)S(1)}, u32[]{:S(2)}, u32[]{:S(2)}) %collective-permute-start) | collective-permute-done | bytes 262176 | tf_op jit(solution)/shard_map/ppermute | solution.py:109
  1.8 0.3 %gather_rows.1 = (bf16[8,32,128]{2,1,0:T(8,128)(2,1)S(1)}, bf16[8,32,128]{2,1,0:T(8,128)(2,1)S(1)}, bf16[8,32,128]{2,1,0:T(8,128)(2,1)S(1)}, bf16[8,32,128]{2,1,0:T(8,128)(2,1)S(1)}) custom-call(bf16[256,256]{1,0:T(8,128)(2,1)S(1)} %get-tuple-element.21.picks_ref, bf16[256,512]{1,0:T(8,128)(2,1)S(1)} %get-tuple-element.22.rest_0_, ...), custom_call_target="tpu_custom_call" | custom-call | flops 47185920000 | tf_op jit(solution)/shard_map/gather_rows/pallas_call | solution.py:132
  2.2 2.7 %collective-permute-start.2 = (bf16[8,32,128]{2,1,0:T(8,128)(2,1)S(1)}, bf16[8,32,128]{2,1,0:T(8,128)(2,1)S(1)}, u32[]{:S(2)}, u32[]{:S(2)}) collective-permute-start(bf16[8,32,128]{2,1,0:T(8,128)(2,1)S(1)} %get-tuple-element.25), channel_id=1, source_target_pairs={{0,3},{1,2},{2,7},{3,6},{4,1},{5,0},{6,5},{7,4},{8,11},{9,10},{10,... | collective-permute-start | bytes 196616 | tf_op jit(solution)/shard_map/ppermute | solution.py:42
  4.9 2.5 %collective-permute-start.1 = (bf16[8,32,128]{2,1,0:T(8,128)(2,1)S(1)}, bf16[8,32,128]{2,1,0:T(8,128)(2,1)S(1)}, u32[]{:S(2)}, u32[]{:S(2)}) collective-permute-start(bf16[8,32,128]{2,1,0:T(8,128)(2,1)S(1)} %get-tuple-element.23), channel_id=1, source_target_pairs={{0,7},{1,6},{2,5},{3,4},{4,3},{5,2},{6,1},{7,0},{8,15},{9,14},{10,... | collective-permute-start | bytes 196616 | tf_op jit(solution)/shard_map/ppermute | solution.py:42
  7.4 1.3 %collective-permute-start.3 = (bf16[8,32,128]{2,1,0:T(8,128)(2,1)S(1)}, bf16[8,32,128]{2,1,0:T(8,128)(2,1)S(1)}, u32[]{:S(2)}, u32[]{:S(2)}) collective-permute-start(bf16[8,32,128]{2,1,0:T(8,128)(2,1)S(1)} %get-tuple-element.26), channel_id=1, source_target_pairs={{0,5},{1,4},{2,1},{3,0},{4,7},{5,6},{6,3},{7,2},{8,13},{9,12},{10,... | collective-permute-start | bytes 196616 | tf_op jit(solution)/shard_map/ppermute | solution.py:42
  8.7 0.0 collective-permute-done.2.rest_1_
  8.7 0.0 copy-done
  8.7 0.9 %towers_early.2.rest_1_ = f32[64,1024]{1,0:T(8,128)S(1)} custom-call(s32[1,32]{1,0:T(1,128)S(4)} %get-tuple-element.18.slots_ref, bf16[2,2048,1024]{2,1,0:T(8,128)(2,1)S(1)} %copy-done, bf16[8,32,128]{2,1,0:T(8,128)(2,1)S(1)} %get-tuple-element.24.rest_0_, bf16[8,32,128]{2,1,0:T(8,128)(2,1)S(1)} %collective-permute-done.2.rest_1_), custom_call_target="tpu_custom_call" | custom-call | flops 268435456 | tf_op jit(solution)/shard_map/towers_early/pallas_call | solution.py:237
  9.6 1.7 %collective-permute-done.1.rest_0_ = bf16[8,32,128]{2,1,0:T(8,128)(2,1)S(1)} collective-permute-done((bf16[8,32,128]{2,1,0:T(8,128)(2,1)S(1)}, bf16[8,32,128]{2,1,0:T(8,128)(2,1)S(1)}, u32[]{:S(2)}, u32[]{:S(2)}) %collective-permute-start.1) | collective-permute-done | bytes 65568 | tf_op jit(solution)/shard_map/ppermute | solution.py:42
  11.3 0.5 %towers_early.3.sums_ref = f32[64,1024]{1,0:T(8,128)S(1)} custom-call(s32[1,32]{1,0:T(1,128)S(4)} %get-tuple-element.18.slots_ref, bf16[2,2048,1024]{2,1,0:T(8,128)(2,1)S(1)} %copy-done, bf16[8,32,128]{2,1,0:T(8,128)(2,1)S(1)} %collective-permute-done.1.rest_0_, f32[64,1024]{1,0:T(8,128)S(1)} %towers_early.2.rest_1_), custom_call_target="tpu_custom_call" | custom-call | flops 268435456 | tf_op jit(solution)/shard_map/towers_early/pallas_call | solution.py:237
  11.8 0.8 %collective-permute-done.3.rest_0_ = bf16[8,32,128]{2,1,0:T(8,128)(2,1)S(1)} collective-permute-done((bf16[8,32,128]{2,1,0:T(8,128)(2,1)S(1)}, bf16[8,32,128]{2,1,0:T(8,128)(2,1)S(1)}, u32[]{:S(2)}, u32[]{:S(2)}) %collective-permute-start.3) | collective-permute-done | bytes 65568 | tf_op jit(solution)/shard_map/ppermute | solution.py:42
  12.6 0.0 copy-done.1
  12.6 0.7 %towers.1 = (bf16[64,128]{1,0:T(8,128)(2,1)S(1)}, bf16[64,128]{1,0:T(8,128)(2,1)S(1)}) custom-call(s32[1,32]{1,0:T(1,128)S(4)} %get-tuple-element.18.slots_ref, bf16[2,2048,1024]{2,1,0:T(8,128)(2,1)S(1)} %copy-done, f32[2,1024]{1,0:T(2,128)S(1)} %get-tuple-element.19.b1_ref, bf16[2,1024,256]{2,1,0:T(8,128)(2,1)S(1)} %copy-done.1, ...), custom_call_target="tpu_custom_call" | custom-call | tf_op jit(solution)/shard_map/towers/pallas_call | solution.py:250
  13.3 1.6 %collective-permute-start.4 = (bf16[64,128]{1,0:T(8,128)(2,1)S(1)}, bf16[64,128]{1,0:T(8,128)(2,1)S(1)}, u32[]{:S(2)}, u32[]{:S(2)}) collective-permute-start(bf16[64,128]{1,0:T(8,128)(2,1)S(1)} %get-tuple-element.27), channel_id=1, source_target_pairs={{0,8},{1,25},{2,10},{3,27},{4,12},{5,29},{6,14},{7,31},{8,0},{9,17... | collective-permute-start | bytes 49160 | tf_op jit(solution)/shard_map/ppermute | solution.py:56
  14.9 0.7 %collective-permute-start.5 = (bf16[64,128]{1,0:T(8,128)(2,1)S(1)}, bf16[64,128]{1,0:T(8,128)(2,1)S(1)}, u32[]{:S(2)}, u32[]{:S(2)}) collective-permute-start(bf16[64,128]{1,0:T(8,128)(2,1)S(1)} %get-tuple-element.28), channel_id=1, source_target_pairs={{0,0},{1,17},{2,2},{3,19},{4,4},{5,21},{6,6},{7,23},{8,8},{9,25},{... | collective-permute-start | bytes 49160 | tf_op jit(solution)/shard_map/ppermute | solution.py:56
  15.5 1.7 %collective-permute-done.4.rest_0_ = bf16[64,128]{1,0:T(8,128)(2,1)S(1)} collective-permute-done((bf16[64,128]{1,0:T(8,128)(2,1)S(1)}, bf16[64,128]{1,0:T(8,128)(2,1)S(1)}, u32[]{:S(2)}, u32[]{:S(2)}) %collective-permute-start.4) | collective-permute-done | bytes 16416 | tf_op jit(solution)/shard_map/ppermute | solution.py:56
  17.2 0.7 %collective-permute-start.6 = (bf16[64,128]{1,0:T(8,128)(2,1)S(1)}, bf16[64,128]{1,0:T(8,128)(2,1)S(1)}, u32[]{:S(2)}, u32[]{:S(2)}) collective-permute-start(bf16[64,128]{1,0:T(8,128)(2,1)S(1)} %collective-permute-done.4.rest_0_), channel_id=1, source_target_pairs={{0,1},{1,0},{2,3},{3,2},{4,5},{5,4},{6,7},{7,6},{8,9},{9,8},{10,11... | collective-permute-start | bytes 49160 | tf_op jit(solution)/shard_map/ppermute | solution.py:58
  17.9 0.0 collective-permute-done.5.rest_1_
  17.9 2.3 %collective-permute-start.7 = (bf16[64,128]{1,0:T(8,128)(2,1)S(1)}, bf16[64,128]{1,0:T(8,128)(2,1)S(1)}, u32[]{:S(2)}, u32[]{:S(2)}) collective-permute-start(bf16[64,128]{1,0:T(8,128)(2,1)S(1)} %collective-permute-done.5.rest_1_), channel_id=1, source_target_pairs={{0,1},{1,0},{2,3},{3,2},{4,5},{5,4},{6,7},{7,6},{8,9},{9,8},{10,11... | collective-permute-start | bytes 49160 | tf_op jit(solution)/shard_map/ppermute | solution.py:58
  20.1 0.0 collective-permute-done.6.rest_2_
  20.1 0.8 %collective-permute-done.7.rest_3_ = bf16[64,128]{1,0:T(8,128)(2,1)S(1)} collective-permute-done((bf16[64,128]{1,0:T(8,128)(2,1)S(1)}, bf16[64,128]{1,0:T(8,128)(2,1)S(1)}, u32[]{:S(2)}, u32[]{:S(2)}) %collective-permute-start.7) | collective-permute-done | bytes 16416 | tf_op jit(solution)/shard_map/ppermute | solution.py:58
  21.0 0.9 %interact.1 = bf16[8,16,128]{2,1,0:T(8,128)(2,1)} custom-call(bf16[16,128]{1,0:T(8,128)(2,1)S(1)} %get-tuple-element.17.proj_ref, bf16[64,128]{1,0:T(8,128)(2,1)S(1)} %collective-permute-done.4.rest_0_, bf16[64,128]{1,0:T(8,128)(2,1)S(1)} %collective-permute-done.5.rest_1_, bf16[64,128]{1,0:T(8,128)(2,1)S(1)} %collective-permute-done.6.rest_2_, ...), custom_call_target="tpu_custom_call" | custom-call | tf_op jit(solution)/shard_map/interact/pallas_call | solution.py:310
  (2 shorter events, 0.0 us)
Async XLA Ops:
  0.0 1.8 %collective-permute-start = (bf16[256,512]{1,0:T(8,128)(2,1)}, bf16[256,512]{1,0:T(8,128)(2,1)S(1)}, u32[]{:S(2)}, u32[]{:S(2)}) collective-permute-start(bf16[256,512]{1,0:T(8,128)(2,1)} %emb_hbm.1), channel_id=1, source_target_pairs={{0,1},{1,0},{2,3},{3,2},{4,5},{5,4},{6,7},{7,6},{8,9},{9,8},{10,11... | collective-permute-start | bytes 786440 | tf_op jit(solution)/shard_map/ppermute | solution.py:109
  1.8 6.9 %copy-start = (bf16[2,2048,1024]{2,1,0:T(8,128)(2,1)S(1)}, bf16[2,2048,1024]{2,1,0:T(8,128)(2,1)}, u32[]{:S(2)}) copy-start(bf16[2,2048,1024]{2,1,0:T(8,128)(2,1)} %w1_ref.5) | copy-start | bytes 25165828
  2.2 6.5 %collective-permute-start.2 = (bf16[8,32,128]{2,1,0:T(8,128)(2,1)S(1)}, bf16[8,32,128]{2,1,0:T(8,128)(2,1)S(1)}, u32[]{:S(2)}, u32[]{:S(2)}) collective-permute-start(bf16[8,32,128]{2,1,0:T(8,128)(2,1)S(1)} %get-tuple-element.25), channel_id=1, source_target_pairs={{0,3},{1,2},{2,7},{3,6},{4,1},{5,0},{6,5},{7,4},{8,11},{9,10},{10,... | collective-permute-start | bytes 196616 | tf_op jit(solution)/shard_map/ppermute | solution.py:42
  4.9 6.4 %collective-permute-start.1 = (bf16[8,32,128]{2,1,0:T(8,128)(2,1)S(1)}, bf16[8,32,128]{2,1,0:T(8,128)(2,1)S(1)}, u32[]{:S(2)}, u32[]{:S(2)}) collective-permute-start(bf16[8,32,128]{2,1,0:T(8,128)(2,1)S(1)} %get-tuple-element.23), channel_id=1, source_target_pairs={{0,7},{1,6},{2,5},{3,4},{4,3},{5,2},{6,1},{7,0},{8,15},{9,14},{10,... | collective-permute-start | bytes 196616 | tf_op jit(solution)/shard_map/ppermute | solution.py:42
  7.4 5.3 %collective-permute-start.3 = (bf16[8,32,128]{2,1,0:T(8,128)(2,1)S(1)}, bf16[8,32,128]{2,1,0:T(8,128)(2,1)S(1)}, u32[]{:S(2)}, u32[]{:S(2)}) collective-permute-start(bf16[8,32,128]{2,1,0:T(8,128)(2,1)S(1)} %get-tuple-element.26), channel_id=1, source_target_pairs={{0,5},{1,4},{2,1},{3,0},{4,7},{5,6},{6,3},{7,2},{8,13},{9,12},{10,... | collective-permute-start | bytes 196616 | tf_op jit(solution)/shard_map/ppermute | solution.py:42
  8.7 3.9 %copy-start.1 = (bf16[2,1024,256]{2,1,0:T(8,128)(2,1)S(1)}, bf16[2,1024,256]{2,1,0:T(8,128)(2,1)}, u32[]{:S(2)}) copy-start(bf16[2,1024,256]{2,1,0:T(8,128)(2,1)} %w2_ref.1) | copy-start | bytes 3145732
  13.3 3.9 %collective-permute-start.4 = (bf16[64,128]{1,0:T(8,128)(2,1)S(1)}, bf16[64,128]{1,0:T(8,128)(2,1)S(1)}, u32[]{:S(2)}, u32[]{:S(2)}) collective-permute-start(bf16[64,128]{1,0:T(8,128)(2,1)S(1)} %get-tuple-element.27), channel_id=1, source_target_pairs={{0,8},{1,25},{2,10},{3,27},{4,12},{5,29},{6,14},{7,31},{8,0},{9,17... | collective-permute-start | bytes 49160 | tf_op jit(solution)/shard_map/ppermute | solution.py:56
  14.9 3.0 %collective-permute-start.5 = (bf16[64,128]{1,0:T(8,128)(2,1)S(1)}, bf16[64,128]{1,0:T(8,128)(2,1)S(1)}, u32[]{:S(2)}, u32[]{:S(2)}) collective-permute-start(bf16[64,128]{1,0:T(8,128)(2,1)S(1)} %get-tuple-element.28), channel_id=1, source_target_pairs={{0,0},{1,17},{2,2},{3,19},{4,4},{5,21},{6,6},{7,23},{8,8},{9,25},{... | collective-permute-start | bytes 49160 | tf_op jit(solution)/shard_map/ppermute | solution.py:56
  17.2 2.9 %collective-permute-start.6 = (bf16[64,128]{1,0:T(8,128)(2,1)S(1)}, bf16[64,128]{1,0:T(8,128)(2,1)S(1)}, u32[]{:S(2)}, u32[]{:S(2)}) collective-permute-start(bf16[64,128]{1,0:T(8,128)(2,1)S(1)} %collective-permute-done.4.rest_0_), channel_id=1, source_target_pairs={{0,1},{1,0},{2,3},{3,2},{4,5},{5,4},{6,7},{7,6},{8,9},{9,8},{10,11... | collective-permute-start | bytes 49160 | tf_op jit(solution)/shard_map/ppermute | solution.py:58
  17.9 3.1 %collective-permute-start.7 = (bf16[64,128]{1,0:T(8,128)(2,1)S(1)}, bf16[64,128]{1,0:T(8,128)(2,1)S(1)}, u32[]{:S(2)}, u32[]{:S(2)}) collective-permute-start(bf16[64,128]{1,0:T(8,128)(2,1)S(1)} %collective-permute-done.5.rest_1_), channel_id=1, source_target_pairs={{0,1},{1,0},{2,3},{3,2},{4,5},{5,4},{6,7},{7,6},{8,9},{9,8},{10,11... | collective-permute-start | bytes 49160 | tf_op jit(solution)/shard_map/ppermute | solution.py:58

commit v7 on v5

--- a/solution.py
+++ b/solution.py
@@ -173,16 +173,10 @@
     wide = 2 * EDIM
     for h in range(0, hid, wide):
         columns = slice(h, min(h + wide, hid))
-        total = None if before_ref is None else before_ref[:, columns]
-        for n in range(0, len(slots), 2):
-            some = slots[n : n + 2]
-            weight = [w1_ref[k, pl.ds(start, EDIM), columns] for k, start in some]
-            term = jnp.dot(
-                x_ref[:, n * EDIM : (n + len(some)) * EDIM],
-                jnp.concatenate(weight, axis=0),
-                preferred_element_type=jnp.float32,
-            )
-            total = term if total is None else total + term
+        weight = [w1_ref[k, pl.ds(start, EDIM), columns] for k, start in slots]
+        total = jnp.dot(x_ref[...], jnp.concatenate(weight, axis=0), preferred_element_type=jnp.float32)
+        if before_ref is not None:
+            total = total + before_ref[:, columns]
         yield columns, total
 
 
@@ -193,17 +187,19 @@
 
 
 def tower_kernel(towers, intra, pair, order, slots_ref, w1_ref, b1_ref, w2_ref, b2_ref, sums_ref, *rest):
-    blocks, outs, (x_ref, hidden_ref, y_ref) = rest[: len(order)], rest[len(order) : -3], rest[-3:]
+    blocks, outs, (x_ref, y_ref) = rest[: len(order)], rest[len(order) : -2], rest[-2:]
     count, rows, _ = y_ref.shape
     vectors = w2_ref.shape[2] // EDIM
     per = rows // towers
+    results = [None] * count
     for columns, total in first_layer(intra, pair, order, slots_ref, w1_ref, x_ref, blocks, sums_ref):
         for k in range(count):
             hidden = total[k * rows : (k + 1) * rows] + b1_ref[k : k + 1, columns]
-            hidden_ref[k, :, columns] = jnp.maximum(hidden, 0.0).astype(jnp.bfloat16)
+            hidden = jnp.maximum(hidden, 0.0).astype(jnp.bfloat16)
+            term = jnp.dot(hidden, w2_ref[k, columns, :], preferred_element_type=jnp.float32)
+            results[k] = term if results[k] is None else results[k] + term
     for k in range(count):
-        result = jnp.dot(hidden_ref[k], w2_ref[k], preferred_element_type=jnp.float32)
-        y_ref[k] = jnp.maximum(result + b2_ref[k : k + 1, :], 0.0)
+        y_ref[k] = jnp.maximum(results[k] + b2_ref[k : k + 1, :], 0.0)
     place = lax.axis_index("tower")
     for o, out in zip(offsets(towers), outs):
         start = pl.multiple_of((place ^ o) * per, per)
@@ -253,7 +249,6 @@
         out_specs=[pl.BlockSpec(memory_space=pltpu.VMEM)] * towers,
         scratch_shapes=[
             pltpu.VMEM((count * rows, max(len(late), 1) * held * EDIM), jnp.bfloat16),
-            pltpu.VMEM((count, rows, hid), jnp.bfloat16),
             pltpu.VMEM((count, rows, width), jnp.float32),
         ],
         compiler_params=params,

time: 20.2 us -> 20.6 us (1.020)
  Pallas kernels: 4.4 us -> 4.74 us
    pallas_call x1, Pallas kernels: 0.69 us -> 1.02 us  [run_towers(): pl.pallas_call(functools.partial(tower_kernel, towers, intra, pair, [orde...]
where the time goes in v7:
time: 20.6 us; the launch traced here: 20.4 us
  starting transfers between devices  9.97 us (48%)
  waiting for transfers between devices  5.67 us (28%)
  Pallas kernels  4.74 us (23%)
    ppermute x3, starting transfers between devices, exchange_chips(): lax.ppermute(block, 'intra', [(i, partner(i, s, intra, pair)) for i in ra...  6.52 us
    ppermute x3, starting transfers between devices, exchange_groups(): lax.ppermute(block, ('tower', 'intra'), pairs)  2.99 us
    ppermute x3, waiting for transfers between devices, exchange_groups(): lax.ppermute(block, ('tower', 'intra'), pairs)  2.82 us
    ppermute x3, waiting for transfers between devices, exchange_chips(): lax.ppermute(block, 'intra', [(i, partner(i, s, intra, pair)) for i in ra...  2.5 us
    pallas_call x2, Pallas kernels, run_towers(): pl.pallas_call(functools.partial(early_kernel, intra, pair, [order[n] for...  1.4 us
    pallas_call x1, Pallas kernels, run_towers(): pl.pallas_call(functools.partial(tower_kernel, towers, intra, pair, [orde...  1.02 us
    pallas_call x1, Pallas kernels, gather_blocks(): pl.pallas_call(functools.partial(load_kernel, len(small)), out_shape=[plt...  1.02 us
    pallas_call x1, Pallas kernels, interact(): pl.pallas_call(functools.partial(interact_kernel, towers), out_shape=jax....  0.94 us
  transfers between devices with their start and end apart: 7, of which 6 were waited for; matrix products, arithmetic and copies ran while one was open for 0% of the time, Pallas kernels for 12%

profile of v7, /device:TPU:0, one launch (start us, length us, event | category | flops | bytes accessed | tf_op | source)
XLA Modules:
  0.0 20.4 jit_solution(9487451102626097935)
XLA Ops:
  0.0 0.5 %collective-permute-start = (bf16[256,512]{1,0:T(8,128)(2,1)}, bf16[256,512]{1,0:T(8,128)(2,1)S(1)}, u32[]{:S(2)}, u32[]{:S(2)}) collective-permute-start(bf16[256,512]{1,0:T(8,128)(2,1)} %emb_hbm.1), channel_id=1, source_target_pairs={{0,1},{1,0},{2,3},{3,2},{4,5},{5,4},{6,7},{7,6},{8,9},{9,8},{10,11... | collective-permute-start | bytes 786440 | tf_op jit(solution)/shard_map/ppermute | solution.py:106
  0.5 1.0 %load.1 = (bf16[256,256]{1,0:T(8,128)(2,1)S(1)}, bf16[256,512]{1,0:T(8,128)(2,1)S(1)}, s32[1,32]{1,0:T(1,128)S(4)}, f32[2,1024]{1,0:T(2,128)S(1)}, f32[2,256]{1,0:T(2,128)S(1)}, /*index=5*/bf16[16,128]{1,0:T(8,128)(2,1)S(1)}) custom-call(s32[256]{0:T(256)} %owner_hbm.1, bf16[256,512]{1,0:T(8,128)(2,1)} %emb_hbm.1, s32[1,32]{1,0:T(1,128)} %rest_0_.1, ...), custom_call_target="tpu_custom_call" | custom-call | tf_op jit(solution)/shard_map/load/pallas_call | solution.py:109
  1.5 0.3 %collective-permute-done.rest_1_ = bf16[256,512]{1,0:T(8,128)(2,1)S(1)} collective-permute-done((bf16[256,512]{1,0:T(8,128)(2,1)}, bf16[256,512]{1,0:T(8,128)(2,1)S(1)}, u32[]{:S(2)}, u32[]{:S(2)}) %collective-permute-start) | collective-permute-done | bytes 262176 | tf_op jit(solution)/shard_map/ppermute | solution.py:106
  1.8 0.0 copy-start
  1.8 0.3 %gather_rows.1 = (bf16[8,32,128]{2,1,0:T(8,128)(2,1)S(1)}, bf16[8,32,128]{2,1,0:T(8,128)(2,1)S(1)}, bf16[8,32,128]{2,1,0:T(8,128)(2,1)S(1)}, bf16[8,32,128]{2,1,0:T(8,128)(2,1)S(1)}) custom-call(bf16[256,256]{1,0:T(8,128)(2,1)S(1)} %get-tuple-element.23.picks_ref, bf16[256,512]{1,0:T(8,128)(2,1)S(1)} %get-tuple-element.24.rest_0_, ...), custom_call_target="tpu_custom_call" | custom-call | flops 47185920000 | tf_op jit(solution)/shard_map/gather_rows/pallas_call | solution.py:129
  2.2 2.7 %collective-permute-start.2 = (bf16[8,32,128]{2,1,0:T(8,128)(2,1)S(1)}, bf16[8,32,128]{2,1,0:T(8,128)(2,1)S(1)}, u32[]{:S(2)}, u32[]{:S(2)}) collective-permute-start(bf16[8,32,128]{2,1,0:T(8,128)(2,1)S(1)} %get-tuple-element.27), channel_id=1, source_target_pairs={{0,3},{1,2},{2,7},{3,6},{4,1},{5,0},{6,5},{7,4},{8,11},{9,10},{10,... | collective-permute-start | bytes 196616 | tf_op jit(solution)/shard_map/ppermute | solution.py:42
  4.9 2.5 %collective-permute-start.1 = (bf16[8,32,128]{2,1,0:T(8,128)(2,1)S(1)}, bf16[8,32,128]{2,1,0:T(8,128)(2,1)S(1)}, u32[]{:S(2)}, u32[]{:S(2)}) collective-permute-start(bf16[8,32,128]{2,1,0:T(8,128)(2,1)S(1)} %get-tuple-element.25), channel_id=1, source_target_pairs={{0,7},{1,6},{2,5},{3,4},{4,3},{5,2},{6,1},{7,0},{8,15},{9,14},{10,... | collective-permute-start | bytes 196616 | tf_op jit(solution)/shard_map/ppermute | solution.py:42
  7.4 1.3 %collective-permute-start.3 = (bf16[8,32,128]{2,1,0:T(8,128)(2,1)S(1)}, bf16[8,32,128]{2,1,0:T(8,128)(2,1)S(1)}, u32[]{:S(2)}, u32[]{:S(2)}) collective-permute-start(bf16[8,32,128]{2,1,0:T(8,128)(2,1)S(1)} %get-tuple-element.28), channel_id=1, source_target_pairs={{0,5},{1,4},{2,1},{3,0},{4,7},{5,6},{6,3},{7,2},{8,13},{9,12},{10,... | collective-permute-start | bytes 196616 | tf_op jit(solution)/shard_map/ppermute | solution.py:42
  8.7 0.0 collective-permute-done.2.rest_1_
  8.7 0.0 copy-done
  8.7 0.0 copy-start.1
  8.7 0.9 %towers_early.2.rest_1_ = f32[64,1024]{1,0:T(8,128)S(1)} custom-call(s32[1,32]{1,0:T(1,128)S(4)} %get-tuple-element.20.slots_ref, bf16[2,2048,1024]{2,1,0:T(8,128)(2,1)S(1)} %copy-done, bf16[8,32,128]{2,1,0:T(8,128)(2,1)S(1)} %get-tuple-element.26.rest_0_, bf16[8,32,128]{2,1,0:T(8,128)(2,1)S(1)} %collective-permute-done.2.rest_1_), custom_call_target="tpu_custom_call" | custom-call | flops 268435456 | tf_op jit(solution)/shard_map/towers_early/pallas_call | solution.py:231
  9.6 1.7 %collective-permute-done.1.rest_0_ = bf16[8,32,128]{2,1,0:T(8,128)(2,1)S(1)} collective-permute-done((bf16[8,32,128]{2,1,0:T(8,128)(2,1)S(1)}, bf16[8,32,128]{2,1,0:T(8,128)(2,1)S(1)}, u32[]{:S(2)}, u32[]{:S(2)}) %collective-permute-start.1) | collective-permute-done | bytes 65568 | tf_op jit(solution)/shard_map/ppermute | solution.py:42
  11.3 0.5 %towers_early.3.sums_ref = f32[64,1024]{1,0:T(8,128)S(1)} custom-call(s32[1,32]{1,0:T(1,128)S(4)} %get-tuple-element.20.slots_ref, bf16[2,2048,1024]{2,1,0:T(8,128)(2,1)S(1)} %copy-done, bf16[8,32,128]{2,1,0:T(8,128)(2,1)S(1)} %collective-permute-done.1.rest_0_, f32[64,1024]{1,0:T(8,128)S(1)} %towers_early.2.rest_1_), custom_call_target="tpu_custom_call" | custom-call | flops 268435456 | tf_op jit(solution)/shard_map/towers_early/pallas_call | solution.py:231
  11.8 0.8 %collective-permute-done.3.rest_0_ = bf16[8,32,128]{2,1,0:T(8,128)(2,1)S(1)} collective-permute-done((bf16[8,32,128]{2,1,0:T(8,128)(2,1)S(1)}, bf16[8,32,128]{2,1,0:T(8,128)(2,1)S(1)}, u32[]{:S(2)}, u32[]{:S(2)}) %collective-permute-start.3) | collective-permute-done | bytes 65568 | tf_op jit(solution)/shard_map/ppermute | solution.py:42
  12.6 0.0 copy-done.1
  12.6 1.0 %towers.1 = (bf16[32,128]{1,0:T(8,128)(2,1)S(1)}, bf16[32,128]{1,0:T(8,128)(2,1)S(1)}, bf16[32,128]{1,0:T(8,128)(2,1)S(1)}, bf16[32,128]{1,0:T(8,128)(2,1)S(1)}) custom-call(s32[1,32]{1,0:T(1,128)S(4)} %get-tuple-element.20.slots_ref, bf16[2,2048,1024]{2,1,0:T(8,128)(2,1)S(1)} %copy-done, f32[2,1024]{1,0:T(2,128)S(1)} %get-tuple-element.21.b1_ref, ...), custom_call_target="tpu_custom_call" | custom-call | tf_op jit(solution)/shard_map/towers/pallas_call | solution.py:244
  13.7 2.2 %collective-permute-start.4 = (bf16[32,128]{1,0:T(8,128)(2,1)S(1)}, bf16[32,128]{1,0:T(8,128)(2,1)S(1)}, u32[]{:S(2)}, u32[]{:S(2)}) collective-permute-start(bf16[32,128]{1,0:T(8,128)(2,1)S(1)} %get-tuple-element.29), channel_id=1, source_target_pairs={{0,25},{1,24},{2,27},{3,26},{4,29},{5,28},{6,31},{7,30},{8,17},{9,... | collective-permute-start | bytes 24584 | tf_op jit(solution)/shard_map/ppermute | solution.py:59
  15.9 0.5 %collective-permute-start.5 = (bf16[32,128]{1,0:T(8,128)(2,1)S(1)}, bf16[32,128]{1,0:T(8,128)(2,1)S(1)}, u32[]{:S(2)}, u32[]{:S(2)}) collective-permute-start(bf16[32,128]{1,0:T(8,128)(2,1)S(1)} %get-tuple-element.30), channel_id=1, source_target_pairs={{0,17},{1,16},{2,19},{3,18},{4,21},{5,20},{6,23},{7,22},{8,25},{9,... | collective-permute-start | bytes 24584 | tf_op jit(solution)/shard_map/ppermute | solution.py:59
  16.4 0.3 %collective-permute-start.6 = (bf16[32,128]{1,0:T(8,128)(2,1)S(1)}, bf16[32,128]{1,0:T(8,128)(2,1)S(1)}, u32[]{:S(2)}, u32[]{:S(2)}) collective-permute-start(bf16[32,128]{1,0:T(8,128)(2,1)S(1)} %get-tuple-element.31), channel_id=1, source_target_pairs={{0,9},{1,8},{2,11},{3,10},{4,13},{5,12},{6,15},{7,14},{8,1},{9,0},... | collective-permute-start | bytes 24584 | tf_op jit(solution)/shard_map/ppermute | solution.py:59
  16.7 1.0 %collective-permute-done.4.rest_0_ = bf16[32,128]{1,0:T(8,128)(2,1)S(1)} collective-permute-done((bf16[32,128]{1,0:T(8,128)(2,1)S(1)}, bf16[32,128]{1,0:T(8,128)(2,1)S(1)}, u32[]{:S(2)}, u32[]{:S(2)}) %collective-permute-start.4) | collective-permute-done | bytes 8224 | tf_op jit(solution)/shard_map/ppermute | solution.py:59
  17.7 1.3 %collective-permute-done.5.rest_1_ = bf16[32,128]{1,0:T(8,128)(2,1)S(1)} collective-permute-done((bf16[32,128]{1,0:T(8,128)(2,1)S(1)}, bf16[32,128]{1,0:T(8,128)(2,1)S(1)}, u32[]{:S(2)}, u32[]{:S(2)}) %collective-permute-start.5) | collective-permute-done | bytes 8224 | tf_op jit(solution)/shard_map/ppermute | solution.py:59
  19.0 0.5 %collective-permute-done.6.rest_2_ = bf16[32,128]{1,0:T(8,128)(2,1)S(1)} collective-permute-done((bf16[32,128]{1,0:T(8,128)(2,1)S(1)}, bf16[32,128]{1,0:T(8,128)(2,1)S(1)}, u32[]{:S(2)}, u32[]{:S(2)}) %collective-permute-start.6) | collective-permute-done | bytes 8224 | tf_op jit(solution)/shard_map/ppermute | solution.py:59
  19.5 0.9 %interact.1 = bf16[8,16,128]{2,1,0:T(8,128)(2,1)} custom-call(bf16[16,128]{1,0:T(8,128)(2,1)S(1)} %get-tuple-element.19.proj_ref, bf16[32,128]{1,0:T(8,128)(2,1)S(1)} %collective-permute-done.4.rest_0_, bf16[32,128]{1,0:T(8,128)(2,1)S(1)} %collective-permute-done.5.rest_1_, bf16[32,128]{1,0:T(8,128)(2,1)S(1)} %collective-permute-done.6.rest_2_, ...), custom_call_target="tpu_custom_call" | custom-call | tf_op jit(solution)/shard_map/interact/pallas_call | solution.py:301
Async XLA Ops:
  0.0 1.8 %collective-permute-start = (bf16[256,512]{1,0:T(8,128)(2,1)}, bf16[256,512]{1,0:T(8,128)(2,1)S(1)}, u32[]{:S(2)}, u32[]{:S(2)}) collective-permute-start(bf16[256,512]{1,0:T(8,128)(2,1)} %emb_hbm.1), channel_id=1, source_target_pairs={{0,1},{1,0},{2,3},{3,2},{4,5},{5,4},{6,7},{7,6},{8,9},{9,8},{10,11... | collective-permute-start | bytes 786440 | tf_op jit(solution)/shard_map/ppermute | solution.py:106
  1.8 6.9 %copy-start = (bf16[2,2048,1024]{2,1,0:T(8,128)(2,1)S(1)}, bf16[2,2048,1024]{2,1,0:T(8,128)(2,1)}, u32[]{:S(2)}) copy-start(bf16[2,2048,1024]{2,1,0:T(8,128)(2,1)} %w1_ref.5) | copy-start | bytes 25165828
  2.2 6.5 %collective-permute-start.2 = (bf16[8,32,128]{2,1,0:T(8,128)(2,1)S(1)}, bf16[8,32,128]{2,1,0:T(8,128)(2,1)S(1)}, u32[]{:S(2)}, u32[]{:S(2)}) collective-permute-start(bf16[8,32,128]{2,1,0:T(8,128)(2,1)S(1)} %get-tuple-element.27), channel_id=1, source_target_pairs={{0,3},{1,2},{2,7},{3,6},{4,1},{5,0},{6,5},{7,4},{8,11},{9,10},{10,... | collective-permute-start | bytes 196616 | tf_op jit(solution)/shard_map/ppermute | solution.py:42
  4.9 6.4 %collective-permute-start.1 = (bf16[8,32,128]{2,1,0:T(8,128)(2,1)S(1)}, bf16[8,32,128]{2,1,0:T(8,128)(2,1)S(1)}, u32[]{:S(2)}, u32[]{:S(2)}) collective-permute-start(bf16[8,32,128]{2,1,0:T(8,128)(2,1)S(1)} %get-tuple-element.25), channel_id=1, source_target_pairs={{0,7},{1,6},{2,5},{3,4},{4,3},{5,2},{6,1},{7,0},{8,15},{9,14},{10,... | collective-permute-start | bytes 196616 | tf_op jit(solution)/shard_map/ppermute | solution.py:42
  7.4 5.3 %collective-permute-start.3 = (bf16[8,32,128]{2,1,0:T(8,128)(2,1)S(1)}, bf16[8,32,128]{2,1,0:T(8,128)(2,1)S(1)}, u32[]{:S(2)}, u32[]{:S(2)}) collective-permute-start(bf16[8,32,128]{2,1,0:T(8,128)(2,1)S(1)} %get-tuple-element.28), channel_id=1, source_target_pairs={{0,5},{1,4},{2,1},{3,0},{4,7},{5,6},{6,3},{7,2},{8,13},{9,12},{10,... | collective-permute-start | bytes 196616 | tf_op jit(solution)/shard_map/ppermute | solution.py:42
  8.7 3.9 %copy-start.1 = (bf16[2,1024,256]{2,1,0:T(8,128)(2,1)S(1)}, bf16[2,1024,256]{2,1,0:T(8,128)(2,1)}, u32[]{:S(2)}) copy-start(bf16[2,1024,256]{2,1,0:T(8,128)(2,1)} %w2_ref.1) | copy-start | bytes 3145732
  13.7 4.0 %collective-permute-start.4 = (bf16[32,128]{1,0:T(8,128)(2,1)S(1)}, bf16[32,128]{1,0:T(8,128)(2,1)S(1)}, u32[]{:S(2)}, u32[]{:S(2)}) collective-permute-start(bf16[32,128]{1,0:T(8,128)(2,1)S(1)} %get-tuple-element.29), channel_id=1, source_target_pairs={{0,25},{1,24},{2,27},{3,26},{4,29},{5,28},{6,31},{7,30},{8,17},{9,... | collective-permute-start | bytes 24584 | tf_op jit(solution)/shard_map/ppermute | solution.py:59
  15.9 3.1 %collective-permute-start.5 = (bf16[32,128]{1,0:T(8,128)(2,1)S(1)}, bf16[32,128]{1,0:T(8,128)(2,1)S(1)}, u32[]{:S(2)}, u32[]{:S(2)}) collective-permute-start(bf16[32,128]{1,0:T(8,128)(2,1)S(1)} %get-tuple-element.30), channel_id=1, source_target_pairs={{0,17},{1,16},{2,19},{3,18},{4,21},{5,20},{6,23},{7,22},{8,25},{9,... | collective-permute-start | bytes 24584 | tf_op jit(solution)/shard_map/ppermute | solution.py:59
  16.4 3.1 %collective-permute-start.6 = (bf16[32,128]{1,0:T(8,128)(2,1)S(1)}, bf16[32,128]{1,0:T(8,128)(2,1)S(1)}, u32[]{:S(2)}, u32[]{:S(2)}) collective-permute-start(bf16[32,128]{1,0:T(8,128)(2,1)S(1)} %get-tuple-element.31), channel_id=1, source_target_pairs={{0,9},{1,8},{2,11},{3,10},{4,13},{5,12},{6,15},{7,14},{8,1},{9,0},... | collective-permute-start | bytes 24584 | tf_op jit(solution)/shard_map/ppermute | solution.py:59

commit v8 on v5

--- a/solution.py
+++ b/solution.py
@@ -60,7 +60,7 @@
     return received
 
 
-def load_kernel(count, owner_hbm, emb_hbm, *rest):
+def load_kernel(towers, intra, pair, count, owner_hbm, emb_hbm, *rest):
     small, (picks_ref, emb_ref, slots_ref), copies = rest[:count], rest[count : count + 3], rest[count + 3 : -3]
     owner_ref, assign_ref, sems = rest[-3:]
     targets = (assign_ref, *copies)
@@ -69,10 +69,23 @@
     for load in loads:
         load.start()
     samples = emb_ref.shape[0]
+    per = samples // (towers * intra)
+    me, place = lax.axis_index("intra"), lax.axis_index("tower")
+    lane = lax.broadcasted_iota(jnp.int32, (per, samples), 1) - lax.broadcasted_iota(jnp.int32, (per, samples), 0)
+    chosen = []
+    for s in steps(intra, pair):
+        block = partner(me, s, intra, pair)
+        for t in range(towers):
+            owner = jnp.where(place == t, block, block ^ other_core(intra))
+            chosen.append(jnp.where(lane == (t * intra + owner) * per, 1.0, 0.0))
+    chosen = jnp.concatenate(chosen, axis=0).astype(jnp.bfloat16)
     loads[0].wait()
     owner = jnp.broadcast_to(owner_ref[...].reshape(1, samples), (samples, samples))
     picks = lax.broadcasted_iota(jnp.int32, (samples, samples), 0) == owner
-    picks_ref[...] = jnp.where(picks, 1.0, 0.0).astype(jnp.bfloat16)
+    picks = jnp.where(picks, 1.0, 0.0).astype(jnp.bfloat16)
+    picks_ref[...] = lax.dot_general(
+        chosen, picks, (((1,), (1,)), ((), ())), preferred_element_type=jnp.float32
+    ).astype(jnp.bfloat16)
     loads[2].wait()
     for slot in range(assign_ref.shape[1]):
         slots_ref[0, assign_ref[0, slot]] = slot
@@ -80,24 +93,16 @@
         load.wait()
 
 
-def gather_kernel(towers, intra, pair, picks_ref, *rest):
-    parts, outs, acc_ref = rest[:pair], rest[pair:-1], rest[-1]
-    samples, width = parts[0].shape
-    per = samples // (towers * intra)
-    held = width // EDIM
-    me, place = lax.axis_index("intra"), lax.axis_index("tower")
+def gather_kernel(pair, picks_ref, *rest):
+    parts, outs = rest[:pair], rest[pair:]
+    held = parts[0].shape[1] // EDIM
+    rows = outs[0].shape[1]
     for q, part in enumerate(parts):
-        acc_ref[:, q * width : (q + 1) * width] = lax.dot_general(
-            picks_ref[...], part[...], (((0,), (0,)), ((), ())), preferred_element_type=jnp.float32
-        )
-    for s, out in zip(steps(intra, pair), outs):
-        block = partner(me, s, intra, pair)
-        owners = [jnp.where(place == t, block, block ^ other_core(intra)) for t in range(towers)]
-        starts = [pl.multiple_of((t * intra + owners[t]) * per, per) for t in range(towers)]
-        for f in range(pair * held):
-            columns = slice(f * EDIM, (f + 1) * EDIM)
-            rows = [acc_ref[pl.ds(start, per), columns] for start in starts]
-            out[f] = jnp.concatenate(rows, axis=0).astype(out.dtype)
+        ordered = jnp.dot(picks_ref[...], part[...], preferred_element_type=jnp.float32)
+        for n, out in enumerate(outs):
+            for f in range(held):
+                block = ordered[n * rows : (n + 1) * rows, f * EDIM : (f + 1) * EDIM]
+                out[q * held + f] = block.astype(out.dtype)
 
 
 def gather_blocks(owner, embeddings, small, towers, intra, pair, ahead):
@@ -107,9 +112,9 @@
     if samples <= FEW_SAMPLES:
         given = [pltpu.with_memory_space_constraint(a, pltpu.HBM) for a in (owner, embeddings, *small)]
         picks, embeddings, *small = pl.pallas_call(
-            functools.partial(load_kernel, len(small)),
+            functools.partial(load_kernel, towers, intra, pair, len(small)),
             out_shape=[
-                pltpu.VMEM((samples, samples), jnp.bfloat16),
+                pltpu.VMEM((samples // pair, samples), jnp.bfloat16),
                 pltpu.VMEM(embeddings.shape, embeddings.dtype),
                 pltpu.SMEM(small[0].shape, small[0].dtype),
             ]
@@ -127,11 +132,10 @@
             name="load",
         )(*given)
         blocks = pl.pallas_call(
-            functools.partial(gather_kernel, towers, intra, pair),
+            functools.partial(gather_kernel, pair),
             out_shape=[pltpu.VMEM((held, rows, EDIM), embeddings.dtype)] * (intra // pair),
             in_specs=[pl.BlockSpec(memory_space=pltpu.VMEM)] * (1 + pair),
             out_specs=[pl.BlockSpec(memory_space=pltpu.VMEM)] * (intra // pair),
-            scratch_shapes=[pltpu.VMEM((samples, pair * width), jnp.float32)],
             compiler_params=pltpu.CompilerParams(vmem_limit_bytes=8 << 20),
             cost_estimate=pl.CostEstimate(flops=ahead, bytes_accessed=0, transcendentals=0),
             name="gather_rows",

time: 20.2 us -> 20.1 us (level)
  no operation moved by 1% of the time
where the time goes in v8:
time: 20.1 us; the launch traced here: 20 us
  starting transfers between devices  9.97 us (50%)
  waiting for transfers between devices  5.66 us (28%)
  Pallas kernels  4.29 us (21%)
    ppermute x3, starting transfers between devices, exchange_chips(): lax.ppermute(block, 'intra', [(i, partner(i, s, intra, pair)) for i in ra...  6.52 us
    ppermute x3, starting transfers between devices, exchange_groups(): lax.ppermute(block, ('tower', 'intra'), pairs)  2.99 us
    ppermute x3, waiting for transfers between devices, exchange_groups(): lax.ppermute(block, ('tower', 'intra'), pairs)  2.82 us
    ppermute x3, waiting for transfers between devices, exchange_chips(): lax.ppermute(block, 'intra', [(i, partner(i, s, intra, pair)) for i in ra...  2.5 us
    pallas_call x2, Pallas kernels, run_towers(): pl.pallas_call(functools.partial(early_kernel, intra, pair, [order[n] for...  1.4 us
    pallas_call x1, Pallas kernels, gather_blocks(): pl.pallas_call(functools.partial(load_kernel, towers, intra, pair, len(sm...  1.02 us
    pallas_call x1, Pallas kernels, interact(): pl.pallas_call(functools.partial(interact_kernel, towers), out_shape=jax....  0.94 us
    pallas_call x1, Pallas kernels, run_towers(): pl.pallas_call(functools.partial(tower_kernel, towers, intra, pair, [orde...  0.69 us
  transfers between devices with their start and end apart: 7, of which 6 were waited for; matrix products, arithmetic and copies ran while one was open for 0% of the time, Pallas kernels for 12%

profile of v8, /device:TPU:0, one launch (start us, length us, event | category | flops | bytes accessed | tf_op | source)
XLA Modules:
  0.0 20.0 jit_solution(6346680885789113323)
XLA Ops:
  0.0 0.5 %collective-permute-start = (bf16[256,512]{1,0:T(8,128)(2,1)}, bf16[256,512]{1,0:T(8,128)(2,1)S(1)}, u32[]{:S(2)}, u32[]{:S(2)}) collective-permute-start(bf16[256,512]{1,0:T(8,128)(2,1)} %emb_hbm.1), channel_id=1, source_target_pairs={{0,1},{1,0},{2,3},{3,2},{4,5},{5,4},{6,7},{7,6},{8,9},{9,8},{10,11... | collective-permute-start | bytes 786440 | tf_op jit(solution)/shard_map/ppermute | solution.py:111
  0.5 1.0 %load.1 = (bf16[128,256]{1,0:T(8,128)(2,1)S(1)}, bf16[256,512]{1,0:T(8,128)(2,1)S(1)}, s32[1,32]{1,0:T(1,128)S(4)}, f32[2,1024]{1,0:T(2,128)S(1)}, f32[2,256]{1,0:T(2,128)S(1)}, /*index=5*/bf16[16,128]{1,0:T(8,128)(2,1)S(1)}) custom-call(s32[256]{0:T(256)} %owner_hbm.1, bf16[256,512]{1,0:T(8,128)(2,1)} %emb_hbm.1, s32[1,32]{1,0:T(1,128)} %rest_0_.1, ...), custom_call_target="tpu_custom_call" | custom-call | tf_op jit(solution)/shard_map/load/pallas_call | solution.py:114
  1.5 0.3 %collective-permute-done.rest_1_ = bf16[256,512]{1,0:T(8,128)(2,1)S(1)} collective-permute-done((bf16[256,512]{1,0:T(8,128)(2,1)}, bf16[256,512]{1,0:T(8,128)(2,1)S(1)}, u32[]{:S(2)}, u32[]{:S(2)}) %collective-permute-start) | collective-permute-done | bytes 262176 | tf_op jit(solution)/shard_map/ppermute | solution.py:111
  1.8 0.0 copy-start
  1.8 0.2 %gather_rows.1 = (bf16[8,32,128]{2,1,0:T(8,128)(2,1)S(1)}, bf16[8,32,128]{2,1,0:T(8,128)(2,1)S(1)}, bf16[8,32,128]{2,1,0:T(8,128)(2,1)S(1)}, bf16[8,32,128]{2,1,0:T(8,128)(2,1)S(1)}) custom-call(bf16[128,256]{1,0:T(8,128)(2,1)S(1)} %get-tuple-element.23.picks_ref, bf16[256,512]{1,0:T(8,128)(2,1)S(1)} %get-tuple-element.24.rest_0_, ...), custom_call_target="tpu_custom_call" | custom-call | flops 47185920000 | tf_op jit(solution)/shard_map/gather_rows/pallas_call | solution.py:134
  2.1 2.7 %collective-permute-start.2 = (bf16[8,32,128]{2,1,0:T(8,128)(2,1)S(1)}, bf16[8,32,128]{2,1,0:T(8,128)(2,1)S(1)}, u32[]{:S(2)}, u32[]{:S(2)}) collective-permute-start(bf16[8,32,128]{2,1,0:T(8,128)(2,1)S(1)} %get-tuple-element.27), channel_id=1, source_target_pairs={{0,3},{1,2},{2,7},{3,6},{4,1},{5,0},{6,5},{7,4},{8,11},{9,10},{10,... | collective-permute-start | bytes 196616 | tf_op jit(solution)/shard_map/ppermute | solution.py:42
  4.8 2.5 %collective-permute-start.1 = (bf16[8,32,128]{2,1,0:T(8,128)(2,1)S(1)}, bf16[8,32,128]{2,1,0:T(8,128)(2,1)S(1)}, u32[]{:S(2)}, u32[]{:S(2)}) collective-permute-start(bf16[8,32,128]{2,1,0:T(8,128)(2,1)S(1)} %get-tuple-element.25), channel_id=1, source_target_pairs={{0,7},{1,6},{2,5},{3,4},{4,3},{5,2},{6,1},{7,0},{8,15},{9,14},{10,... | collective-permute-start | bytes 196616 | tf_op jit(solution)/shard_map/ppermute | solution.py:42
  7.3 1.3 %collective-permute-start.3 = (bf16[8,32,128]{2,1,0:T(8,128)(2,1)S(1)}, bf16[8,32,128]{2,1,0:T(8,128)(2,1)S(1)}, u32[]{:S(2)}, u32[]{:S(2)}) collective-permute-start(bf16[8,32,128]{2,1,0:T(8,128)(2,1)S(1)} %get-tuple-element.28), channel_id=1, source_target_pairs={{0,5},{1,4},{2,1},{3,0},{4,7},{5,6},{6,3},{7,2},{8,13},{9,12},{10,... | collective-permute-start | bytes 196616 | tf_op jit(solution)/shard_map/ppermute | solution.py:42
  8.6 0.0 collective-permute-done.2.rest_1_
  8.6 0.0 copy-done
  8.6 0.0 copy-start.1
  8.6 0.9 %towers_early.2.rest_1_ = f32[64,1024]{1,0:T(8,128)S(1)} custom-call(s32[1,32]{1,0:T(1,128)S(4)} %get-tuple-element.20.slots_ref, bf16[2,2048,1024]{2,1,0:T(8,128)(2,1)S(1)} %copy-done, bf16[8,32,128]{2,1,0:T(8,128)(2,1)S(1)} %get-tuple-element.26.rest_0_, bf16[8,32,128]{2,1,0:T(8,128)(2,1)S(1)} %collective-permute-done.2.rest_1_), custom_call_target="tpu_custom_call" | custom-call | flops 268435456 | tf_op jit(solution)/shard_map/towers_early/pallas_call | solution.py:239
  9.5 1.7 %collective-permute-done.1.rest_0_ = bf16[8,32,128]{2,1,0:T(8,128)(2,1)S(1)} collective-permute-done((bf16[8,32,128]{2,1,0:T(8,128)(2,1)S(1)}, bf16[8,32,128]{2,1,0:T(8,128)(2,1)S(1)}, u32[]{:S(2)}, u32[]{:S(2)}) %collective-permute-start.1) | collective-permute-done | bytes 65568 | tf_op jit(solution)/shard_map/ppermute | solution.py:42
  11.2 0.5 %towers_early.3.sums_ref = f32[64,1024]{1,0:T(8,128)S(1)} custom-call(s32[1,32]{1,0:T(1,128)S(4)} %get-tuple-element.20.slots_ref, bf16[2,2048,1024]{2,1,0:T(8,128)(2,1)S(1)} %copy-done, bf16[8,32,128]{2,1,0:T(8,128)(2,1)S(1)} %collective-permute-done.1.rest_0_, f32[64,1024]{1,0:T(8,128)S(1)} %towers_early.2.rest_1_), custom_call_target="tpu_custom_call" | custom-call | flops 268435456 | tf_op jit(solution)/shard_map/towers_early/pallas_call | solution.py:239
  11.7 0.8 %collective-permute-done.3.rest_0_ = bf16[8,32,128]{2,1,0:T(8,128)(2,1)S(1)} collective-permute-done((bf16[8,32,128]{2,1,0:T(8,128)(2,1)S(1)}, bf16[8,32,128]{2,1,0:T(8,128)(2,1)S(1)}, u32[]{:S(2)}, u32[]{:S(2)}) %collective-permute-start.3) | collective-permute-done | bytes 65568 | tf_op jit(solution)/shard_map/ppermute | solution.py:42
  12.5 0.0 copy-done.1
  12.5 0.7 %towers.1 = (bf16[32,128]{1,0:T(8,128)(2,1)S(1)}, bf16[32,128]{1,0:T(8,128)(2,1)S(1)}, bf16[32,128]{1,0:T(8,128)(2,1)S(1)}, bf16[32,128]{1,0:T(8,128)(2,1)S(1)}) custom-call(s32[1,32]{1,0:T(1,128)S(4)} %get-tuple-element.20.slots_ref, bf16[2,2048,1024]{2,1,0:T(8,128)(2,1)S(1)} %copy-done, f32[2,1024]{1,0:T(2,128)S(1)} %get-tuple-element.21.b1_ref, ...), custom_call_target="tpu_custom_call" | custom-call | tf_op jit(solution)/shard_map/towers/pallas_call | solution.py:252
  13.2 2.2 %collective-permute-start.4 = (bf16[32,128]{1,0:T(8,128)(2,1)S(1)}, bf16[32,128]{1,0:T(8,128)(2,1)S(1)}, u32[]{:S(2)}, u32[]{:S(2)}) collective-permute-start(bf16[32,128]{1,0:T(8,128)(2,1)S(1)} %get-tuple-element.29), channel_id=1, source_target_pairs={{0,25},{1,24},{2,27},{3,26},{4,29},{5,28},{6,31},{7,30},{8,17},{9,... | collective-permute-start | bytes 24584 | tf_op jit(solution)/shard_map/ppermute | solution.py:59
  15.4 0.5 %collective-permute-start.5 = (bf16[32,128]{1,0:T(8,128)(2,1)S(1)}, bf16[32,128]{1,0:T(8,128)(2,1)S(1)}, u32[]{:S(2)}, u32[]{:S(2)}) collective-permute-start(bf16[32,128]{1,0:T(8,128)(2,1)S(1)} %get-tuple-element.30), channel_id=1, source_target_pairs={{0,17},{1,16},{2,19},{3,18},{4,21},{5,20},{6,23},{7,22},{8,25},{9,... | collective-permute-start | bytes 24584 | tf_op jit(solution)/shard_map/ppermute | solution.py:59
  16.0 0.3 %collective-permute-start.6 = (bf16[32,128]{1,0:T(8,128)(2,1)S(1)}, bf16[32,128]{1,0:T(8,128)(2,1)S(1)}, u32[]{:S(2)}, u32[]{:S(2)}) collective-permute-start(bf16[32,128]{1,0:T(8,128)(2,1)S(1)} %get-tuple-element.31), channel_id=1, source_target_pairs={{0,9},{1,8},{2,11},{3,10},{4,13},{5,12},{6,15},{7,14},{8,1},{9,0},... | collective-permute-start | bytes 24584 | tf_op jit(solution)/shard_map/ppermute | solution.py:59
  16.2 1.0 %collective-permute-done.4.rest_0_ = bf16[32,128]{1,0:T(8,128)(2,1)S(1)} collective-permute-done((bf16[32,128]{1,0:T(8,128)(2,1)S(1)}, bf16[32,128]{1,0:T(8,128)(2,1)S(1)}, u32[]{:S(2)}, u32[]{:S(2)}) %collective-permute-start.4) | collective-permute-done | bytes 8224 | tf_op jit(solution)/shard_map/ppermute | solution.py:59
  17.3 1.3 %collective-permute-done.5.rest_1_ = bf16[32,128]{1,0:T(8,128)(2,1)S(1)} collective-permute-done((bf16[32,128]{1,0:T(8,128)(2,1)S(1)}, bf16[32,128]{1,0:T(8,128)(2,1)S(1)}, u32[]{:S(2)}, u32[]{:S(2)}) %collective-permute-start.5) | collective-permute-done | bytes 8224 | tf_op jit(solution)/shard_map/ppermute | solution.py:59
  18.5 0.5 %collective-permute-done.6.rest_2_ = bf16[32,128]{1,0:T(8,128)(2,1)S(1)} collective-permute-done((bf16[32,128]{1,0:T(8,128)(2,1)S(1)}, bf16[32,128]{1,0:T(8,128)(2,1)S(1)}, u32[]{:S(2)}, u32[]{:S(2)}) %collective-permute-start.6) | collective-permute-done | bytes 8224 | tf_op jit(solution)/shard_map/ppermute | solution.py:59
  19.0 0.9 %interact.1 = bf16[8,16,128]{2,1,0:T(8,128)(2,1)} custom-call(bf16[16,128]{1,0:T(8,128)(2,1)S(1)} %get-tuple-element.19.proj_ref, bf16[32,128]{1,0:T(8,128)(2,1)S(1)} %collective-permute-done.4.rest_0_, bf16[32,128]{1,0:T(8,128)(2,1)S(1)} %collective-permute-done.5.rest_1_, bf16[32,128]{1,0:T(8,128)(2,1)S(1)} %collective-permute-done.6.rest_2_, ...), custom_call_target="tpu_custom_call" | custom-call | tf_op jit(solution)/shard_map/interact/pallas_call | solution.py:310
Async XLA Ops:
  0.0 1.8 %collective-permute-start = (bf16[256,512]{1,0:T(8,128)(2,1)}, bf16[256,512]{1,0:T(8,128)(2,1)S(1)}, u32[]{:S(2)}, u32[]{:S(2)}) collective-permute-start(bf16[256,512]{1,0:T(8,128)(2,1)} %emb_hbm.1), channel_id=1, source_target_pairs={{0,1},{1,0},{2,3},{3,2},{4,5},{5,4},{6,7},{7,6},{8,9},{9,8},{10,11... | collective-permute-start | bytes 786440 | tf_op jit(solution)/shard_map/ppermute | solution.py:111
  1.8 6.8 %copy-start = (bf16[2,2048,1024]{2,1,0:T(8,128)(2,1)S(1)}, bf16[2,2048,1024]{2,1,0:T(8,128)(2,1)}, u32[]{:S(2)}) copy-start(bf16[2,2048,1024]{2,1,0:T(8,128)(2,1)} %w1_ref.5) | copy-start | bytes 25165828
  2.1 6.5 %collective-permute-start.2 = (bf16[8,32,128]{2,1,0:T(8,128)(2,1)S(1)}, bf16[8,32,128]{2,1,0:T(8,128)(2,1)S(1)}, u32[]{:S(2)}, u32[]{:S(2)}) collective-permute-start(bf16[8,32,128]{2,1,0:T(8,128)(2,1)S(1)} %get-tuple-element.27), channel_id=1, source_target_pairs={{0,3},{1,2},{2,7},{3,6},{4,1},{5,0},{6,5},{7,4},{8,11},{9,10},{10,... | collective-permute-start | bytes 196616 | tf_op jit(solution)/shard_map/ppermute | solution.py:42
  4.8 6.4 %collective-permute-start.1 = (bf16[8,32,128]{2,1,0:T(8,128)(2,1)S(1)}, bf16[8,32,128]{2,1,0:T(8,128)(2,1)S(1)}, u32[]{:S(2)}, u32[]{:S(2)}) collective-permute-start(bf16[8,32,128]{2,1,0:T(8,128)(2,1)S(1)} %get-tuple-element.25), channel_id=1, source_target_pairs={{0,7},{1,6},{2,5},{3,4},{4,3},{5,2},{6,1},{7,0},{8,15},{9,14},{10,... | collective-permute-start | bytes 196616 | tf_op jit(solution)/shard_map/ppermute | solution.py:42
  7.3 5.3 %collective-permute-start.3 = (bf16[8,32,128]{2,1,0:T(8,128)(2,1)S(1)}, bf16[8,32,128]{2,1,0:T(8,128)(2,1)S(1)}, u32[]{:S(2)}, u32[]{:S(2)}) collective-permute-start(bf16[8,32,128]{2,1,0:T(8,128)(2,1)S(1)} %get-tuple-element.28), channel_id=1, source_target_pairs={{0,5},{1,4},{2,1},{3,0},{4,7},{5,6},{6,3},{7,2},{8,13},{9,12},{10,... | collective-permute-start | bytes 196616 | tf_op jit(solution)/shard_map/ppermute | solution.py:42
  8.6 3.9 %copy-start.1 = (bf16[2,1024,256]{2,1,0:T(8,128)(2,1)S(1)}, bf16[2,1024,256]{2,1,0:T(8,128)(2,1)}, u32[]{:S(2)}) copy-start(bf16[2,1024,256]{2,1,0:T(8,128)(2,1)} %w2_ref.1) | copy-start | bytes 3145732
  13.2 4.0 %collective-permute-start.4 = (bf16[32,128]{1,0:T(8,128)(2,1)S(1)}, bf16[32,128]{1,0:T(8,128)(2,1)S(1)}, u32[]{:S(2)}, u32[]{:S(2)}) collective-permute-start(bf16[32,128]{1,0:T(8,128)(2,1)S(1)} %get-tuple-element.29), channel_id=1, source_target_pairs={{0,25},{1,24},{2,27},{3,26},{4,29},{5,28},{6,31},{7,30},{8,17},{9,... | collective-permute-start | bytes 24584 | tf_op jit(solution)/shard_map/ppermute | solution.py:59
  15.4 3.1 %collective-permute-start.5 = (bf16[32,128]{1,0:T(8,128)(2,1)S(1)}, bf16[32,128]{1,0:T(8,128)(2,1)S(1)}, u32[]{:S(2)}, u32[]{:S(2)}) collective-permute-start(bf16[32,128]{1,0:T(8,128)(2,1)S(1)} %get-tuple-element.30), channel_id=1, source_target_pairs={{0,17},{1,16},{2,19},{3,18},{4,21},{5,20},{6,23},{7,22},{8,25},{9,... | collective-permute-start | bytes 24584 | tf_op jit(solution)/shard_map/ppermute | solution.py:59
  16.0 3.1 %collective-permute-start.6 = (bf16[32,128]{1,0:T(8,128)(2,1)S(1)}, bf16[32,128]{1,0:T(8,128)(2,1)S(1)}, u32[]{:S(2)}, u32[]{:S(2)}) collective-permute-start(bf16[32,128]{1,0:T(8,128)(2,1)S(1)} %get-tuple-element.31), channel_id=1, source_target_pairs={{0,9},{1,8},{2,11},{3,10},{4,13},{5,12},{6,15},{7,14},{8,1},{9,0},... | collective-permute-start | bytes 24584 | tf_op jit(solution)/shard_map/ppermute | solution.py:59

commit v9 on v8

--- a/solution.py
+++ b/solution.py
@@ -19,22 +19,9 @@
     return (*range(1, intra // pair), 0)
 
 
-def ring_place(chip, chips):
-    place = chip
-    bits = (chips - 1).bit_length() if chips & (chips - 1) == 0 else 0
-    for n in range(1, bits):
-        place = place ^ (chip >> n)
-    return place
-
-
-def ring_chip(place, chips):
-    return place ^ (place >> 1) if chips & (chips - 1) == 0 else place
-
-
 def partner(me, step, intra, pair):
     chips = intra // pair
-    place = (ring_place(me // pair, chips) + step + chips) % chips
-    return ring_chip(place, chips) * pair + (me % pair + (pair - 1 if step else 0)) % pair
+    return (me // pair + step + chips) % chips * pair + (me % pair + (pair - 1 if step else 0)) % pair
 
 
 def exchange_chips(blocks, intra, pair):

time: 20.1 us -> 20.7 us (1.030)
  waiting for transfers between devices: 5.66 us -> 6.26 us
    ppermute x3, waiting for transfers between devices: 2.5 us -> 2.98 us  [exchange_chips(): lax.ppermute(block, 'intra', [(i, partner(i, s, intra, pair)) for i in ra...]
where the time goes in v9:
time: 20.7 us; the launch traced here: 20.5 us
  starting transfers between devices  9.94 us (48%)
  waiting for transfers between devices  6.26 us (30%)
  Pallas kernels  4.28 us (21%)
    ppermute x3, starting transfers between devices, exchange_chips(): lax.ppermute(block, 'intra', [(i, partner(i, s, intra, pair)) for i in ra...  6.41 us
    ppermute x3, starting transfers between devices, exchange_groups(): lax.ppermute(block, ('tower', 'intra'), pairs)  3.07 us
    ppermute x3, waiting for transfers between devices, exchange_chips(): lax.ppermute(block, 'intra', [(i, partner(i, s, intra, pair)) for i in ra...  2.98 us
    ppermute x3, waiting for transfers between devices, exchange_groups(): lax.ppermute(block, ('tower', 'intra'), pairs)  2.93 us
    pallas_call x2, Pallas kernels, run_towers(): pl.pallas_call(functools.partial(early_kernel, intra, pair, [order[n] for...  1.37 us
    pallas_call x1, Pallas kernels, gather_blocks(): pl.pallas_call(functools.partial(load_kernel, towers, intra, pair, len(sm...  1.02 us
    pallas_call x1, Pallas kernels, interact(): pl.pallas_call(functools.partial(interact_kernel, towers), out_shape=jax....  0.94 us
    pallas_call x1, Pallas kernels, run_towers(): pl.pallas_call(functools.partial(tower_kernel, towers, intra, pair, [orde...  0.72 us
  transfers between devices with their start and end apart: 7, of which 6 were waited for; matrix products, arithmetic and copies ran while one was open for 0% of the time, Pallas kernels for 12%

profile of v9, /device:TPU:0, one launch (start us, length us, event | category | flops | bytes accessed | tf_op | source)
XLA Modules:
  0.0 20.5 jit_solution(16931967239316965643)
XLA Ops:
  0.0 0.5 %collective-permute-start = (bf16[256,512]{1,0:T(8,128)(2,1)}, bf16[256,512]{1,0:T(8,128)(2,1)S(1)}, u32[]{:S(2)}, u32[]{:S(2)}) collective-permute-start(bf16[256,512]{1,0:T(8,128)(2,1)} %emb_hbm.1), channel_id=1, source_target_pairs={{0,1},{1,0},{2,3},{3,2},{4,5},{5,4},{6,7},{7,6},{8,9},{9,8},{10,11... | collective-permute-start | bytes 786440 | tf_op jit(solution)/shard_map/ppermute | solution.py:98
  0.5 1.0 %load.1 = (bf16[128,256]{1,0:T(8,128)(2,1)S(1)}, bf16[256,512]{1,0:T(8,128)(2,1)S(1)}, s32[1,32]{1,0:T(1,128)S(4)}, f32[2,1024]{1,0:T(2,128)S(1)}, f32[2,256]{1,0:T(2,128)S(1)}, /*index=5*/bf16[16,128]{1,0:T(8,128)(2,1)S(1)}) custom-call(s32[256]{0:T(256)} %owner_hbm.1, bf16[256,512]{1,0:T(8,128)(2,1)} %emb_hbm.1, s32[1,32]{1,0:T(1,128)} %rest_0_.1, ...), custom_call_target="tpu_custom_call" | custom-call | tf_op jit(solution)/shard_map/load/pallas_call | solution.py:101
  1.5 0.3 %collective-permute-done.rest_1_ = bf16[256,512]{1,0:T(8,128)(2,1)S(1)} collective-permute-done((bf16[256,512]{1,0:T(8,128)(2,1)}, bf16[256,512]{1,0:T(8,128)(2,1)S(1)}, u32[]{:S(2)}, u32[]{:S(2)}) %collective-permute-start) | collective-permute-done | bytes 262176 | tf_op jit(solution)/shard_map/ppermute | solution.py:98
  1.8 0.0 copy-start
  1.8 0.2 %gather_rows.1 = (bf16[8,32,128]{2,1,0:T(8,128)(2,1)S(1)}, bf16[8,32,128]{2,1,0:T(8,128)(2,1)S(1)}, bf16[8,32,128]{2,1,0:T(8,128)(2,1)S(1)}, bf16[8,32,128]{2,1,0:T(8,128)(2,1)S(1)}) custom-call(bf16[128,256]{1,0:T(8,128)(2,1)S(1)} %get-tuple-element.23.picks_ref, bf16[256,512]{1,0:T(8,128)(2,1)S(1)} %get-tuple-element.24.rest_0_, ...), custom_call_target="tpu_custom_call" | custom-call | flops 47185920000 | tf_op jit(solution)/shard_map/gather_rows/pallas_call | solution.py:121
  2.1 2.7 %collective-permute-start.2 = (bf16[8,32,128]{2,1,0:T(8,128)(2,1)S(1)}, bf16[8,32,128]{2,1,0:T(8,128)(2,1)S(1)}, u32[]{:S(2)}, u32[]{:S(2)}) collective-permute-start(bf16[8,32,128]{2,1,0:T(8,128)(2,1)S(1)} %get-tuple-element.27), channel_id=1, source_target_pairs={{0,3},{1,2},{2,5},{3,4},{4,7},{5,6},{6,1},{7,0},{8,11},{9,10},{10,... | collective-permute-start | bytes 196616 | tf_op jit(solution)/shard_map/ppermute | solution.py:29
  4.8 2.6 %collective-permute-start.1 = (bf16[8,32,128]{2,1,0:T(8,128)(2,1)S(1)}, bf16[8,32,128]{2,1,0:T(8,128)(2,1)S(1)}, u32[]{:S(2)}, u32[]{:S(2)}) collective-permute-start(bf16[8,32,128]{2,1,0:T(8,128)(2,1)S(1)} %get-tuple-element.25), channel_id=1, source_target_pairs={{0,5},{1,4},{2,7},{3,6},{4,1},{5,0},{6,3},{7,2},{8,13},{9,12},{10,... | collective-permute-start | bytes 196616 | tf_op jit(solution)/shard_map/ppermute | solution.py:29
  7.4 1.1 %collective-permute-start.3 = (bf16[8,32,128]{2,1,0:T(8,128)(2,1)S(1)}, bf16[8,32,128]{2,1,0:T(8,128)(2,1)S(1)}, u32[]{:S(2)}, u32[]{:S(2)}) collective-permute-start(bf16[8,32,128]{2,1,0:T(8,128)(2,1)S(1)} %get-tuple-element.28), channel_id=1, source_target_pairs={{0,7},{1,6},{2,1},{3,0},{4,3},{5,2},{6,5},{7,4},{8,15},{9,14},{10,... | collective-permute-start | bytes 196616 | tf_op jit(solution)/shard_map/ppermute | solution.py:29
  8.5 0.5 %collective-permute-done.2.rest_1_ = bf16[8,32,128]{2,1,0:T(8,128)(2,1)S(1)} collective-permute-done((bf16[8,32,128]{2,1,0:T(8,128)(2,1)S(1)}, bf16[8,32,128]{2,1,0:T(8,128)(2,1)S(1)}, u32[]{:S(2)}, u32[]{:S(2)}) %collective-permute-start.2) | collective-permute-done | bytes 65568 | tf_op jit(solution)/shard_map/ppermute | solution.py:29
  9.0 0.0 copy-done
  9.0 0.0 copy-start.1
  9.0 0.9 %towers_early.2.rest_1_ = f32[64,1024]{1,0:T(8,128)S(1)} custom-call(s32[1,32]{1,0:T(1,128)S(4)} %get-tuple-element.20.slots_ref, bf16[2,2048,1024]{2,1,0:T(8,128)(2,1)S(1)} %copy-done, bf16[8,32,128]{2,1,0:T(8,128)(2,1)S(1)} %get-tuple-element.26.rest_0_, bf16[8,32,128]{2,1,0:T(8,128)(2,1)S(1)} %collective-permute-done.2.rest_1_), custom_call_target="tpu_custom_call" | custom-call | flops 268435456 | tf_op jit(solution)/shard_map/towers_early/pallas_call | solution.py:226
  9.9 2.4 %collective-permute-done.1.rest_0_ = bf16[8,32,128]{2,1,0:T(8,128)(2,1)S(1)} collective-permute-done((bf16[8,32,128]{2,1,0:T(8,128)(2,1)S(1)}, bf16[8,32,128]{2,1,0:T(8,128)(2,1)S(1)}, u32[]{:S(2)}, u32[]{:S(2)}) %collective-permute-start.1) | collective-permute-done | bytes 65568 | tf_op jit(solution)/shard_map/ppermute | solution.py:29
  12.3 0.5 %towers_early.3.sums_ref = f32[64,1024]{1,0:T(8,128)S(1)} custom-call(s32[1,32]{1,0:T(1,128)S(4)} %get-tuple-element.20.slots_ref, bf16[2,2048,1024]{2,1,0:T(8,128)(2,1)S(1)} %copy-done, bf16[8,32,128]{2,1,0:T(8,128)(2,1)S(1)} %collective-permute-done.1.rest_0_, f32[64,1024]{1,0:T(8,128)S(1)} %towers_early.2.rest_1_), custom_call_target="tpu_custom_call" | custom-call | flops 268435456 | tf_op jit(solution)/shard_map/towers_early/pallas_call | solution.py:226
  12.8 0.0 collective-permute-done.3.rest_0_
  12.9 0.0 copy-done.1
  12.9 0.7 %towers.1 = (bf16[32,128]{1,0:T(8,128)(2,1)S(1)}, bf16[32,128]{1,0:T(8,128)(2,1)S(1)}, bf16[32,128]{1,0:T(8,128)(2,1)S(1)}, bf16[32,128]{1,0:T(8,128)(2,1)S(1)}) custom-call(s32[1,32]{1,0:T(1,128)S(4)} %get-tuple-element.20.slots_ref, bf16[2,2048,1024]{2,1,0:T(8,128)(2,1)S(1)} %copy-done, f32[2,1024]{1,0:T(2,128)S(1)} %get-tuple-element.21.b1_ref, ...), custom_call_target="tpu_custom_call" | custom-call | tf_op jit(solution)/shard_map/towers/pallas_call | solution.py:239
  13.6 2.3 %collective-permute-start.4 = (bf16[32,128]{1,0:T(8,128)(2,1)S(1)}, bf16[32,128]{1,0:T(8,128)(2,1)S(1)}, u32[]{:S(2)}, u32[]{:S(2)}) collective-permute-start(bf16[32,128]{1,0:T(8,128)(2,1)S(1)} %get-tuple-element.29), channel_id=1, source_target_pairs={{0,25},{1,24},{2,27},{3,26},{4,29},{5,28},{6,31},{7,30},{8,17},{9,... | collective-permute-start | bytes 24584 | tf_op jit(solution)/shard_map/ppermute | solution.py:46
  15.9 0.6 %collective-permute-start.5 = (bf16[32,128]{1,0:T(8,128)(2,1)S(1)}, bf16[32,128]{1,0:T(8,128)(2,1)S(1)}, u32[]{:S(2)}, u32[]{:S(2)}) collective-permute-start(bf16[32,128]{1,0:T(8,128)(2,1)S(1)} %get-tuple-element.30), channel_id=1, source_target_pairs={{0,17},{1,16},{2,19},{3,18},{4,21},{5,20},{6,23},{7,22},{8,25},{9,... | collective-permute-start | bytes 24584 | tf_op jit(solution)/shard_map/ppermute | solution.py:46
  16.5 0.1 collective-permute-start.6
  16.7 1.0 %collective-permute-done.4.rest_0_ = bf16[32,128]{1,0:T(8,128)(2,1)S(1)} collective-permute-done((bf16[32,128]{1,0:T(8,128)(2,1)S(1)}, bf16[32,128]{1,0:T(8,128)(2,1)S(1)}, u32[]{:S(2)}, u32[]{:S(2)}) %collective-permute-start.4) | collective-permute-done | bytes 8224 | tf_op jit(solution)/shard_map/ppermute | solution.py:46
  17.6 1.4 %collective-permute-done.5.rest_1_ = bf16[32,128]{1,0:T(8,128)(2,1)S(1)} collective-permute-done((bf16[32,128]{1,0:T(8,128)(2,1)S(1)}, bf16[32,128]{1,0:T(8,128)(2,1)S(1)}, u32[]{:S(2)}, u32[]{:S(2)}) %collective-permute-start.5) | collective-permute-done | bytes 8224 | tf_op jit(solution)/shard_map/ppermute | solution.py:46
  19.0 0.6 %collective-permute-done.6.rest_2_ = bf16[32,128]{1,0:T(8,128)(2,1)S(1)} collective-permute-done((bf16[32,128]{1,0:T(8,128)(2,1)S(1)}, bf16[32,128]{1,0:T(8,128)(2,1)S(1)}, u32[]{:S(2)}, u32[]{:S(2)}) %collective-permute-start.6) | collective-permute-done | bytes 8224 | tf_op jit(solution)/shard_map/ppermute | solution.py:46
  19.6 0.9 %interact.1 = bf16[8,16,128]{2,1,0:T(8,128)(2,1)} custom-call(bf16[16,128]{1,0:T(8,128)(2,1)S(1)} %get-tuple-element.19.proj_ref, bf16[32,128]{1,0:T(8,128)(2,1)S(1)} %collective-permute-done.4.rest_0_, bf16[32,128]{1,0:T(8,128)(2,1)S(1)} %collective-permute-done.5.rest_1_, bf16[32,128]{1,0:T(8,128)(2,1)S(1)} %collective-permute-done.6.rest_2_, ...), custom_call_target="tpu_custom_call" | custom-call | tf_op jit(solution)/shard_map/interact/pallas_call | solution.py:297
Async XLA Ops:
  0.0 1.8 %collective-permute-start = (bf16[256,512]{1,0:T(8,128)(2,1)}, bf16[256,512]{1,0:T(8,128)(2,1)S(1)}, u32[]{:S(2)}, u32[]{:S(2)}) collective-permute-start(bf16[256,512]{1,0:T(8,128)(2,1)} %emb_hbm.1), channel_id=1, source_target_pairs={{0,1},{1,0},{2,3},{3,2},{4,5},{5,4},{6,7},{7,6},{8,9},{9,8},{10,11... | collective-permute-start | bytes 786440 | tf_op jit(solution)/shard_map/ppermute | solution.py:98
  1.8 7.2 %copy-start = (bf16[2,2048,1024]{2,1,0:T(8,128)(2,1)S(1)}, bf16[2,2048,1024]{2,1,0:T(8,128)(2,1)}, u32[]{:S(2)}) copy-start(bf16[2,2048,1024]{2,1,0:T(8,128)(2,1)} %w1_ref.5) | copy-start | bytes 25165828
  2.1 7.0 %collective-permute-start.2 = (bf16[8,32,128]{2,1,0:T(8,128)(2,1)S(1)}, bf16[8,32,128]{2,1,0:T(8,128)(2,1)S(1)}, u32[]{:S(2)}, u32[]{:S(2)}) collective-permute-start(bf16[8,32,128]{2,1,0:T(8,128)(2,1)S(1)} %get-tuple-element.27), channel_id=1, source_target_pairs={{0,3},{1,2},{2,5},{3,4},{4,7},{5,6},{6,1},{7,0},{8,11},{9,10},{10,... | collective-permute-start | bytes 196616 | tf_op jit(solution)/shard_map/ppermute | solution.py:29
  4.8 7.5 %collective-permute-start.1 = (bf16[8,32,128]{2,1,0:T(8,128)(2,1)S(1)}, bf16[8,32,128]{2,1,0:T(8,128)(2,1)S(1)}, u32[]{:S(2)}, u32[]{:S(2)}) collective-permute-start(bf16[8,32,128]{2,1,0:T(8,128)(2,1)S(1)} %get-tuple-element.25), channel_id=1, source_target_pairs={{0,5},{1,4},{2,7},{3,6},{4,1},{5,0},{6,3},{7,2},{8,13},{9,12},{10,... | collective-permute-start | bytes 196616 | tf_op jit(solution)/shard_map/ppermute | solution.py:29
  7.4 5.5 %collective-permute-start.3 = (bf16[8,32,128]{2,1,0:T(8,128)(2,1)S(1)}, bf16[8,32,128]{2,1,0:T(8,128)(2,1)S(1)}, u32[]{:S(2)}, u32[]{:S(2)}) collective-permute-start(bf16[8,32,128]{2,1,0:T(8,128)(2,1)S(1)} %get-tuple-element.28), channel_id=1, source_target_pairs={{0,7},{1,6},{2,1},{3,0},{4,3},{5,2},{6,5},{7,4},{8,15},{9,14},{10,... | collective-permute-start | bytes 196616 | tf_op jit(solution)/shard_map/ppermute | solution.py:29
  9.0 3.8 %copy-start.1 = (bf16[2,1024,256]{2,1,0:T(8,128)(2,1)S(1)}, bf16[2,1024,256]{2,1,0:T(8,128)(2,1)}, u32[]{:S(2)}) copy-start(bf16[2,1024,256]{2,1,0:T(8,128)(2,1)} %w2_ref.1) | copy-start | bytes 3145732
  13.6 4.0 %collective-permute-start.4 = (bf16[32,128]{1,0:T(8,128)(2,1)S(1)}, bf16[32,128]{1,0:T(8,128)(2,1)S(1)}, u32[]{:S(2)}, u32[]{:S(2)}) collective-permute-start(bf16[32,128]{1,0:T(8,128)(2,1)S(1)} %get-tuple-element.29), channel_id=1, source_target_pairs={{0,25},{1,24},{2,27},{3,26},{4,29},{5,28},{6,31},{7,30},{8,17},{9,... | collective-permute-start | bytes 24584 | tf_op jit(solution)/shard_map/ppermute | solution.py:46
  15.9 3.1 %collective-permute-start.5 = (bf16[32,128]{1,0:T(8,128)(2,1)S(1)}, bf16[32,128]{1,0:T(8,128)(2,1)S(1)}, u32[]{:S(2)}, u32[]{:S(2)}) collective-permute-start(bf16[32,128]{1,0:T(8,128)(2,1)S(1)} %get-tuple-element.30), channel_id=1, source_target_pairs={{0,17},{1,16},{2,19},{3,18},{4,21},{5,20},{6,23},{7,22},{8,25},{9,... | collective-permute-start | bytes 24584 | tf_op jit(solution)/shard_map/ppermute | solution.py:46
  16.5 3.1 %collective-permute-start.6 = (bf16[32,128]{1,0:T(8,128)(2,1)S(1)}, bf16[32,128]{1,0:T(8,128)(2,1)S(1)}, u32[]{:S(2)}, u32[]{:S(2)}) collective-permute-start(bf16[32,128]{1,0:T(8,128)(2,1)S(1)} %get-tuple-element.31), channel_id=1, source_target_pairs={{0,9},{1,8},{2,11},{3,10},{4,13},{5,12},{6,15},{7,14},{8,1},{9,0},... | collective-permute-start | bytes 24584 | tf_op jit(solution)/shard_map/ppermute | solution.py:46

commit v10 on v8

--- a/solution.py
+++ b/solution.py
@@ -34,7 +34,7 @@
 def partner(me, step, intra, pair):
     chips = intra // pair
     place = (ring_place(me // pair, chips) + step + chips) % chips
-    return ring_chip(place, chips) * pair + (me % pair + (pair - 1 if step else 0)) % pair
+    return ring_chip(place, chips) * pair + me % pair
 
 
 def exchange_chips(blocks, intra, pair):

time: 20.1 us -> 20.1 us (level)
  waiting for transfers between devices: 5.66 us -> 5.2 us
  starting transfers between devices: 9.97 us -> 10.4 us
    ppermute x3, waiting for transfers between devices: 2.5 us -> 1.91 us  [exchange_chips(): lax.ppermute(block, 'intra', [(i, partner(i, s, intra, pair)) for i in ra...]
    ppermute x3, starting transfers between devices: 6.52 us -> 7.05 us  [exchange_chips(): lax.ppermute(block, 'intra', [(i, partner(i, s, intra, pair)) for i in ra...]
  transfers between devices with their start and end apart: 7 -> 7, of which waited for: 6 -> 5; matrix products, arithmetic and copies ran while one was open for 0% -> 0% of each run, Pallas kernels for 12% -> 12%
where the time goes in v10:
time: 20.1 us; the launch traced here: 20 us
  starting transfers between devices  10.4 us (52%)
  waiting for transfers between devices  5.2 us (26%)
  Pallas kernels  4.31 us (21%)
    ppermute x3, starting transfers between devices, exchange_chips(): lax.ppermute(block, 'intra', [(i, partner(i, s, intra, pair)) for i in ra...  7.05 us
    ppermute x3, waiting for transfers between devices, exchange_groups(): lax.ppermute(block, ('tower', 'intra'), pairs)  2.95 us
    ppermute x3, starting transfers between devices, exchange_groups(): lax.ppermute(block, ('tower', 'intra'), pairs)  2.89 us
    ppermute x3, waiting for transfers between devices, exchange_chips(): lax.ppermute(block, 'intra', [(i, partner(i, s, intra, pair)) for i in ra...  1.91 us
    pallas_call x2, Pallas kernels, run_towers(): pl.pallas_call(functools.partial(early_kernel, intra, pair, [order[n] for...  1.39 us
    pallas_call x1, Pallas kernels, gather_blocks(): pl.pallas_call(functools.partial(load_kernel, towers, intra, pair, len(sm...  1.02 us
    pallas_call x1, Pallas kernels, interact(): pl.pallas_call(functools.partial(interact_kernel, towers), out_shape=jax....  0.94 us
    pallas_call x1, Pallas kernels, run_towers(): pl.pallas_call(functools.partial(tower_kernel, towers, intra, pair, [orde...  0.72 us
  transfers between devices with their start and end apart: 7, of which 5 were waited for; matrix products, arithmetic and copies ran while one was open for 0% of the time, Pallas kernels for 12%

profile of v10, /device:TPU:0, one launch (start us, length us, event | category | flops | bytes accessed | tf_op | source)
XLA Modules:
  0.0 20.0 jit_solution(15350105244134924662)
XLA Ops:
  0.0 0.5 %collective-permute-start = (bf16[256,512]{1,0:T(8,128)(2,1)}, bf16[256,512]{1,0:T(8,128)(2,1)S(1)}, u32[]{:S(2)}, u32[]{:S(2)}) collective-permute-start(bf16[256,512]{1,0:T(8,128)(2,1)} %emb_hbm.1), channel_id=1, source_target_pairs={{0,1},{1,0},{2,3},{3,2},{4,5},{5,4},{6,7},{7,6},{8,9},{9,8},{10,11... | collective-permute-start | bytes 786440 | tf_op jit(solution)/shard_map/ppermute | solution.py:111
  0.5 1.0 %load.1 = (bf16[128,256]{1,0:T(8,128)(2,1)S(1)}, bf16[256,512]{1,0:T(8,128)(2,1)S(1)}, s32[1,32]{1,0:T(1,128)S(4)}, f32[2,1024]{1,0:T(2,128)S(1)}, f32[2,256]{1,0:T(2,128)S(1)}, /*index=5*/bf16[16,128]{1,0:T(8,128)(2,1)S(1)}) custom-call(s32[256]{0:T(256)} %owner_hbm.1, bf16[256,512]{1,0:T(8,128)(2,1)} %emb_hbm.1, s32[1,32]{1,0:T(1,128)} %rest_0_.1, ...), custom_call_target="tpu_custom_call" | custom-call | tf_op jit(solution)/shard_map/load/pallas_call | solution.py:114
  1.5 0.3 %collective-permute-done.rest_1_ = bf16[256,512]{1,0:T(8,128)(2,1)S(1)} collective-permute-done((bf16[256,512]{1,0:T(8,128)(2,1)}, bf16[256,512]{1,0:T(8,128)(2,1)S(1)}, u32[]{:S(2)}, u32[]{:S(2)}) %collective-permute-start) | collective-permute-done | bytes 262176 | tf_op jit(solution)/shard_map/ppermute | solution.py:111
  1.8 0.0 copy-start
  1.8 0.2 %gather_rows.1 = (bf16[8,32,128]{2,1,0:T(8,128)(2,1)S(1)}, bf16[8,32,128]{2,1,0:T(8,128)(2,1)S(1)}, bf16[8,32,128]{2,1,0:T(8,128)(2,1)S(1)}, bf16[8,32,128]{2,1,0:T(8,128)(2,1)S(1)}) custom-call(bf16[128,256]{1,0:T(8,128)(2,1)S(1)} %get-tuple-element.23.picks_ref, bf16[256,512]{1,0:T(8,128)(2,1)S(1)} %get-tuple-element.24.rest_0_, ...), custom_call_target="tpu_custom_call" | custom-call | flops 47185920000 | tf_op jit(solution)/shard_map/gather_rows/pallas_call | solution.py:134
  2.1 3.0 %collective-permute-start.2 = (bf16[8,32,128]{2,1,0:T(8,128)(2,1)S(1)}, bf16[8,32,128]{2,1,0:T(8,128)(2,1)S(1)}, u32[]{:S(2)}, u32[]{:S(2)}) collective-permute-start(bf16[8,32,128]{2,1,0:T(8,128)(2,1)S(1)} %get-tuple-element.27), channel_id=1, source_target_pairs={{0,2},{1,3},{2,6},{3,7},{4,0},{5,1},{6,4},{7,5},{8,10},{9,11},{10,... | collective-permute-start | bytes 196616 | tf_op jit(solution)/shard_map/ppermute | solution.py:42
  5.1 2.5 %collective-permute-start.1 = (bf16[8,32,128]{2,1,0:T(8,128)(2,1)S(1)}, bf16[8,32,128]{2,1,0:T(8,128)(2,1)S(1)}, u32[]{:S(2)}, u32[]{:S(2)}) collective-permute-start(bf16[8,32,128]{2,1,0:T(8,128)(2,1)S(1)} %get-tuple-element.25), channel_id=1, source_target_pairs={{0,6},{1,7},{2,4},{3,5},{4,2},{5,3},{6,0},{7,1},{8,14},{9,15},{10,... | collective-permute-start | bytes 196616 | tf_op jit(solution)/shard_map/ppermute | solution.py:42
  7.5 1.6 %collective-permute-start.3 = (bf16[8,32,128]{2,1,0:T(8,128)(2,1)S(1)}, bf16[8,32,128]{2,1,0:T(8,128)(2,1)S(1)}, u32[]{:S(2)}, u32[]{:S(2)}) collective-permute-start(bf16[8,32,128]{2,1,0:T(8,128)(2,1)S(1)} %get-tuple-element.28), channel_id=1, source_target_pairs={{0,4},{1,5},{2,0},{3,1},{4,6},{5,7},{6,2},{7,3},{8,12},{9,13},{10,... | collective-permute-start | bytes 196616 | tf_op jit(solution)/shard_map/ppermute | solution.py:42
  9.1 0.0 collective-permute-done.2.rest_1_
  9.1 0.0 copy-done
  9.1 0.0 copy-start.1
  9.1 0.9 %towers_early.2.rest_1_ = f32[64,1024]{1,0:T(8,128)S(1)} custom-call(s32[1,32]{1,0:T(1,128)S(4)} %get-tuple-element.20.slots_ref, bf16[2,2048,1024]{2,1,0:T(8,128)(2,1)S(1)} %copy-done, bf16[8,32,128]{2,1,0:T(8,128)(2,1)S(1)} %get-tuple-element.26.rest_0_, bf16[8,32,128]{2,1,0:T(8,128)(2,1)S(1)} %collective-permute-done.2.rest_1_), custom_call_target="tpu_custom_call" | custom-call | flops 268435456 | tf_op jit(solution)/shard_map/towers_early/pallas_call | solution.py:239
  10.0 1.9 %collective-permute-done.1.rest_0_ = bf16[8,32,128]{2,1,0:T(8,128)(2,1)S(1)} collective-permute-done((bf16[8,32,128]{2,1,0:T(8,128)(2,1)S(1)}, bf16[8,32,128]{2,1,0:T(8,128)(2,1)S(1)}, u32[]{:S(2)}, u32[]{:S(2)}) %collective-permute-start.1) | collective-permute-done | bytes 65568 | tf_op jit(solution)/shard_map/ppermute | solution.py:42
  11.9 0.5 %towers_early.3.sums_ref = f32[64,1024]{1,0:T(8,128)S(1)} custom-call(s32[1,32]{1,0:T(1,128)S(4)} %get-tuple-element.20.slots_ref, bf16[2,2048,1024]{2,1,0:T(8,128)(2,1)S(1)} %copy-done, bf16[8,32,128]{2,1,0:T(8,128)(2,1)S(1)} %collective-permute-done.1.rest_0_, f32[64,1024]{1,0:T(8,128)S(1)} %towers_early.2.rest_1_), custom_call_target="tpu_custom_call" | custom-call | flops 268435456 | tf_op jit(solution)/shard_map/towers_early/pallas_call | solution.py:239
  12.4 0.0 collective-permute-done.3.rest_0_
  12.5 0.0 copy-done.1
  12.5 0.7 %towers.1 = (bf16[32,128]{1,0:T(8,128)(2,1)S(1)}, bf16[32,128]{1,0:T(8,128)(2,1)S(1)}, bf16[32,128]{1,0:T(8,128)(2,1)S(1)}, bf16[32,128]{1,0:T(8,128)(2,1)S(1)}) custom-call(s32[1,32]{1,0:T(1,128)S(4)} %get-tuple-element.20.slots_ref, bf16[2,2048,1024]{2,1,0:T(8,128)(2,1)S(1)} %copy-done, f32[2,1024]{1,0:T(2,128)S(1)} %get-tuple-element.21.b1_ref, ...), custom_call_target="tpu_custom_call" | custom-call | tf_op jit(solution)/shard_map/towers/pallas_call | solution.py:252
  13.2 1.1 %collective-permute-start.4 = (bf16[32,128]{1,0:T(8,128)(2,1)S(1)}, bf16[32,128]{1,0:T(8,128)(2,1)S(1)}, u32[]{:S(2)}, u32[]{:S(2)}) collective-permute-start(bf16[32,128]{1,0:T(8,128)(2,1)S(1)} %get-tuple-element.29), channel_id=1, source_target_pairs={{0,25},{1,24},{2,27},{3,26},{4,29},{5,28},{6,31},{7,30},{8,17},{9,... | collective-permute-start | bytes 24584 | tf_op jit(solution)/shard_map/ppermute | solution.py:59
  14.3 1.7 %collective-permute-start.5 = (bf16[32,128]{1,0:T(8,128)(2,1)S(1)}, bf16[32,128]{1,0:T(8,128)(2,1)S(1)}, u32[]{:S(2)}, u32[]{:S(2)}) collective-permute-start(bf16[32,128]{1,0:T(8,128)(2,1)S(1)} %get-tuple-element.30), channel_id=1, source_target_pairs={{0,17},{1,16},{2,19},{3,18},{4,21},{5,20},{6,23},{7,22},{8,25},{9,... | collective-permute-start | bytes 24584 | tf_op jit(solution)/shard_map/ppermute | solution.py:59
  15.9 0.1 collective-permute-start.6
  16.1 1.2 %collective-permute-done.4.rest_0_ = bf16[32,128]{1,0:T(8,128)(2,1)S(1)} collective-permute-done((bf16[32,128]{1,0:T(8,128)(2,1)S(1)}, bf16[32,128]{1,0:T(8,128)(2,1)S(1)}, u32[]{:S(2)}, u32[]{:S(2)}) %collective-permute-start.4) | collective-permute-done | bytes 8224 | tf_op jit(solution)/shard_map/ppermute | solution.py:59
  17.2 0.2 %collective-permute-done.5.rest_1_ = bf16[32,128]{1,0:T(8,128)(2,1)S(1)} collective-permute-done((bf16[32,128]{1,0:T(8,128)(2,1)S(1)}, bf16[32,128]{1,0:T(8,128)(2,1)S(1)}, u32[]{:S(2)}, u32[]{:S(2)}) %collective-permute-start.5) | collective-permute-done | bytes 8224 | tf_op jit(solution)/shard_map/ppermute | solution.py:59
  17.4 1.6 %collective-permute-done.6.rest_2_ = bf16[32,128]{1,0:T(8,128)(2,1)S(1)} collective-permute-done((bf16[32,128]{1,0:T(8,128)(2,1)S(1)}, bf16[32,128]{1,0:T(8,128)(2,1)S(1)}, u32[]{:S(2)}, u32[]{:S(2)}) %collective-permute-start.6) | collective-permute-done | bytes 8224 | tf_op jit(solution)/shard_map/ppermute | solution.py:59
  19.0 0.9 %interact.1 = bf16[8,16,128]{2,1,0:T(8,128)(2,1)} custom-call(bf16[16,128]{1,0:T(8,128)(2,1)S(1)} %get-tuple-element.19.proj_ref, bf16[32,128]{1,0:T(8,128)(2,1)S(1)} %collective-permute-done.4.rest_0_, bf16[32,128]{1,0:T(8,128)(2,1)S(1)} %collective-permute-done.5.rest_1_, bf16[32,128]{1,0:T(8,128)(2,1)S(1)} %collective-permute-done.6.rest_2_, ...), custom_call_target="tpu_custom_call" | custom-call | tf_op jit(solution)/shard_map/interact/pallas_call | solution.py:310
Async XLA Ops:
  0.0 1.8 %collective-permute-start = (bf16[256,512]{1,0:T(8,128)(2,1)}, bf16[256,512]{1,0:T(8,128)(2,1)S(1)}, u32[]{:S(2)}, u32[]{:S(2)}) collective-permute-start(bf16[256,512]{1,0:T(8,128)(2,1)} %emb_hbm.1), channel_id=1, source_target_pairs={{0,1},{1,0},{2,3},{3,2},{4,5},{5,4},{6,7},{7,6},{8,9},{9,8},{10,11... | collective-permute-start | bytes 786440 | tf_op jit(solution)/shard_map/ppermute | solution.py:111
  1.8 7.3 %copy-start = (bf16[2,2048,1024]{2,1,0:T(8,128)(2,1)S(1)}, bf16[2,2048,1024]{2,1,0:T(8,128)(2,1)}, u32[]{:S(2)}) copy-start(bf16[2,2048,1024]{2,1,0:T(8,128)(2,1)} %w1_ref.5) | copy-start | bytes 25165828
  2.1 7.1 %collective-permute-start.2 = (bf16[8,32,128]{2,1,0:T(8,128)(2,1)S(1)}, bf16[8,32,128]{2,1,0:T(8,128)(2,1)S(1)}, u32[]{:S(2)}, u32[]{:S(2)}) collective-permute-start(bf16[8,32,128]{2,1,0:T(8,128)(2,1)S(1)} %get-tuple-element.27), channel_id=1, source_target_pairs={{0,2},{1,3},{2,6},{3,7},{4,0},{5,1},{6,4},{7,5},{8,10},{9,11},{10,... | collective-permute-start | bytes 196616 | tf_op jit(solution)/shard_map/ppermute | solution.py:42
  5.1 6.9 %collective-permute-start.1 = (bf16[8,32,128]{2,1,0:T(8,128)(2,1)S(1)}, bf16[8,32,128]{2,1,0:T(8,128)(2,1)S(1)}, u32[]{:S(2)}, u32[]{:S(2)}) collective-permute-start(bf16[8,32,128]{2,1,0:T(8,128)(2,1)S(1)} %get-tuple-element.25), channel_id=1, source_target_pairs={{0,6},{1,7},{2,4},{3,5},{4,2},{5,3},{6,0},{7,1},{8,14},{9,15},{10,... | collective-permute-start | bytes 196616 | tf_op jit(solution)/shard_map/ppermute | solution.py:42
  7.5 4.9 %collective-permute-start.3 = (bf16[8,32,128]{2,1,0:T(8,128)(2,1)S(1)}, bf16[8,32,128]{2,1,0:T(8,128)(2,1)S(1)}, u32[]{:S(2)}, u32[]{:S(2)}) collective-permute-start(bf16[8,32,128]{2,1,0:T(8,128)(2,1)S(1)} %get-tuple-element.28), channel_id=1, source_target_pairs={{0,4},{1,5},{2,0},{3,1},{4,6},{5,7},{6,2},{7,3},{8,12},{9,13},{10,... | collective-permute-start | bytes 196616 | tf_op jit(solution)/shard_map/ppermute | solution.py:42
  9.1 3.3 %copy-start.1 = (bf16[2,1024,256]{2,1,0:T(8,128)(2,1)S(1)}, bf16[2,1024,256]{2,1,0:T(8,128)(2,1)}, u32[]{:S(2)}) copy-start(bf16[2,1024,256]{2,1,0:T(8,128)(2,1)} %w2_ref.1) | copy-start | bytes 3145732
  13.2 4.0 %collective-permute-start.4 = (bf16[32,128]{1,0:T(8,128)(2,1)S(1)}, bf16[32,128]{1,0:T(8,128)(2,1)S(1)}, u32[]{:S(2)}, u32[]{:S(2)}) collective-permute-start(bf16[32,128]{1,0:T(8,128)(2,1)S(1)} %get-tuple-element.29), channel_id=1, source_target_pairs={{0,25},{1,24},{2,27},{3,26},{4,29},{5,28},{6,31},{7,30},{8,17},{9,... | collective-permute-start | bytes 24584 | tf_op jit(solution)/shard_map/ppermute | solution.py:59
  14.3 3.2 %collective-permute-start.5 = (bf16[32,128]{1,0:T(8,128)(2,1)S(1)}, bf16[32,128]{1,0:T(8,128)(2,1)S(1)}, u32[]{:S(2)}, u32[]{:S(2)}) collective-permute-start(bf16[32,128]{1,0:T(8,128)(2,1)S(1)} %get-tuple-element.30), channel_id=1, source_target_pairs={{0,17},{1,16},{2,19},{3,18},{4,21},{5,20},{6,23},{7,22},{8,25},{9,... | collective-permute-start | bytes 24584 | tf_op jit(solution)/shard_map/ppermute | solution.py:59
  15.9 3.1 %collective-permute-start.6 = (bf16[32,128]{1,0:T(8,128)(2,1)S(1)}, bf16[32,128]{1,0:T(8,128)(2,1)S(1)}, u32[]{:S(2)}, u32[]{:S(2)}) collective-permute-start(bf16[32,128]{1,0:T(8,128)(2,1)S(1)} %get-tuple-element.31), channel_id=1, source_target_pairs={{0,9},{1,8},{2,11},{3,10},{4,13},{5,12},{6,15},{7,14},{8,1},{9,0},... | collective-permute-start | bytes 24584 | tf_op jit(solution)/shard_map/ppermute | solution.py:59

commit v11 on v8

--- a/solution.py
+++ b/solution.py
@@ -12,7 +12,7 @@
 
 
 def offsets(size):
-    return range(size - 1, -1, -1)
+    return sorted(range(size), key=lambda o: (-o.bit_count(), o))
 
 
 def steps(intra, pair):

time: 20.1 us -> 20.2 us (level)
  no operation moved by 1% of the time
where the time goes in v11:
time: 20.2 us; the launch traced here: 20 us
  starting transfers between devices  9.97 us (49%)
  waiting for transfers between devices  5.69 us (28%)
  Pallas kernels  4.29 us (21%)
    ppermute x3, starting transfers between devices, exchange_chips(): lax.ppermute(block, 'intra', [(i, partner(i, s, intra, pair)) for i in ra...  6.52 us
    ppermute x3, starting transfers between devices, exchange_groups(): lax.ppermute(block, ('tower', 'intra'), pairs)  2.99 us
    ppermute x3, waiting for transfers between devices, exchange_groups(): lax.ppermute(block, ('tower', 'intra'), pairs)  2.85 us
    ppermute x3, waiting for transfers between devices, exchange_chips(): lax.ppermute(block, 'intra', [(i, partner(i, s, intra, pair)) for i in ra...  2.5 us
    pallas_call x2, Pallas kernels, run_towers(): pl.pallas_call(functools.partial(early_kernel, intra, pair, [order[n] for...  1.4 us
    pallas_call x1, Pallas kernels, gather_blocks(): pl.pallas_call(functools.partial(load_kernel, towers, intra, pair, len(sm...  1.02 us
    pallas_call x1, Pallas kernels, interact(): pl.pallas_call(functools.partial(interact_kernel, towers), out_shape=jax....  0.94 us
    pallas_call x1, Pallas kernels, run_towers(): pl.pallas_call(functools.partial(tower_kernel, towers, intra, pair, [orde...  0.69 us
  transfers between devices with their start and end apart: 7, of which 6 were waited for; matrix products, arithmetic and copies ran while one was open for 0% of the time, Pallas kernels for 12%

profile of v11, /device:TPU:0, one launch (start us, length us, event | category | flops | bytes accessed | tf_op | source)
XLA Modules:
  0.0 20.0 jit_solution(3489416191795893356)
XLA Ops:
  0.0 0.5 %collective-permute-start = (bf16[256,512]{1,0:T(8,128)(2,1)}, bf16[256,512]{1,0:T(8,128)(2,1)S(1)}, u32[]{:S(2)}, u32[]{:S(2)}) collective-permute-start(bf16[256,512]{1,0:T(8,128)(2,1)} %emb_hbm.1), channel_id=1, source_target_pairs={{0,1},{1,0},{2,3},{3,2},{4,5},{5,4},{6,7},{7,6},{8,9},{9,8},{10,11... | collective-permute-start | bytes 786440 | tf_op jit(solution)/shard_map/ppermute | solution.py:111
  0.5 1.0 %load.1 = (bf16[128,256]{1,0:T(8,128)(2,1)S(1)}, bf16[256,512]{1,0:T(8,128)(2,1)S(1)}, s32[1,32]{1,0:T(1,128)S(4)}, f32[2,1024]{1,0:T(2,128)S(1)}, f32[2,256]{1,0:T(2,128)S(1)}, /*index=5*/bf16[16,128]{1,0:T(8,128)(2,1)S(1)}) custom-call(s32[256]{0:T(256)} %owner_hbm.1, bf16[256,512]{1,0:T(8,128)(2,1)} %emb_hbm.1, s32[1,32]{1,0:T(1,128)} %rest_0_.1, ...), custom_call_target="tpu_custom_call" | custom-call | tf_op jit(solution)/shard_map/load/pallas_call | solution.py:114
  1.5 0.3 %collective-permute-done.rest_1_ = bf16[256,512]{1,0:T(8,128)(2,1)S(1)} collective-permute-done((bf16[256,512]{1,0:T(8,128)(2,1)}, bf16[256,512]{1,0:T(8,128)(2,1)S(1)}, u32[]{:S(2)}, u32[]{:S(2)}) %collective-permute-start) | collective-permute-done | bytes 262176 | tf_op jit(solution)/shard_map/ppermute | solution.py:111
  1.8 0.0 copy-start
  1.8 0.2 %gather_rows.1 = (bf16[8,32,128]{2,1,0:T(8,128)(2,1)S(1)}, bf16[8,32,128]{2,1,0:T(8,128)(2,1)S(1)}, bf16[8,32,128]{2,1,0:T(8,128)(2,1)S(1)}, bf16[8,32,128]{2,1,0:T(8,128)(2,1)S(1)}) custom-call(bf16[128,256]{1,0:T(8,128)(2,1)S(1)} %get-tuple-element.23.picks_ref, bf16[256,512]{1,0:T(8,128)(2,1)S(1)} %get-tuple-element.24.rest_0_, ...), custom_call_target="tpu_custom_call" | custom-call | flops 47185920000 | tf_op jit(solution)/shard_map/gather_rows/pallas_call | solution.py:134
  2.1 2.7 %collective-permute-start.2 = (bf16[8,32,128]{2,1,0:T(8,128)(2,1)S(1)}, bf16[8,32,128]{2,1,0:T(8,128)(2,1)S(1)}, u32[]{:S(2)}, u32[]{:S(2)}) collective-permute-start(bf16[8,32,128]{2,1,0:T(8,128)(2,1)S(1)} %get-tuple-element.27), channel_id=1, source_target_pairs={{0,3},{1,2},{2,7},{3,6},{4,1},{5,0},{6,5},{7,4},{8,11},{9,10},{10,... | collective-permute-start | bytes 196616 | tf_op jit(solution)/shard_map/ppermute | solution.py:42
  4.8 2.5 %collective-permute-start.1 = (bf16[8,32,128]{2,1,0:T(8,128)(2,1)S(1)}, bf16[8,32,128]{2,1,0:T(8,128)(2,1)S(1)}, u32[]{:S(2)}, u32[]{:S(2)}) collective-permute-start(bf16[8,32,128]{2,1,0:T(8,128)(2,1)S(1)} %get-tuple-element.25), channel_id=1, source_target_pairs={{0,7},{1,6},{2,5},{3,4},{4,3},{5,2},{6,1},{7,0},{8,15},{9,14},{10,... | collective-permute-start | bytes 196616 | tf_op jit(solution)/shard_map/ppermute | solution.py:42
  7.3 1.3 %collective-permute-start.3 = (bf16[8,32,128]{2,1,0:T(8,128)(2,1)S(1)}, bf16[8,32,128]{2,1,0:T(8,128)(2,1)S(1)}, u32[]{:S(2)}, u32[]{:S(2)}) collective-permute-start(bf16[8,32,128]{2,1,0:T(8,128)(2,1)S(1)} %get-tuple-element.28), channel_id=1, source_target_pairs={{0,5},{1,4},{2,1},{3,0},{4,7},{5,6},{6,3},{7,2},{8,13},{9,12},{10,... | collective-permute-start | bytes 196616 | tf_op jit(solution)/shard_map/ppermute | solution.py:42
  8.6 0.0 collective-permute-done.2.rest_1_
  8.6 0.0 copy-done
  8.6 0.0 copy-start.1
  8.6 0.9 %towers_early.2.rest_1_ = f32[64,1024]{1,0:T(8,128)S(1)} custom-call(s32[1,32]{1,0:T(1,128)S(4)} %get-tuple-element.20.slots_ref, bf16[2,2048,1024]{2,1,0:T(8,128)(2,1)S(1)} %copy-done, bf16[8,32,128]{2,1,0:T(8,128)(2,1)S(1)} %get-tuple-element.26.rest_0_, bf16[8,32,128]{2,1,0:T(8,128)(2,1)S(1)} %collective-permute-done.2.rest_1_), custom_call_target="tpu_custom_call" | custom-call | flops 268435456 | tf_op jit(solution)/shard_map/towers_early/pallas_call | solution.py:239
  9.5 1.7 %collective-permute-done.1.rest_0_ = bf16[8,32,128]{2,1,0:T(8,128)(2,1)S(1)} collective-permute-done((bf16[8,32,128]{2,1,0:T(8,128)(2,1)S(1)}, bf16[8,32,128]{2,1,0:T(8,128)(2,1)S(1)}, u32[]{:S(2)}, u32[]{:S(2)}) %collective-permute-start.1) | collective-permute-done | bytes 65568 | tf_op jit(solution)/shard_map/ppermute | solution.py:42
  11.2 0.5 %towers_early.3.sums_ref = f32[64,1024]{1,0:T(8,128)S(1)} custom-call(s32[1,32]{1,0:T(1,128)S(4)} %get-tuple-element.20.slots_ref, bf16[2,2048,1024]{2,1,0:T(8,128)(2,1)S(1)} %copy-done, bf16[8,32,128]{2,1,0:T(8,128)(2,1)S(1)} %collective-permute-done.1.rest_0_, f32[64,1024]{1,0:T(8,128)S(1)} %towers_early.2.rest_1_), custom_call_target="tpu_custom_call" | custom-call | flops 268435456 | tf_op jit(solution)/shard_map/towers_early/pallas_call | solution.py:239
  11.7 0.8 %collective-permute-done.3.rest_0_ = bf16[8,32,128]{2,1,0:T(8,128)(2,1)S(1)} collective-permute-done((bf16[8,32,128]{2,1,0:T(8,128)(2,1)S(1)}, bf16[8,32,128]{2,1,0:T(8,128)(2,1)S(1)}, u32[]{:S(2)}, u32[]{:S(2)}) %collective-permute-start.3) | collective-permute-done | bytes 65568 | tf_op jit(solution)/shard_map/ppermute | solution.py:42
  12.5 0.0 copy-done.1
  12.5 0.7 %towers.1 = (bf16[32,128]{1,0:T(8,128)(2,1)S(1)}, bf16[32,128]{1,0:T(8,128)(2,1)S(1)}, bf16[32,128]{1,0:T(8,128)(2,1)S(1)}, bf16[32,128]{1,0:T(8,128)(2,1)S(1)}) custom-call(s32[1,32]{1,0:T(1,128)S(4)} %get-tuple-element.20.slots_ref, bf16[2,2048,1024]{2,1,0:T(8,128)(2,1)S(1)} %copy-done, f32[2,1024]{1,0:T(2,128)S(1)} %get-tuple-element.21.b1_ref, ...), custom_call_target="tpu_custom_call" | custom-call | tf_op jit(solution)/shard_map/towers/pallas_call | solution.py:252
  13.2 2.2 %collective-permute-start.4 = (bf16[32,128]{1,0:T(8,128)(2,1)S(1)}, bf16[32,128]{1,0:T(8,128)(2,1)S(1)}, u32[]{:S(2)}, u32[]{:S(2)}) collective-permute-start(bf16[32,128]{1,0:T(8,128)(2,1)S(1)} %get-tuple-element.29), channel_id=1, source_target_pairs={{0,25},{1,24},{2,27},{3,26},{4,29},{5,28},{6,31},{7,30},{8,17},{9,... | collective-permute-start | bytes 24584 | tf_op jit(solution)/shard_map/ppermute | solution.py:59
  15.4 0.5 %collective-permute-start.5 = (bf16[32,128]{1,0:T(8,128)(2,1)S(1)}, bf16[32,128]{1,0:T(8,128)(2,1)S(1)}, u32[]{:S(2)}, u32[]{:S(2)}) collective-permute-start(bf16[32,128]{1,0:T(8,128)(2,1)S(1)} %get-tuple-element.30), channel_id=1, source_target_pairs={{0,9},{1,8},{2,11},{3,10},{4,13},{5,12},{6,15},{7,14},{8,1},{9,0},... | collective-permute-start | bytes 24584 | tf_op jit(solution)/shard_map/ppermute | solution.py:59
  16.0 0.2 %collective-permute-start.6 = (bf16[32,128]{1,0:T(8,128)(2,1)S(1)}, bf16[32,128]{1,0:T(8,128)(2,1)S(1)}, u32[]{:S(2)}, u32[]{:S(2)}) collective-permute-start(bf16[32,128]{1,0:T(8,128)(2,1)S(1)} %get-tuple-element.31), channel_id=1, source_target_pairs={{0,17},{1,16},{2,19},{3,18},{4,21},{5,20},{6,23},{7,22},{8,25},{9,... | collective-permute-start | bytes 24584 | tf_op jit(solution)/shard_map/ppermute | solution.py:59
  16.2 1.0 %collective-permute-done.4.rest_0_ = bf16[32,128]{1,0:T(8,128)(2,1)S(1)} collective-permute-done((bf16[32,128]{1,0:T(8,128)(2,1)S(1)}, bf16[32,128]{1,0:T(8,128)(2,1)S(1)}, u32[]{:S(2)}, u32[]{:S(2)}) %collective-permute-start.4) | collective-permute-done | bytes 8224 | tf_op jit(solution)/shard_map/ppermute | solution.py:59
  17.3 1.3 %collective-permute-done.5.rest_1_ = bf16[32,128]{1,0:T(8,128)(2,1)S(1)} collective-permute-done((bf16[32,128]{1,0:T(8,128)(2,1)S(1)}, bf16[32,128]{1,0:T(8,128)(2,1)S(1)}, u32[]{:S(2)}, u32[]{:S(2)}) %collective-permute-start.5) | collective-permute-done | bytes 8224 | tf_op jit(solution)/shard_map/ppermute | solution.py:59
  18.5 0.5 %collective-permute-done.6.rest_2_ = bf16[32,128]{1,0:T(8,128)(2,1)S(1)} collective-permute-done((bf16[32,128]{1,0:T(8,128)(2,1)S(1)}, bf16[32,128]{1,0:T(8,128)(2,1)S(1)}, u32[]{:S(2)}, u32[]{:S(2)}) %collective-permute-start.6) | collective-permute-done | bytes 8224 | tf_op jit(solution)/shard_map/ppermute | solution.py:59
  19.1 0.9 %interact.1 = bf16[8,16,128]{2,1,0:T(8,128)(2,1)} custom-call(bf16[16,128]{1,0:T(8,128)(2,1)S(1)} %get-tuple-element.19.proj_ref, bf16[32,128]{1,0:T(8,128)(2,1)S(1)} %collective-permute-done.4.rest_0_, bf16[32,128]{1,0:T(8,128)(2,1)S(1)} %collective-permute-done.5.rest_1_, bf16[32,128]{1,0:T(8,128)(2,1)S(1)} %collective-permute-done.6.rest_2_, ...), custom_call_target="tpu_custom_call" | custom-call | tf_op jit(solution)/shard_map/interact/pallas_call | solution.py:310
Async XLA Ops:
  0.0 1.8 %collective-permute-start = (bf16[256,512]{1,0:T(8,128)(2,1)}, bf16[256,512]{1,0:T(8,128)(2,1)S(1)}, u32[]{:S(2)}, u32[]{:S(2)}) collective-permute-start(bf16[256,512]{1,0:T(8,128)(2,1)} %emb_hbm.1), channel_id=1, source_target_pairs={{0,1},{1,0},{2,3},{3,2},{4,5},{5,4},{6,7},{7,6},{8,9},{9,8},{10,11... | collective-permute-start | bytes 786440 | tf_op jit(solution)/shard_map/ppermute | solution.py:111
  1.8 6.8 %copy-start = (bf16[2,2048,1024]{2,1,0:T(8,128)(2,1)S(1)}, bf16[2,2048,1024]{2,1,0:T(8,128)(2,1)}, u32[]{:S(2)}) copy-start(bf16[2,2048,1024]{2,1,0:T(8,128)(2,1)} %w1_ref.5) | copy-start | bytes 25165828
  2.1 6.5 %collective-permute-start.2 = (bf16[8,32,128]{2,1,0:T(8,128)(2,1)S(1)}, bf16[8,32,128]{2,1,0:T(8,128)(2,1)S(1)}, u32[]{:S(2)}, u32[]{:S(2)}) collective-permute-start(bf16[8,32,128]{2,1,0:T(8,128)(2,1)S(1)} %get-tuple-element.27), channel_id=1, source_target_pairs={{0,3},{1,2},{2,7},{3,6},{4,1},{5,0},{6,5},{7,4},{8,11},{9,10},{10,... | collective-permute-start | bytes 196616 | tf_op jit(solution)/shard_map/ppermute | solution.py:42
  4.8 6.4 %collective-permute-start.1 = (bf16[8,32,128]{2,1,0:T(8,128)(2,1)S(1)}, bf16[8,32,128]{2,1,0:T(8,128)(2,1)S(1)}, u32[]{:S(2)}, u32[]{:S(2)}) collective-permute-start(bf16[8,32,128]{2,1,0:T(8,128)(2,1)S(1)} %get-tuple-element.25), channel_id=1, source_target_pairs={{0,7},{1,6},{2,5},{3,4},{4,3},{5,2},{6,1},{7,0},{8,15},{9,14},{10,... | collective-permute-start | bytes 196616 | tf_op jit(solution)/shard_map/ppermute | solution.py:42
  7.3 5.3 %collective-permute-start.3 = (bf16[8,32,128]{2,1,0:T(8,128)(2,1)S(1)}, bf16[8,32,128]{2,1,0:T(8,128)(2,1)S(1)}, u32[]{:S(2)}, u32[]{:S(2)}) collective-permute-start(bf16[8,32,128]{2,1,0:T(8,128)(2,1)S(1)} %get-tuple-element.28), channel_id=1, source_target_pairs={{0,5},{1,4},{2,1},{3,0},{4,7},{5,6},{6,3},{7,2},{8,13},{9,12},{10,... | collective-permute-start | bytes 196616 | tf_op jit(solution)/shard_map/ppermute | solution.py:42
  8.6 3.9 %copy-start.1 = (bf16[2,1024,256]{2,1,0:T(8,128)(2,1)S(1)}, bf16[2,1024,256]{2,1,0:T(8,128)(2,1)}, u32[]{:S(2)}) copy-start(bf16[2,1024,256]{2,1,0:T(8,128)(2,1)} %w2_ref.1) | copy-start | bytes 3145732
  13.2 4.0 %collective-permute-start.4 = (bf16[32,128]{1,0:T(8,128)(2,1)S(1)}, bf16[32,128]{1,0:T(8,128)(2,1)S(1)}, u32[]{:S(2)}, u32[]{:S(2)}) collective-permute-start(bf16[32,128]{1,0:T(8,128)(2,1)S(1)} %get-tuple-element.29), channel_id=1, source_target_pairs={{0,25},{1,24},{2,27},{3,26},{4,29},{5,28},{6,31},{7,30},{8,17},{9,... | collective-permute-start | bytes 24584 | tf_op jit(solution)/shard_map/ppermute | solution.py:59
  15.4 3.1 %collective-permute-start.5 = (bf16[32,128]{1,0:T(8,128)(2,1)S(1)}, bf16[32,128]{1,0:T(8,128)(2,1)S(1)}, u32[]{:S(2)}, u32[]{:S(2)}) collective-permute-start(bf16[32,128]{1,0:T(8,128)(2,1)S(1)} %get-tuple-element.30), channel_id=1, source_target_pairs={{0,9},{1,8},{2,11},{3,10},{4,13},{5,12},{6,15},{7,14},{8,1},{9,0},... | collective-permute-start | bytes 24584 | tf_op jit(solution)/shard_map/ppermute | solution.py:59
  16.0 3.1 %collective-permute-start.6 = (bf16[32,128]{1,0:T(8,128)(2,1)S(1)}, bf16[32,128]{1,0:T(8,128)(2,1)S(1)}, u32[]{:S(2)}, u32[]{:S(2)}) collective-permute-start(bf16[32,128]{1,0:T(8,128)(2,1)S(1)} %get-tuple-element.31), channel_id=1, source_target_pairs={{0,17},{1,16},{2,19},{3,18},{4,21},{5,20},{6,23},{7,22},{8,25},{9,... | collective-permute-start | bytes 24584 | tf_op jit(solution)/shard_map/ppermute | solution.py:59

commit v12 on v8

--- a/solution.py
+++ b/solution.py
@@ -223,7 +223,7 @@
     order = steps(intra, pair)
     remote = len(blocks) - 1
     cuts = (0, max(remote // 2, min(remote - 1, 1)), remote - 1)
-    stages = [[-1, *range(*cuts[:2])], [*range(*cuts[1:])]]
+    stages = [[-1], [*range(*cuts[:2])], [*range(*cuts[1:])]]
     late = [remote - 1] if remote else []
     held, rows, _ = blocks[0].shape
     count, depth, hid = w1.shape

time: 20.1 us -> 20.1 us (level)
    pallas_call x2 -> x3, Pallas kernels: 1.4 us -> 1.51 us  [run_towers(): pl.pallas_call(functools.partial(early_kernel, intra, pair, [order[n] for...]
  transfers between devices with their start and end apart: 7 -> 7, of which waited for: 6 -> 6; matrix products, arithmetic and copies ran while one was open for 0% -> 0% of each run, Pallas kernels for 12% -> 13%
where the time goes in v12:
time: 20.1 us; the launch traced here: 20 us
  starting transfers between devices  9.97 us (50%)
  waiting for transfers between devices  5.53 us (28%)
  Pallas kernels  4.4 us (22%)
    ppermute x3, starting transfers between devices, exchange_chips(): lax.ppermute(block, 'intra', [(i, partner(i, s, intra, pair)) for i in ra...  6.52 us
    ppermute x3, starting transfers between devices, exchange_groups(): lax.ppermute(block, ('tower', 'intra'), pairs)  2.99 us
    ppermute x3, waiting for transfers between devices, exchange_groups(): lax.ppermute(block, ('tower', 'intra'), pairs)  2.82 us
    ppermute x3, waiting for transfers between devices, exchange_chips(): lax.ppermute(block, 'intra', [(i, partner(i, s, intra, pair)) for i in ra...  2.37 us
    pallas_call x3, Pallas kernels, run_towers(): pl.pallas_call(functools.partial(early_kernel, intra, pair, [order[n] for...  1.51 us
    pallas_call x1, Pallas kernels, gather_blocks(): pl.pallas_call(functools.partial(load_kernel, towers, intra, pair, len(sm...  1.02 us
    pallas_call x1, Pallas kernels, interact(): pl.pallas_call(functools.partial(interact_kernel, towers), out_shape=jax....  0.94 us
    pallas_call x1, Pallas kernels, run_towers(): pl.pallas_call(functools.partial(tower_kernel, towers, intra, pair, [orde...  0.69 us
  transfers between devices with their start and end apart: 7, of which 6 were waited for; matrix products, arithmetic and copies ran while one was open for 0% of the time, Pallas kernels for 13%

profile of v12, /device:TPU:0, one launch (start us, length us, event | category | flops | bytes accessed | tf_op | source)
XLA Modules:
  0.0 20.0 jit_solution(13115488226659638125)
XLA Ops:
  0.0 0.5 %collective-permute-start = (bf16[256,512]{1,0:T(8,128)(2,1)}, bf16[256,512]{1,0:T(8,128)(2,1)S(1)}, u32[]{:S(2)}, u32[]{:S(2)}) collective-permute-start(bf16[256,512]{1,0:T(8,128)(2,1)} %emb_hbm.1), channel_id=1, source_target_pairs={{0,1},{1,0},{2,3},{3,2},{4,5},{5,4},{6,7},{7,6},{8,9},{9,8},{10,11... | collective-permute-start | bytes 786440 | tf_op jit(solution)/shard_map/ppermute | solution.py:111
  0.5 1.0 %load.1 = (bf16[128,256]{1,0:T(8,128)(2,1)S(1)}, bf16[256,512]{1,0:T(8,128)(2,1)S(1)}, s32[1,32]{1,0:T(1,128)S(4)}, f32[2,1024]{1,0:T(2,128)S(1)}, f32[2,256]{1,0:T(2,128)S(1)}, /*index=5*/bf16[16,128]{1,0:T(8,128)(2,1)S(1)}) custom-call(s32[256]{0:T(256)} %owner_hbm.1, bf16[256,512]{1,0:T(8,128)(2,1)} %emb_hbm.1, s32[1,32]{1,0:T(1,128)} %rest_0_.1, ...), custom_call_target="tpu_custom_call" | custom-call | tf_op jit(solution)/shard_map/load/pallas_call | solution.py:114
  1.5 0.3 %collective-permute-done.rest_1_ = bf16[256,512]{1,0:T(8,128)(2,1)S(1)} collective-permute-done((bf16[256,512]{1,0:T(8,128)(2,1)}, bf16[256,512]{1,0:T(8,128)(2,1)S(1)}, u32[]{:S(2)}, u32[]{:S(2)}) %collective-permute-start) | collective-permute-done | bytes 262176 | tf_op jit(solution)/shard_map/ppermute | solution.py:111
  1.8 0.2 %gather_rows.1 = (bf16[8,32,128]{2,1,0:T(8,128)(2,1)S(1)}, bf16[8,32,128]{2,1,0:T(8,128)(2,1)S(1)}, bf16[8,32,128]{2,1,0:T(8,128)(2,1)S(1)}, bf16[8,32,128]{2,1,0:T(8,128)(2,1)S(1)}) custom-call(bf16[128,256]{1,0:T(8,128)(2,1)S(1)} %get-tuple-element.23.picks_ref, bf16[256,512]{1,0:T(8,128)(2,1)S(1)} %get-tuple-element.24.rest_0_, ...), custom_call_target="tpu_custom_call" | custom-call | flops 47185920000 | tf_op jit(solution)/shard_map/gather_rows/pallas_call | solution.py:134
  2.1 2.7 %collective-permute-start.2 = (bf16[8,32,128]{2,1,0:T(8,128)(2,1)S(1)}, bf16[8,32,128]{2,1,0:T(8,128)(2,1)S(1)}, u32[]{:S(2)}, u32[]{:S(2)}) collective-permute-start(bf16[8,32,128]{2,1,0:T(8,128)(2,1)S(1)} %get-tuple-element.26), channel_id=1, source_target_pairs={{0,3},{1,2},{2,7},{3,6},{4,1},{5,0},{6,5},{7,4},{8,11},{9,10},{10,... | collective-permute-start | bytes 196616 | tf_op jit(solution)/shard_map/ppermute | solution.py:42
  4.8 2.5 %collective-permute-start.1 = (bf16[8,32,128]{2,1,0:T(8,128)(2,1)S(1)}, bf16[8,32,128]{2,1,0:T(8,128)(2,1)S(1)}, u32[]{:S(2)}, u32[]{:S(2)}) collective-permute-start(bf16[8,32,128]{2,1,0:T(8,128)(2,1)S(1)} %get-tuple-element.25), channel_id=1, source_target_pairs={{0,7},{1,6},{2,5},{3,4},{4,3},{5,2},{6,1},{7,0},{8,15},{9,14},{10,... | collective-permute-start | bytes 196616 | tf_op jit(solution)/shard_map/ppermute | solution.py:42
  7.3 1.3 %collective-permute-start.3 = (bf16[8,32,128]{2,1,0:T(8,128)(2,1)S(1)}, bf16[8,32,128]{2,1,0:T(8,128)(2,1)S(1)}, u32[]{:S(2)}, u32[]{:S(2)}) collective-permute-start(bf16[8,32,128]{2,1,0:T(8,128)(2,1)S(1)} %get-tuple-element.28), channel_id=1, source_target_pairs={{0,5},{1,4},{2,1},{3,0},{4,7},{5,6},{6,3},{7,2},{8,13},{9,12},{10,... | collective-permute-start | bytes 196616 | tf_op jit(solution)/shard_map/ppermute | solution.py:42
  8.6 0.0 copy-done
  8.6 0.5 %towers_early.3.rest_1_ = f32[64,1024]{1,0:T(8,128)S(1)} custom-call(s32[1,32]{1,0:T(1,128)S(4)} %get-tuple-element.20.slots_ref, bf16[2,2048,1024]{2,1,0:T(8,128)(2,1)S(1)} %copy-done, bf16[8,32,128]{2,1,0:T(8,128)(2,1)S(1)} %get-tuple-element.27.rest_0_), custom_call_target="tpu_custom_call" | custom-call | flops 268435456 | tf_op jit(solution)/shard_map/towers_early/pallas_call | solution.py:239
  9.1 0.0 copy-start.1
  9.1 0.0 collective-permute-done.2.rest_0_
  9.1 0.5 %towers_early.4.rest_1_ = f32[64,1024]{1,0:T(8,128)S(1)} custom-call(s32[1,32]{1,0:T(1,128)S(4)} %get-tuple-element.20.slots_ref, bf16[2,2048,1024]{2,1,0:T(8,128)(2,1)S(1)} %copy-done, bf16[8,32,128]{2,1,0:T(8,128)(2,1)S(1)} %collective-permute-done.2.rest_0_, f32[64,1024]{1,0:T(8,128)S(1)} %towers_early.3.rest_1_), custom_call_target="tpu_custom_call" | custom-call | flops 268435456 | tf_op jit(solution)/shard_map/towers_early/pallas_call | solution.py:239
  9.7 1.5 %collective-permute-done.1.rest_0_ = bf16[8,32,128]{2,1,0:T(8,128)(2,1)S(1)} collective-permute-done((bf16[8,32,128]{2,1,0:T(8,128)(2,1)S(1)}, bf16[8,32,128]{2,1,0:T(8,128)(2,1)S(1)}, u32[]{:S(2)}, u32[]{:S(2)}) %collective-permute-start.1) | collective-permute-done | bytes 65568 | tf_op jit(solution)/shard_map/ppermute | solution.py:42
  11.2 0.5 %towers_early.5.sums_ref = f32[64,1024]{1,0:T(8,128)S(1)} custom-call(s32[1,32]{1,0:T(1,128)S(4)} %get-tuple-element.20.slots_ref, bf16[2,2048,1024]{2,1,0:T(8,128)(2,1)S(1)} %copy-done, bf16[8,32,128]{2,1,0:T(8,128)(2,1)S(1)} %collective-permute-done.1.rest_0_, f32[64,1024]{1,0:T(8,128)S(1)} %towers_early.4.rest_1_), custom_call_target="tpu_custom_call" | custom-call | flops 268435456 | tf_op jit(solution)/shard_map/towers_early/pallas_call | solution.py:239
  11.7 0.8 %collective-permute-done.3.rest_0_ = bf16[8,32,128]{2,1,0:T(8,128)(2,1)S(1)} collective-permute-done((bf16[8,32,128]{2,1,0:T(8,128)(2,1)S(1)}, bf16[8,32,128]{2,1,0:T(8,128)(2,1)S(1)}, u32[]{:S(2)}, u32[]{:S(2)}) %collective-permute-start.3) | collective-permute-done | bytes 65568 | tf_op jit(solution)/shard_map/ppermute | solution.py:42
  12.5 0.0 copy-done.1
  12.5 0.7 %towers.1 = (bf16[32,128]{1,0:T(8,128)(2,1)S(1)}, bf16[32,128]{1,0:T(8,128)(2,1)S(1)}, bf16[32,128]{1,0:T(8,128)(2,1)S(1)}, bf16[32,128]{1,0:T(8,128)(2,1)S(1)}) custom-call(s32[1,32]{1,0:T(1,128)S(4)} %get-tuple-element.20.slots_ref, bf16[2,2048,1024]{2,1,0:T(8,128)(2,1)S(1)} %copy-done, f32[2,1024]{1,0:T(2,128)S(1)} %get-tuple-element.21.b1_ref, ...), custom_call_target="tpu_custom_call" | custom-call | tf_op jit(solution)/shard_map/towers/pallas_call | solution.py:252
  13.2 2.2 %collective-permute-start.4 = (bf16[32,128]{1,0:T(8,128)(2,1)S(1)}, bf16[32,128]{1,0:T(8,128)(2,1)S(1)}, u32[]{:S(2)}, u32[]{:S(2)}) collective-permute-start(bf16[32,128]{1,0:T(8,128)(2,1)S(1)} %get-tuple-element.29), channel_id=1, source_target_pairs={{0,25},{1,24},{2,27},{3,26},{4,29},{5,28},{6,31},{7,30},{8,17},{9,... | collective-permute-start | bytes 24584 | tf_op jit(solution)/shard_map/ppermute | solution.py:59
  15.4 0.5 %collective-permute-start.5 = (bf16[32,128]{1,0:T(8,128)(2,1)S(1)}, bf16[32,128]{1,0:T(8,128)(2,1)S(1)}, u32[]{:S(2)}, u32[]{:S(2)}) collective-permute-start(bf16[32,128]{1,0:T(8,128)(2,1)S(1)} %get-tuple-element.30), channel_id=1, source_target_pairs={{0,17},{1,16},{2,19},{3,18},{4,21},{5,20},{6,23},{7,22},{8,25},{9,... | collective-permute-start | bytes 24584 | tf_op jit(solution)/shard_map/ppermute | solution.py:59
  15.9 0.3 %collective-permute-start.6 = (bf16[32,128]{1,0:T(8,128)(2,1)S(1)}, bf16[32,128]{1,0:T(8,128)(2,1)S(1)}, u32[]{:S(2)}, u32[]{:S(2)}) collective-permute-start(bf16[32,128]{1,0:T(8,128)(2,1)S(1)} %get-tuple-element.31), channel_id=1, source_target_pairs={{0,9},{1,8},{2,11},{3,10},{4,13},{5,12},{6,15},{7,14},{8,1},{9,0},... | collective-permute-start | bytes 24584 | tf_op jit(solution)/shard_map/ppermute | solution.py:59
  16.2 1.0 %collective-permute-done.4.rest_0_ = bf16[32,128]{1,0:T(8,128)(2,1)S(1)} collective-permute-done((bf16[32,128]{1,0:T(8,128)(2,1)S(1)}, bf16[32,128]{1,0:T(8,128)(2,1)S(1)}, u32[]{:S(2)}, u32[]{:S(2)}) %collective-permute-start.4) | collective-permute-done | bytes 8224 | tf_op jit(solution)/shard_map/ppermute | solution.py:59
  17.3 1.3 %collective-permute-done.5.rest_1_ = bf16[32,128]{1,0:T(8,128)(2,1)S(1)} collective-permute-done((bf16[32,128]{1,0:T(8,128)(2,1)S(1)}, bf16[32,128]{1,0:T(8,128)(2,1)S(1)}, u32[]{:S(2)}, u32[]{:S(2)}) %collective-permute-start.5) | collective-permute-done | bytes 8224 | tf_op jit(solution)/shard_map/ppermute | solution.py:59
  18.5 0.5 %collective-permute-done.6.rest_2_ = bf16[32,128]{1,0:T(8,128)(2,1)S(1)} collective-permute-done((bf16[32,128]{1,0:T(8,128)(2,1)S(1)}, bf16[32,128]{1,0:T(8,128)(2,1)S(1)}, u32[]{:S(2)}, u32[]{:S(2)}) %collective-permute-start.6) | collective-permute-done | bytes 8224 | tf_op jit(solution)/shard_map/ppermute | solution.py:59
  19.0 0.9 %interact.1 = bf16[8,16,128]{2,1,0:T(8,128)(2,1)} custom-call(bf16[16,128]{1,0:T(8,128)(2,1)S(1)} %get-tuple-element.19.proj_ref, bf16[32,128]{1,0:T(8,128)(2,1)S(1)} %collective-permute-done.4.rest_0_, bf16[32,128]{1,0:T(8,128)(2,1)S(1)} %collective-permute-done.5.rest_1_, bf16[32,128]{1,0:T(8,128)(2,1)S(1)} %collective-permute-done.6.rest_2_, ...), custom_call_target="tpu_custom_call" | custom-call | tf_op jit(solution)/shard_map/interact/pallas_call | solution.py:310
  (1 shorter events, 0.0 us)
Async XLA Ops:
  0.0 1.8 %collective-permute-start = (bf16[256,512]{1,0:T(8,128)(2,1)}, bf16[256,512]{1,0:T(8,128)(2,1)S(1)}, u32[]{:S(2)}, u32[]{:S(2)}) collective-permute-start(bf16[256,512]{1,0:T(8,128)(2,1)} %emb_hbm.1), channel_id=1, source_target_pairs={{0,1},{1,0},{2,3},{3,2},{4,5},{5,4},{6,7},{7,6},{8,9},{9,8},{10,11... | collective-permute-start | bytes 786440 | tf_op jit(solution)/shard_map/ppermute | solution.py:111
  1.8 6.8 %copy-start = (bf16[2,2048,1024]{2,1,0:T(8,128)(2,1)S(1)}, bf16[2,2048,1024]{2,1,0:T(8,128)(2,1)}, u32[]{:S(2)}) copy-start(bf16[2,2048,1024]{2,1,0:T(8,128)(2,1)} %w1_ref.7) | copy-start | bytes 25165828
  2.1 7.0 %collective-permute-start.2 = (bf16[8,32,128]{2,1,0:T(8,128)(2,1)S(1)}, bf16[8,32,128]{2,1,0:T(8,128)(2,1)S(1)}, u32[]{:S(2)}, u32[]{:S(2)}) collective-permute-start(bf16[8,32,128]{2,1,0:T(8,128)(2,1)S(1)} %get-tuple-element.26), channel_id=1, source_target_pairs={{0,3},{1,2},{2,7},{3,6},{4,1},{5,0},{6,5},{7,4},{8,11},{9,10},{10,... | collective-permute-start | bytes 196616 | tf_op jit(solution)/shard_map/ppermute | solution.py:42
  4.8 6.4 %collective-permute-start.1 = (bf16[8,32,128]{2,1,0:T(8,128)(2,1)S(1)}, bf16[8,32,128]{2,1,0:T(8,128)(2,1)S(1)}, u32[]{:S(2)}, u32[]{:S(2)}) collective-permute-start(bf16[8,32,128]{2,1,0:T(8,128)(2,1)S(1)} %get-tuple-element.25), channel_id=1, source_target_pairs={{0,7},{1,6},{2,5},{3,4},{4,3},{5,2},{6,1},{7,0},{8,15},{9,14},{10,... | collective-permute-start | bytes 196616 | tf_op jit(solution)/shard_map/ppermute | solution.py:42
  7.3 5.3 %collective-permute-start.3 = (bf16[8,32,128]{2,1,0:T(8,128)(2,1)S(1)}, bf16[8,32,128]{2,1,0:T(8,128)(2,1)S(1)}, u32[]{:S(2)}, u32[]{:S(2)}) collective-permute-start(bf16[8,32,128]{2,1,0:T(8,128)(2,1)S(1)} %get-tuple-element.28), channel_id=1, source_target_pairs={{0,5},{1,4},{2,1},{3,0},{4,7},{5,6},{6,3},{7,2},{8,13},{9,12},{10,... | collective-permute-start | bytes 196616 | tf_op jit(solution)/shard_map/ppermute | solution.py:42
  9.1 3.4 %copy-start.1 = (bf16[2,1024,256]{2,1,0:T(8,128)(2,1)S(1)}, bf16[2,1024,256]{2,1,0:T(8,128)(2,1)}, u32[]{:S(2)}) copy-start(bf16[2,1024,256]{2,1,0:T(8,128)(2,1)} %w2_ref.1) | copy-start | bytes 3145732
  13.2 4.0 %collective-permute-start.4 = (bf16[32,128]{1,0:T(8,128)(2,1)S(1)}, bf16[32,128]{1,0:T(8,128)(2,1)S(1)}, u32[]{:S(2)}, u32[]{:S(2)}) collective-permute-start(bf16[32,128]{1,0:T(8,128)(2,1)S(1)} %get-tuple-element.29), channel_id=1, source_target_pairs={{0,25},{1,24},{2,27},{3,26},{4,29},{5,28},{6,31},{7,30},{8,17},{9,... | collective-permute-start | bytes 24584 | tf_op jit(solution)/shard_map/ppermute | solution.py:59
  15.4 3.1 %collective-permute-start.5 = (bf16[32,128]{1,0:T(8,128)(2,1)S(1)}, bf16[32,128]{1,0:T(8,128)(2,1)S(1)}, u32[]{:S(2)}, u32[]{:S(2)}) collective-permute-start(bf16[32,128]{1,0:T(8,128)(2,1)S(1)} %get-tuple-element.30), channel_id=1, source_target_pairs={{0,17},{1,16},{2,19},{3,18},{4,21},{5,20},{6,23},{7,22},{8,25},{9,... | collective-permute-start | bytes 24584 | tf_op jit(solution)/shard_map/ppermute | solution.py:59
  15.9 3.1 %collective-permute-start.6 = (bf16[32,128]{1,0:T(8,128)(2,1)S(1)}, bf16[32,128]{1,0:T(8,128)(2,1)S(1)}, u32[]{:S(2)}, u32[]{:S(2)}) collective-permute-start(bf16[32,128]{1,0:T(8,128)(2,1)S(1)} %get-tuple-element.31), channel_id=1, source_target_pairs={{0,9},{1,8},{2,11},{3,10},{4,13},{5,12},{6,15},{7,14},{8,1},{9,0},... | collective-permute-start | bytes 24584 | tf_op jit(solution)/shard_map/ppermute | solution.py:59
